TPU v7x, 128 devices: a whole 4x4x4 slice. The times are simulated.
128 devices in a mesh: grp: 4 (over y_lo, core), gx: 32 (over x, z, y_hi).
Axes of the slice: x: 4, y: 4 (y_hi: 2, y_lo: 2; y = y_hi * 2 + y_lo), z: 4, core: 2. Of those that a mesh axis runs over, the one named last changes fastest.
Arguments:
- atmosphere: float32 [40, 64, 4096], P(None, 'grp', 'gx'), may hold values from -6 to 6
- diffusion: float32 [64, 4096], P('grp', 'gx'), may hold values from 0.01 to 0.09
- coriolis: float32 [64], P('grp'), may hold values from -0.25 to 0.25
- mixing: float32 [10], replicated, may hold values from 0.02 to 0.2
- stencil_owner: int32 [32, 3, 288], replicated, may hold values from 0 to 95, as said below
- stencil_cell: int32 [32, 3, 288], replicated, may hold values from 0 to 2047, as said below
- stencil_weight: float32 [32, 3, 288], replicated, as said below
- feedback_owner: int32 [32, 128], replicated, may hold values from 0 to 95, as said below
- feedback_cell: int32 [32, 128], replicated, may hold values from 0 to 2047, as said below
Outputs:
- evolved: float32 [40, 64, 4096], P(None, 'grp', 'gx')
Inputs may be any that keep to these rules, and one draw needn't show every extreme that they name: `stencil_owner`: parent devices; any parent device may serve any cycle point. The 3 pairs of one cycle point name different cells. `stencil_cell`: cells of the owners in stencil_owner. `stencil_weight`: Positive; the 3 weights of a cycle point sum to one. `feedback_owner`: parent devices; no parent cell is named by two feedback entries. `feedback_cell`: cells of the owners in feedback_owner.
All inputs are finite; a program needn't handle non-finite values.
Results may differ from a plain program's by a relative error of at most 0.0001.
Values sent between devices are 32-bit elements; how exact they have to be, the bound alone decides.
No kernel may reach another device: no remote copies, remote signals or barrier semaphores. Data moves between devices by JAX's collectives and lax.ppermute only.
A program may use at most 128 MiB of HBM per device.

v0:
```python
import jax
import jax.numpy as jnp
from jax import lax
from jax.sharding import PartitionSpec as P

SUBSTEPS = 2


def padded(cells, sides, width):
    for axis, dim in sides:
        count = lax.axis_size(axis)
        head = lax.slice_in_dim(cells, 0, width, axis=dim)
        tail = lax.slice_in_dim(cells, cells.shape[dim] - width, cells.shape[dim], axis=dim)
        cells = jnp.concatenate(
            [
                lax.ppermute(tail, axis, [(i, (i + 1) % count) for i in range(count)]),
                cells,
                lax.ppermute(head, axis, [((i + 1) % count, i) for i in range(count)]),
            ],
            axis=dim,
        )
    return cells


def broadcast(value, axis, source):
    kept = jnp.where(lax.axis_index(axis) == source, value, 0).astype(value.dtype)
    return lax.psum(kept, axis)


def advance(extended, center, diffusion, coriolis, mixing):
    neighbours = (
        extended[:, 1:-1, :-2]
        + extended[:, 1:-1, 2:]
        + extended[:, :-2, 1:-1]
        + extended[:, 2:, 1:-1]
        + extended[:, :-2, 2:]
        + extended[:, 2:, :-2]
    )
    laplace = neighbours - 6.0 * center
    lane_count, row_count, col_count = center.shape
    level_count = mixing.shape[0]
    stacked = center.reshape(lane_count // level_count, level_count, row_count, col_count)
    upper = jnp.concatenate([stacked[:, 1:], stacked[:, -1:]], axis=1)
    lower = jnp.concatenate([stacked[:, :1], stacked[:, :-1]], axis=1)
    vertical = mixing[None, :, None, None] * (upper - 2.0 * stacked + lower)
    rotation = jnp.concatenate(
        [
            (coriolis[:, None] * stacked[1])[None],
            (-coriolis[:, None] * stacked[0])[None],
            jnp.zeros_like(stacked[2:]),
        ],
        axis=0,
    )
    return center + diffusion * laplace + (vertical + rotation).reshape(center.shape)


def shards(
    atmosphere,
    diffusion,
    coriolis,
    mixing,
    stencil_owner,
    stencil_cell,
    stencil_weight,
    feedback_owner,
    feedback_cell,
):
    lane_count, row_count, col_count = atmosphere.shape
    cell_count = row_count * col_count
    column_count = lax.axis_size("gx")
    group_count = lax.axis_size("grp")
    group_index = lax.axis_index("grp")
    column_index = lax.axis_index("gx")
    own_rank = group_index * column_count + column_index
    is_nested = group_index == group_count - 1
    perimeter = stencil_owner.shape[2]
    owner_flat = feedback_owner.reshape(-1)
    target_flat = feedback_cell.reshape(-1)
    current = atmosphere
    for substep in range(SUBSTEPS):
        flat_now = current.reshape(lane_count, cell_count)
        cycle_terms = jnp.zeros((lane_count, column_count * perimeter), jnp.float32)
        for member in range(stencil_owner.shape[1]):
            mine = stencil_owner[:, member, :].reshape(-1) == own_rank
            positions = jnp.where(mine, stencil_cell[:, member, :].reshape(-1), 0)
            weights = jnp.where(mine, stencil_weight[:, member, :].reshape(-1), 0.0)
            cycle_terms = cycle_terms + jnp.take(flat_now, positions, axis=1) * weights
        padding = jnp.zeros((lane_count, (group_count - 1) * column_count * perimeter), jnp.float32)
        everything = jnp.concatenate([padding, cycle_terms], axis=1)
        cycle = lax.psum_scatter(everything, ("grp", "gx"), scatter_dimension=1, tiled=True)
        extended = padded(current, (("grp", 1), ("gx", 2)), 1)
        upper_rim = jnp.where(group_index == 0, extended[:, 1:2, :], extended[:, 0:1, :])
        lower_rim = jnp.where(
            group_index == group_count - 2, extended[:, -2:-1, :], extended[:, -1:, :]
        )
        extended = jnp.concatenate([upper_rim, extended[:, 1:-1, :], lower_rim], axis=1)
        fresh = advance(extended, current, diffusion, coriolis, mixing)
        left_edge = jnp.where(
            column_index == 0, cycle[:, 2 * col_count : 2 * col_count + row_count], fresh[:, :, 0]
        )
        right_edge = jnp.where(
            column_index == column_count - 1, cycle[:, 2 * col_count + row_count :], fresh[:, :, -1]
        )
        framed = fresh.at[:, :, 0].set(left_edge).at[:, :, -1].set(right_edge)
        framed = (
            framed.at[:, 0, :]
            .set(cycle[:, :col_count])
            .at[:, -1, :]
            .set(cycle[:, col_count : 2 * col_count])
        )
        fresh = jnp.where(is_nested, framed, fresh)
        coarse = fresh.reshape(lane_count, row_count // 4, 4, col_count // 4, 4).mean(axis=(2, 4))
        coarse = coarse.reshape(lane_count, -1)
        fresh_flat = fresh.reshape(lane_count, cell_count)
        shared = broadcast(coarse, "grp", group_count - 1)
        place_positions = jnp.where(owner_flat == own_rank, target_flat, cell_count)
        result_flat = fresh_flat.at[:, place_positions].set(
            lax.all_gather(shared, "gx", axis=1, tiled=True), mode="drop"
        )
        current = result_flat.reshape(lane_count, row_count, col_count)
    return current


def solution(mesh):
    placed = (P(None, "grp", "gx"), P("grp", "gx"), P("grp"), P(), P(), P(), P(), P(), P())
    return jax.shard_map(
        shards, mesh=mesh, in_specs=placed, out_specs=P(None, "grp", "gx"), check_vma=False
    )
```

profile of v0, /device:TPU:1, one launch (start us, length us, event | category | flops | bytes accessed | tf_op | source)
XLA Modules:
  0.0 1910.3 jit_solution(9846317157565839711)
XLA Ops:
  10.1 31.0 %gather_fusion = f32[9216,40]{1,0:T(8,128)} fusion(f32[40,2048]{0,1:T(8,128)S(1)} %bitcast.134, s32[9216]{0:T(1024)S(1)} %fusion.4), kind=kCustom, calls=%fused_computation.clone | custom fusion | bytes 2985984 | tf_op jit(solution)/shard_map/jit(_take)/gather | solution.py:87
  41.1 31.0 %gather_fusion.1 = f32[9216,40]{1,0:T(8,128)} fusion(f32[40,2048]{0,1:T(8,128)S(1)} %bitcast.135, s32[9216]{0:T(1024)S(1)} %fusion.5), kind=kCustom, calls=%fused_computation.1.clone | custom fusion | bytes 2985984 | tf_op jit(solution)/shard_map/jit(_take)/gather | solution.py:87
  72.1 31.0 %gather_fusion.2 = f32[9216,40]{1,0:T(8,128)} fusion(f32[40,2048]{0,1:T(8,128)S(1)} %bitcast.136, s32[9216]{0:T(1024)S(1)} %fusion.6), kind=kCustom, calls=%fused_computation.2.clone | custom fusion | bytes 2985984 | tf_op jit(solution)/shard_map/jit(_take)/gather | solution.py:87
  103.4 11.8 fusion.2
  115.3 10.7 concatenate.106
  127.1 2.8 collective-permute-start
  134.0 2.6 collective-permute-start.2
  136.7 5.7 collective-permute-start.3
  143.7 1.5 copy.123
  145.2 1.5 copy.124
  146.7 2.4 copy.125
  149.1 1.4 copy.110
  150.6 12.0 collective-permute-done.2
  167.6 2.4 copy.164
  170.0 2.4 copy.165
  172.4 2.4 copy.166
  174.7 2.4 copy.167
  181.2 4.2 add_add_fusion.1
  185.5 655.6 %reduce-scatter.3.cloned.1.call-done = f32[40,288]{0,1:T(8,128)} async-done(((f32[40,36864]{0,1:T(8,128)}), f32[40,288]{0,1:T(8,128)}) %reduce-scatter.3.cloned.1.call-update) | async-done | bytes 46096 | tf_op jit(solution)/shard_map/reduce_scatter | solution.py:90
  843.3 1.5 scatter.44
  844.8 1.5 scatter.45
  847.5 10.1 psum.14
  857.6 85.5 %all_gather.6 = f32[40,4096]{1,0:T(8,128)} all-gather(f32[40,128]{1,0:T(8,128)S(1)} %psum.14), channel_id=1, replica_groups=mesh['grp'=4,'gx'=32] {'gx'}, dimensions={1}, use_global_device_ids=true | all-gather | bytes 675840 | tf_op jit(solution)/shard_map/all_gather | solution.py:118
  943.1 1.7 copy.132
  944.9 11.2 scatter_fusion
  956.1 31.0 %gather_fusion.4 = f32[9216,40]{1,0:T(8,128)} fusion(f32[40,2048]{0,1:T(8,128)S(1)} %scatter_fusion, s32[9216]{0:T(1024)S(1)} %fusion.5), kind=kCustom, calls=%fused_computation.4.clone | custom fusion | bytes 2985984 | tf_op jit(solution)/shard_map/jit(_take)/gather | solution.py:87
  987.1 31.0 %gather_fusion.5 = f32[9216,40]{1,0:T(8,128)} fusion(f32[40,2048]{0,1:T(8,128)S(1)} %scatter_fusion, s32[9216]{0:T(1024)S(1)} %copy-done.4), kind=kCustom, calls=%fused_computation.5.clone | custom fusion | bytes 2985984 | tf_op jit(solution)/shard_map/jit(_take)/gather | solution.py:87
  1018.1 31.0 %gather_fusion.3 = f32[9216,40]{1,0:T(8,128)} fusion(f32[40,2048]{0,1:T(8,128)S(1)} %scatter_fusion, s32[9216]{0:T(1024)S(1)} %copy-done.6), kind=kCustom, calls=%fused_computation.3.clone | custom fusion | bytes 2985984 | tf_op jit(solution)/shard_map/jit(_take)/gather | solution.py:87
  1049.2 11.8 fusion
  1061.0 10.7 concatenate.119
  1072.9 15.3 collective-permute-start.4
  1093.6 7.9 collective-permute-start.7
  1102.8 1.5 copy.147
  1104.3 2.4 copy.148
  1106.7 2.4 copy.151
  1109.2 8.3 collective-permute-done.6
  1117.4 2.5 collective-permute-done.7
  1121.0 2.3 copy.168
  1125.7 1.5 copy.170
  1129.9 1.4 copy.173
  1131.3 4.2 add_add_fusion
  1135.5 651.7 %reduce-scatter.5.cloned.1.call-done = f32[40,288]{0,1:T(8,128)} async-done(((f32[40,36864]{0,1:T(8,128)}), f32[40,288]{0,1:T(8,128)}) %reduce-scatter.5.cloned.1.call-update) | async-done | bytes 46096 | tf_op jit(solution)/shard_map/reduce_scatter | solution.py:90
  1789.5 1.5 scatter.61
  1791.0 1.5 scatter.62
  1793.7 11.6 psum.15
  1805.3 84.4 %all_gather.7 = f32[40,4096]{1,0:T(8,128)} all-gather(f32[40,128]{1,0:T(8,128)S(1)} %psum.15), channel_id=1, replica_groups=mesh['grp'=4,'gx'=32] {'gx'}, dimensions={1}, use_global_device_ids=true | all-gather | bytes 675840 | tf_op jit(solution)/shard_map/all_gather | solution.py:118
  1889.7 1.7 copy.156
  1891.4 11.0 scatter_fusion.1
  (160 shorter events, 41.3 us)
Async XLA Ops:
  6.5 834.5 %reduce-scatter.3.cloned.1.call-start = ((), (), s32[]{:S(2)}) async-start(), calls=%async_computation.2 | async-start | bytes 19021824 | tf_op jit(solution)/shard_map/reduce_scatter | solution.py:90
  8.6 94.8 %copy-start.15 = (pred[9216]{0:T(1024)(128)(4,1)}, pred[9216]{0:T(1024)(128)(4,1)S(1)}, u32[]{:S(2)}) copy-start(pred[9216]{0:T(1024)(128)(4,1)S(1)} %get-tuple-element.159) | copy-start | bytes 27652
  8.6 94.8 %copy-start.17 = (pred[9216]{0:T(1024)(128)(4,1)}, pred[9216]{0:T(1024)(128)(4,1)S(1)}, u32[]{:S(2)}) copy-start(pred[9216]{0:T(1024)(128)(4,1)S(1)} %get-tuple-element.160) | copy-start | bytes 27652
  8.6 63.4 %copy-start.3 = (s32[9216]{0:T(1024)}, s32[9216]{0:T(1024)S(1)}, u32[]{:S(2)}) copy-start(s32[9216]{0:T(1024)S(1)} %fusion.6) | copy-start | bytes 110596
  8.8 32.4 %copy-start.5 = (s32[9216]{0:T(1024)}, s32[9216]{0:T(1024)S(1)}, u32[]{:S(2)}) copy-start(s32[9216]{0:T(1024)S(1)} %fusion.4) | copy-start | bytes 110596
  8.8 94.6 %copy-start.19 = (pred[9216]{0:T(1024)(128)(4,1)}, pred[9216]{0:T(1024)(128)(4,1)S(1)}, u32[]{:S(2)}) copy-start(pred[9216]{0:T(1024)(128)(4,1)S(1)} %compare_and_fusion.2) | copy-start | bytes 27652
  103.2 12.1 copy-start.7
  103.3 12.0 copy-start.9
  103.4 11.9 copy-start.11
  126.0 1.0 copy-start
  126.0 3.8 copy-start.23
  126.0 3.9 copy-start.21
  126.0 3.9 copy-start.22
  126.1 1661.2 %reduce-scatter.5.cloned.1.call-start = ((), (), s32[]{:S(2)}) async-start(), calls=%async_computation.3 | async-start | bytes 19021824 | tf_op jit(solution)/shard_map/reduce_scatter | solution.py:90
  127.1 4.5 collective-permute-start
  129.8 3.2 collective-permute-start.1
  129.8 1.7 copy-start.27
  129.9 1.6 copy-start.25
  130.9 19.6 %copy-start.29 = (f32[10]{0:T(128)S(1)}, f32[10]{0:T(128)}, u32[]{:S(2)}) copy-start(f32[10]{0:T(128)} %param.30) | copy-start | bytes 124
  134.0 28.5 %collective-permute-start.2 = (f32[40,18,1]{2,0,1:T(8,128)}, f32[40,18,1]{2,0,1:T(8,128)S(1)}, u32[]{:S(2)}, u32[]{:S(2)}) collective-permute-start(f32[40,18,1]{2,0,1:T(8,128)} %get-tuple-element.130), channel_id=1, source_target_pairs={{0,1},{1,2},{2,3},{3,4},{4,5},{5,6},{6,7},{7,8},{8,9},{9,10},{10,1... | collective-permute-start | bytes 8648 | tf_op jit(solution)/shard_map/ppermute | solution.py:16
  136.7 27.3 %collective-permute-start.3 = (f32[40,18,1]{2,0,1:T(8,128)}, f32[40,18,1]{2,0,1:T(8,128)}, u32[]{:S(2)}, u32[]{:S(2)}) collective-permute-start(f32[40,18,1]{2,0,1:T(8,128)} %get-tuple-element.131), channel_id=1, source_target_pairs={{1,0},{2,1},{3,2},{4,3},{5,4},{6,5},{7,6},{8,7},{9,8},{10,9},{11,1... | collective-permute-start | bytes 8648 | tf_op jit(solution)/shard_map/ppermute | solution.py:18
  846.4 98.5 %copy-start.13 = (s32[4096,1]{0,1:T(1,128)S(1)}, s32[4096,1]{0,1:T(1,128)}, u32[]{:S(2)}) copy-start(s32[4096,1]{0,1:T(1,128)} %compare_select_fusion.3) | copy-start | bytes 49156
  956.1 31.0 %copy-start.4 = (s32[9216]{0:T(1024)S(1)}, s32[9216]{0:T(1024)}, u32[]{:S(2)}) copy-start(s32[9216]{0:T(1024)} %copy-done.3) | copy-start | bytes 110596
  987.1 31.0 %copy-start.6 = (s32[9216]{0:T(1024)S(1)}, s32[9216]{0:T(1024)}, u32[]{:S(2)}) copy-start(s32[9216]{0:T(1024)} %copy-done.5) | copy-start | bytes 110596
  1018.1 31.0 %copy-start.8 = (f32[9216]{0:T(1024)S(1)}, f32[9216]{0:T(1024)}, u32[]{:S(2)}) copy-start(f32[9216]{0:T(1024)} %copy-done.7) | copy-start | bytes 110596
  1018.1 31.0 %copy-start.10 = (f32[9216]{0:T(1024)S(1)}, f32[9216]{0:T(1024)}, u32[]{:S(2)}) copy-start(f32[9216]{0:T(1024)} %copy-done.9) | copy-start | bytes 110596
  1018.1 31.0 %copy-start.12 = (f32[9216]{0:T(1024)S(1)}, f32[9216]{0:T(1024)}, u32[]{:S(2)}) copy-start(f32[9216]{0:T(1024)} %copy-done.11) | copy-start | bytes 110596
  1018.1 31.0 %copy-start.16 = (pred[9216]{0:T(1024)(128)(4,1)S(1)}, pred[9216]{0:T(1024)(128)(4,1)}, u32[]{:S(2)}) copy-start(pred[9216]{0:T(1024)(128)(4,1)} %copy-done.15) | copy-start | bytes 27652
  1018.1 31.0 %copy-start.18 = (pred[9216]{0:T(1024)(128)(4,1)S(1)}, pred[9216]{0:T(1024)(128)(4,1)}, u32[]{:S(2)}) copy-start(pred[9216]{0:T(1024)(128)(4,1)} %copy-done.17) | copy-start | bytes 27652
  1018.1 31.0 %copy-start.20 = (pred[9216]{0:T(1024)(128)(4,1)S(1)}, pred[9216]{0:T(1024)(128)(4,1)}, u32[]{:S(2)}) copy-start(pred[9216]{0:T(1024)(128)(4,1)} %copy-done.19) | copy-start | bytes 27652
  1071.8 17.4 copy-start.28
  1071.8 17.5 copy-start.24
  1071.8 17.6 copy-start.26
  1072.1 16.1 copy-start.1
  1072.9 19.1 %collective-permute-start.4 = (f32[40,1,128]{2,1,0:T(1,128)}, f32[40,1,128]{2,1,0:T(1,128)S(1)}, u32[]{:S(2)}, u32[]{:S(2)}) collective-permute-start(f32[40,1,128]{2,1,0:T(1,128)} %get-tuple-element.132), channel_id=1, source_target_pairs={{0,32},{32,64},{64,96},{96,0},{1,33},{33,65},{65,97},{97,1},{2,34}... | collective-permute-start | bytes 61448 | tf_op jit(solution)/shard_map/ppermute | solution.py:16
  1088.2 3.8 collective-permute-start.5
  1093.1 24.3 %collective-permute-start.6 = (f32[40,18,1]{2,0,1:T(8,128)}, f32[40,18,1]{2,0,1:T(8,128)S(1)}, u32[]{:S(2)}, u32[]{:S(2)}) collective-permute-start(f32[40,18,1]{2,0,1:T(8,128)} %get-tuple-element.126), channel_id=1, source_target_pairs={{0,1},{1,2},{2,3},{3,4},{4,5},{5,6},{6,7},{7,8},{8,9},{9,10},{10,1... | collective-permute-start | bytes 8648 | tf_op jit(solution)/shard_map/ppermute | solution.py:16
  1093.6 26.4 %collective-permute-start.7 = (f32[40,18,1]{2,0,1:T(8,128)}, f32[40,18,1]{2,0,1:T(8,128)S(1)}, u32[]{:S(2)}, u32[]{:S(2)}) collective-permute-start(f32[40,18,1]{2,0,1:T(8,128)} %get-tuple-element.127), channel_id=1, source_target_pairs={{1,0},{2,1},{3,2},{4,3},{5,4},{6,5},{7,6},{8,7},{9,8},{10,9},{11,1... | collective-permute-start | bytes 8648 | tf_op jit(solution)/shard_map/ppermute | solution.py:18
  1125.1 6.2 copy-start.2
  1792.5 98.8 %copy-start.14 = (s32[4096,1]{0,1:T(1,128)S(1)}, s32[4096,1]{0,1:T(1,128)}, u32[]{:S(2)}) copy-start(s32[4096,1]{0,1:T(1,128)} %compare_select_fusion.3) | copy-start | bytes 49156
Sparse Core Ops, SparseCore 0:
  126.2 714.8 reduce-scatter.2
  1071.9 715.3 reduce-scatter.4
where the time goes:
time: 1920 us; the launch traced here: 1910 us
  waiting for transfers between devices  1330 us (69%)
  local copies, waits for them, and re-layouts  287 us (15%)
  blocking collectives  192 us (10%)
  other arithmetic  49.5 us (3%)
  starting transfers between devices  34.8 us (2%)
    reduce_scatter x2, waiting for transfers between devices, shards(): lax.psum_scatter(everything, ('grp', 'gx'), scatter_dimension=1, tiled=True)  1310 us
    gather x6, local copies, waits for them, and re-layouts, shards(): cycle_terms = cycle_terms + jnp.take(flat_now, positions, axis=1) * weights  186 us
    all_gather x2, blocking collectives, shards(): lax.all_gather(shared, 'gx', axis=1, tiled=True)  170 us
  transfers between devices with their start and end apart: 10, of which 7 were waited for; matrix products, arithmetic and copies ran while one was open for 3% of the time, Pallas kernels for 0%

commit v1 on v0

--- a/solution.py
+++ b/solution.py
@@ -1,9 +1,31 @@
 import jax
 import jax.numpy as jnp
 from jax import lax
+from jax.experimental import pallas as pl
+from jax.experimental.pallas import tpu as pltpu
 from jax.sharding import PartitionSpec as P
 
 SUBSTEPS = 2
+F32 = jnp.float32
+LANES = 40
+ROWS = 16
+COLS = 128
+LEVELS = 10
+GX = 32
+PARENTS = 96
+DEVICES = 128
+PERIM = 288
+TILES = 9
+SLOTS = 25
+HITS = 8
+EDGE = 40
+FG = 5
+T1_ROW = 128
+T2_ROW = 144
+TAB_ROWS = 160
+PGROUPS = 20
+GROUPS = 22
+VMEM_LIMIT = 48 * 1024 * 1024
 
 
 def padded(cells, sides, width):
@@ -54,7 +76,7 @@
     return center + diffusion * laplace + (vertical + rotation).reshape(center.shape)
 
 
-def shards(
+def dense_plan(
     atmosphere,
     diffusion,
     coriolis,
@@ -121,6 +143,634 @@
     return current
 
 
+def iota(shape, dim):
+    return lax.broadcasted_iota(jnp.int32, shape, dim)
+
+
+def chunks(count, step, body):
+    def run(c, carry):
+        for s in range(step):
+            body(c * step + s)
+        return carry
+
+    lax.fori_loop(0, count // step, run, 0)
+
+
+def take(tile, index):
+    return jnp.take_along_axis(tile, index, axis=1, mode="promise_in_bounds")
+
+
+def ranks(masks):
+    rows = masks[0].shape[0]
+    stacked = jnp.concatenate([jnp.where(m, 1.0, 0.0) for m in masks], axis=0)
+    stacked = stacked.astype(jnp.bfloat16)
+    before = jnp.where(iota((128, 128), 0) < iota((128, 128), 1), 1.0, 0.0).astype(jnp.bfloat16)
+    ones = jnp.ones((128, 128), jnp.bfloat16)
+    within = jnp.dot(stacked, before, preferred_element_type=F32)
+    totals = jnp.dot(stacked, ones, preferred_element_type=F32)
+    carry = jnp.zeros((rows, 128), F32)
+    found = []
+    for t in range(len(masks)):
+        found.append(within[t * rows : (t + 1) * rows] + carry)
+        carry = carry + totals[t * rows : (t + 1) * rows]
+    return found, carry
+
+
+def slot_table(masks, values, slots, mark_s, value_s):
+    found, total = ranks(masks)
+    for t in range(TILES):
+        mark_s[t] = jnp.where(masks[t], found[t], -1.0)
+        value_s[t] = values[t]
+    slot_of = lax.rem(iota((8, 128), 1), slots)
+    parts = []
+    for part in range(GX // 8):
+        span = slice(8 * part, 8 * part + 8)
+        marks = [mark_s[t, span, :] for t in range(TILES)]
+        vals = [value_s[t, span, :] for t in range(TILES)]
+        table = jnp.zeros((8, 128), F32)
+        for j in range(slots):
+            picked = [jnp.where(m == float(j), v, 0.0) for m, v in zip(marks, vals)]
+            while len(picked) > 1:
+                picked = [sum(picked[k : k + 2]) for k in range(0, len(picked), 2)]
+            table = jnp.where(slot_of == j, jnp.sum(picked[0], axis=1, keepdims=True), table)
+        parts.append(table)
+    return jnp.concatenate(parts, axis=0), total
+
+
+def send_cells(rows_s, table_ref, send_ref, flag):
+    lane = iota((8, 128), 1)
+    group_of = lane // SLOTS
+    table = table_ref[0:GX, :]
+    for g in range(7):
+        index = jnp.zeros((1, 128), jnp.int32)
+        members = [q for q in range(5 * g, 5 * g + 5) if q < GX]
+        for q in members:
+            index = jnp.where(group_of[0:1] == q - 5 * g, table[q : q + 1, :], index)
+        index = jnp.broadcast_to(index, (8, 128))
+        col = jnp.bitwise_and(index, 127)
+        row = jnp.right_shift(index, 7)
+        cells = [jnp.zeros((8, 128), F32) for _ in range(FG)]
+        for r in range(ROWS):
+            here = row == r
+            for k in range(FG):
+                cells[k] = jnp.where(here, take(rows_s[r, 8 * k : 8 * k + 8, :], col), cells[k])
+        for q in members:
+            block = jnp.zeros((8, 128), F32) if flag is None else flag
+            for k in range(FG):
+                shift = (SLOTS * (k - (q - 5 * g))) % 128
+                moved = cells[k] if shift == 0 else pltpu.roll(cells[k], shift, 1)
+                block = jnp.where(group_of == k, moved, block)
+            send_ref[PARENTS + q] = block
+
+
+def edge_block(x_ref, col, base):
+    lane = iota((8, 128), 1)
+    block = base
+    for h in range(2):
+        for f in range(LANES):
+            edge = x_ref[f, 8 * h : 8 * h + 8, col : col + 1]
+            block = jnp.where(lane == EDGE + h * LANES + f, edge, block)
+    return block
+
+
+def send_parent_edges(x_ref, send_ref, grp, gx, base):
+    first = edge_block(x_ref, 0, base)
+    last = edge_block(x_ref, COLS - 1, base)
+    right = lax.rem(gx + 1, GX)
+    left = lax.rem(gx + GX - 1, GX)
+    send_ref[grp * GX + right] = last
+    send_ref[grp * GX + left] = first
+
+    @pl.when(grp > 0)
+    def _():
+        send_ref[(grp - 1) * GX + right] = last
+
+    @pl.when(grp < 2)
+    def _():
+        send_ref[(grp + 1) * GX + left] = first
+
+
+def unpack_edge(block):
+    return jnp.concatenate([block, pltpu.roll(block, 128 - LANES, 1)], axis=0)
+
+
+def update(x_ref, out_ref, recv_ref, above_ref, below_ref, diff_ref, cor_ref, mix_ref, grp, gx):
+    nest = grp == 3
+    right = lax.rem(gx + 1, GX)
+    left = lax.rem(gx + GX - 1, GX)
+    lane = iota((ROWS, COLS), 1)
+    row = iota((ROWS, COLS), 0)
+    from_left = unpack_edge(recv_ref[grp * GX + left])
+    from_right = unpack_edge(recv_ref[grp * GX + right])
+    top_right = unpack_edge(recv_ref[jnp.maximum(grp - 1, 0) * GX + right])[ROWS - 1 : ROWS]
+    low_left = unpack_edge(recv_ref[jnp.minimum(grp + 1, 3) * GX + left])[0:1]
+    top_right = jnp.where(grp == 0, from_right[0:1], top_right)
+    low_left = jnp.where(grp == 2, from_left[ROWS - 1 : ROWS], low_left)
+    left_sum = from_left + jnp.where(row == ROWS - 1, low_left, pltpu.roll(from_left, ROWS - 1, 0))
+    right_sum = from_right + jnp.where(row == 0, top_right, pltpu.roll(from_right, 1, 0))
+    nest_left = from_left + jnp.where(row == ROWS - 1, 0.0, pltpu.roll(from_left, ROWS - 1, 0))
+    nest_right = from_right + jnp.where(row == 0, 0.0, pltpu.roll(from_right, 1, 0))
+    left_sum = jnp.where(nest, jnp.where(gx == 0, 0.0, nest_left), left_sum)
+    right_sum = jnp.where(nest, jnp.where(gx == GX - 1, 0.0, nest_right), right_sum)
+    diff = diff_ref[...]
+    cor = jnp.zeros((ROWS, COLS), F32)
+    for r in range(ROWS):
+        cor = jnp.where(row == r, cor_ref[r], cor)
+    for f in range(LANES):
+        level = f % LEVELS
+        x = x_ref[f]
+        if above_ref is None:
+            above = jnp.zeros((1, COLS), F32)
+            below = jnp.zeros((1, COLS), F32)
+        else:
+            above = jnp.where(grp == 0, x[0:1], above_ref[f : f + 1, :])
+            below = jnp.where(grp == 2, x[ROWS - 1 : ROWS], below_ref[f : f + 1, :])
+            above = jnp.where(nest, 0.0, above)
+            below = jnp.where(nest, 0.0, below)
+        up = jnp.where(row == 0, above, pltpu.roll(x, 1, 0))
+        down = jnp.where(row == ROWS - 1, below, pltpu.roll(x, ROWS - 1, 0))
+        at = EDGE + f
+        westward = jnp.where(lane == 0, left_sum[:, at : at + 1], pltpu.roll(x + down, 1, 1))
+        eastward = jnp.where(
+            lane == COLS - 1, right_sum[:, at : at + 1], pltpu.roll(x + up, COLS - 1, 1)
+        )
+        laplace = (westward + eastward) + (up + down) - 6.0 * x
+        upper = x if level == LEVELS - 1 else x_ref[f + 1]
+        lower = x if level == 0 else x_ref[f - 1]
+        extra = mix_ref[level] * (upper - 2.0 * x + lower)
+        if f < LEVELS:
+            extra = extra + cor * x_ref[f + LEVELS]
+        elif f < 2 * LEVELS:
+            extra = extra - cor * x_ref[f - LEVELS]
+        out_ref[f] = x + diff * laplace + extra
+
+
+def regroup(recv_ref, base, groups, per, width, group_s, first):
+    lane = iota((8, 128), 1)
+    member_of = lane // width
+
+    def body(g):
+        tiles = [jnp.zeros((8, 128), F32) for _ in range(FG)]
+        for i in range(per):
+            block = recv_ref[jnp.minimum(base + g * per + i, DEVICES - 1)]
+            for k in range(FG):
+                shift = (width * (i - k)) % 128
+                moved = block if shift == 0 else pltpu.roll(block, shift, 1)
+                tiles[k] = jnp.where(member_of == i, moved, tiles[k])
+        for k in range(FG):
+            group_s[first + g, 8 * k : 8 * k + 8, :] = tiles[k]
+
+    chunks(groups, 2 if groups % 2 == 0 else 1, body)
+
+
+def interpolate(tabs_ref, first_row, weight_s, group_s, groups, cycle_s):
+    cycle_s[...] = jnp.zeros((3, LANES, 128), F32)
+
+    def body(t):
+        code = jnp.broadcast_to(tabs_ref[pl.ds(first_row + t, 1), :], (8, 128))
+        index = jnp.bitwise_and(code, 127)
+        group = jnp.right_shift(code, 7)
+        cells = [jnp.zeros((8, 128), F32) for _ in range(FG)]
+        for g in range(groups):
+            here = group == g
+            for k in range(FG):
+                cells[k] = jnp.where(here, take(group_s[g, 8 * k : 8 * k + 8, :], index), cells[k])
+        weight = weight_s[pl.ds(t, 1), :]
+        span = lax.rem(t, 3)
+        for k in range(FG):
+            cycle_s[span, 8 * k : 8 * k + 8, :] += weight * cells[k]
+
+    chunks(TILES, 1, body)
+
+
+def load_weights(weight_ref, weight_s, gx):
+    weight_s[...] = jnp.zeros((16, 128), F32)
+    for k in range(3):
+        own = weight_ref[pl.ds(gx, 1), k, :]
+        weight_s[3 * k : 3 * k + 1, :] = own[:, 0:128]
+        weight_s[3 * k + 1 : 3 * k + 2, :] = own[:, 128:256]
+        weight_s[3 * k + 2 : 3 * k + 3, 0:32] = own[:, 256:288]
+
+
+def prescribe(out_ref, cycle_s, gx):
+    lane = iota((ROWS, COLS), 1)
+
+    @pl.when(jnp.logical_or(gx == 0, gx == GX - 1))
+    def _():
+        turned = jnp.concatenate([cycle_s[2], jnp.zeros((88, 128), F32)], axis=0).T
+        column = jnp.where(gx == 0, turned[0:ROWS, :], turned[ROWS : 2 * ROWS, :])
+        at = jnp.where(gx == 0, 0, COLS - 1)
+        for f in range(LANES):
+            out_ref[f] = jnp.where(lane == at, column[:, f : f + 1], out_ref[f])
+
+    out_ref[:, 0, :] = cycle_s[0]
+    out_ref[:, ROWS - 1, :] = cycle_s[1]
+
+
+def coarsen(out_ref):
+    coarse = jnp.zeros((LANES, 128), F32)
+    for i in range(4):
+        total = (out_ref[:, 4 * i, :] + out_ref[:, 4 * i + 1, :]) + (
+            out_ref[:, 4 * i + 2, :] + out_ref[:, 4 * i + 3, :]
+        )
+        mean = jnp.where(iota((128, 128), 1) == 32 * i + iota((128, 128), 0) // 4, 1.0 / 16.0, 0.0)
+        coarse = coarse + jnp.dot(
+            total, mean, precision=lax.Precision.HIGHEST, preferred_element_type=F32
+        )
+    return coarse
+
+
+def send_coarse(coarse, tabs_ref, send_ref):
+    group_of = iota((8, 128), 1) // SLOTS
+
+    def body(o):
+        index = jnp.broadcast_to(tabs_ref[pl.ds(o, 1), :], (8, 128))
+        block = take(coarse[0:8], index)
+        for k in range(1, FG):
+            block = jnp.where(group_of == k, take(coarse[8 * k : 8 * k + 8], index), block)
+        send_ref[o] = block
+
+    chunks(PARENTS, 8, body)
+
+
+def send_hits(coarse, tabs_ref, send_ref, base):
+    group_of = iota((8, 128), 1) // HITS
+
+    def body(q):
+        index = jnp.broadcast_to(tabs_ref[pl.ds(PARENTS + q, 1), :], (8, 128))
+        block = base
+        for k in range(FG):
+            block = jnp.where(group_of == k, take(coarse[8 * k : 8 * k + 8], index), block)
+        send_ref[PARENTS + q] = block
+
+    chunks(GX, 8, body)
+
+
+def feed_back(src_ref, out_ref, recv_ref, map_ref, group_s):
+    regroup(recv_ref, PARENTS, 7, 5, SLOTS, group_s, 0)
+    for r in range(ROWS):
+        code = jnp.broadcast_to(map_ref[r : r + 1, :], (8, 128))
+        index = jnp.bitwise_and(code, 127)
+        group = jnp.right_shift(code, 7)
+        cells = [src_ref[8 * k : 8 * k + 8, r, :] for k in range(FG)]
+        for g in range(7):
+            here = group == g
+            for k in range(FG):
+                cells[k] = jnp.where(here, take(group_s[g, 8 * k : 8 * k + 8, :], index), cells[k])
+        for k in range(FG):
+            out_ref[8 * k : 8 * k + 8, r, :] = cells[k]
+
+
+def feedback_map(owner_ref, cell_ref, map_ref, me):
+    owner = owner_ref[...]
+    cell = cell_ref[...]
+    own = owner == me
+    found, _ = ranks([own])
+    slot = jnp.minimum(found[0], float(SLOTS - 1))
+    row = jnp.where(own, jnp.right_shift(cell, 7), -1)
+    col = jnp.bitwise_and(cell, 127)
+    planes = jnp.zeros((2 * ROWS, 128), F32)
+    for q in range(GX):
+        here = iota((ROWS, 128), 0) == row[q : q + 1, :]
+        codes = jnp.concatenate(
+            [jnp.where(here, float(q + 1), 0.0), jnp.where(here, slot[q : q + 1, :], 0.0)], axis=0
+        )
+        hot = jnp.where(iota((128, 128), 0) == col[q : q + 1, :], 1.0, 0.0)
+        planes = planes + lax.dot_general(
+            codes.astype(jnp.bfloat16),
+            hot.astype(jnp.bfloat16),
+            (((1,), (1,)), ((), ())),
+            preferred_element_type=F32,
+        )
+    block = planes[0:ROWS].astype(jnp.int32) - 1
+    slots = planes[ROWS : 2 * ROWS].astype(jnp.int32)
+    group = jnp.right_shift(block * 205, 10)
+    code = group * 128 + (block - 5 * group) * SLOTS + slots
+    map_ref[...] = jnp.where(block < 0, -1, code)
+
+
+def first_kernel(
+    x_ref,
+    owner_ref,
+    cell_ref,
+    fb_owner_ref,
+    fb_cell_ref,
+    fb_owner_sm,
+    fb_cell_sm,
+    send_ref,
+    tabs_ref,
+    last_row_ref,
+    first_row_ref,
+    gid_s,
+    mark_s,
+    value_s,
+    rows_s,
+    turned_s,
+):
+    grp = lax.axis_index("grp")
+    gx = lax.axis_index("gx")
+    me = grp * GX + gx
+    lane = iota((8, 128), 1)
+    last_row_ref[...] = x_ref[:, ROWS - 1, :]
+    first_row_ref[...] = x_ref[:, 0, :]
+    for k in range(3):
+        gid = owner_ref[:, k, :] * 2048 + cell_ref[:, k, :]
+        gid_s[3 * k] = gid[:, 0:128]
+        gid_s[3 * k + 1] = gid[:, 128:256]
+        gid_s[3 * k + 2] = jnp.full((GX, 128), -1, jnp.int32)
+        gid_s[3 * k + 2, :, 0:32] = gid[:, 256:288]
+
+    def flag_block(over):
+        worst = jnp.max(over, axis=0, keepdims=True)
+        flag = jnp.where(worst > 0.5, 1.0, 0.0)
+        return jnp.where(lane == 127, jnp.broadcast_to(flag, (8, 128)), 0.0)
+
+    @pl.when(grp < 3)
+    def _():
+        gids = [gid_s[t] for t in range(TILES)]
+        masks = [jnp.right_shift(g, 11) == me for g in gids]
+        values = [jnp.bitwise_and(g, 2047).astype(F32) for g in gids]
+        table, total = slot_table(masks, values, SLOTS, mark_s, value_s)
+        tabs_ref[0:GX, :] = table.astype(jnp.int32)
+        base = flag_block(jnp.where(total > float(SLOTS), 1.0, 0.0))
+        send_ref[...] = jnp.broadcast_to(base[None], (DEVICES, 8, 128))
+        for r in range(ROWS):
+            rows_s[r] = x_ref[:, r, :]
+        send_cells(rows_s, tabs_ref, send_ref, base)
+        send_parent_edges(x_ref, send_ref, grp, gx, base)
+
+    @pl.when(grp == 3)
+    def _():
+        own = fb_owner_ref[pl.ds(gx, 1), :]
+        hot = iota((PARENTS, 128), 0) == own
+        found, total = ranks([hot])
+        over = jnp.max(jnp.where(total > float(SLOTS), 1.0, 0.0), axis=0, keepdims=True)
+        rank = jnp.sum(jnp.where(hot, found[0], 0.0), axis=0, keepdims=True)
+        slot_of = lax.rem(iota((128, 128), 0), SLOTS).astype(F32)
+        chosen = jnp.where(slot_of == rank, iota((128, 128), 1).astype(F32), 0.0)
+        table = lax.dot_general(
+            jnp.where(hot, 1.0, 0.0).astype(jnp.bfloat16),
+            chosen.astype(jnp.bfloat16),
+            (((1,), (1,)), ((), ())),
+            preferred_element_type=F32,
+        )
+        tabs_ref[0:PARENTS, :] = table.astype(jnp.int32)
+
+        terms = [gid_s[t, pl.ds(gx, 1), :] for t in range(TILES)]
+        owners = [jnp.right_shift(t, 11) for t in terms]
+        hots = [iota((PARENTS, 128), 0) == o for o in owners]
+        found, _ = ranks(hots)
+        codes = []
+        for t in range(TILES):
+            slot = jnp.sum(jnp.where(hots[t], found[t], 0.0), axis=0, keepdims=True)
+            slot = jnp.minimum(slot.astype(jnp.int32), SLOTS - 1)
+            group = jnp.right_shift(owners[t] * 205, 10)
+            codes.append(group * 128 + (owners[t] - 5 * group) * SLOTS + slot)
+            tabs_ref[T1_ROW + t : T1_ROW + t + 1, :] = codes[t]
+
+        def seek(c, found_at):
+            for s in range(4):
+                b = 4 * c + s
+                wanted = fb_owner_sm[gx, b] * 2048 + fb_cell_sm[gx, b]
+                found_at = [jnp.where(gid_s[t] == wanted, b, found_at[t]) for t in range(TILES)]
+            return found_at
+
+        none = [jnp.full((GX, 128), -1, jnp.int32) for _ in range(TILES)]
+        found_at = lax.fori_loop(0, 32, seek, none)
+        table, total = slot_table(
+            [f >= 0 for f in found_at], [f.astype(F32) for f in found_at], HITS, mark_s, value_s
+        )
+        tabs_ref[PARENTS : PARENTS + GX, :] = table.astype(jnp.int32)
+        over = jnp.maximum(
+            over,
+            jnp.max(jnp.where(total > float(HITS), 1.0, 0.0), axis=0, keepdims=True),
+        )
+
+        fed = (fb_owner_ref[...] * 2048 + fb_cell_ref[...]).astype(F32)
+        turned_s[...] = jnp.concatenate([fed, jnp.full((96, 128), -2.0, F32)], axis=0).T
+        wide = [jnp.broadcast_to(t.astype(F32), (8, 128)) for t in terms]
+
+        def match(q, from_block):
+            column = pltpu.roll(turned_s[...], lax.rem(128 - q, 128), 1)[:, 0:1]
+            for s in range(16):
+                part = jnp.broadcast_to(column[8 * s : 8 * s + 8, :], (8, 128))
+                from_block = [jnp.where(part == w, q, f) for w, f in zip(wide, from_block)]
+            return from_block
+
+        none = [jnp.full((8, 128), -1, jnp.int32) for _ in range(TILES)]
+        from_block = lax.fori_loop(0, GX, match, none)
+        sources = [jnp.max(f, axis=0, keepdims=True) for f in from_block]
+        hots = [iota((GX, 128), 0) == s for s in sources]
+        found, _ = ranks(hots)
+        for t in range(TILES):
+            slot = jnp.sum(jnp.where(hots[t], found[t], 0.0), axis=0, keepdims=True)
+            slot = jnp.minimum(slot.astype(jnp.int32), HITS - 1)
+            code = (PGROUPS + jnp.right_shift(sources[t], 4)) * 128
+            code = code + jnp.bitwise_and(sources[t], 15) * HITS + slot
+            tabs_ref[T2_ROW + t : T2_ROW + t + 1, :] = jnp.where(sources[t] >= 0, code, codes[t])
+
+        base = flag_block(over)
+        send_ref[...] = jnp.broadcast_to(base[None], (DEVICES, 8, 128))
+        send_ref[PARENTS + lax.rem(gx + 1, GX)] = edge_block(x_ref, COLS - 1, base)
+        send_ref[PARENTS + lax.rem(gx + GX - 1, GX)] = edge_block(x_ref, 0, base)
+
+
+def second_kernel(
+    recv_ref,
+    x_ref,
+    diff_ref,
+    cor_ref,
+    mix_ref,
+    above_ref,
+    below_ref,
+    weight_ref,
+    tabs_ref,
+    fb_owner_ref,
+    fb_cell_ref,
+    out_ref,
+    send_ref,
+    flag_ref,
+    map_ref,
+    rows_s,
+    group_s,
+    cycle_s,
+    weight_s,
+):
+    grp = lax.axis_index("grp")
+    gx = lax.axis_index("gx")
+    flag = recv_ref[0]
+    for d in range(1, DEVICES):
+        flag = jnp.maximum(flag, recv_ref[d])
+    flag_ref[...] = flag
+    update(x_ref, out_ref, recv_ref, above_ref, below_ref, diff_ref, cor_ref, mix_ref, grp, gx)
+
+    @pl.when(grp < 3)
+    def _():
+        for r in range(ROWS):
+            rows_s[r] = out_ref[:, r, :]
+        send_cells(rows_s, tabs_ref, send_ref, None)
+        feedback_map(fb_owner_ref, fb_cell_ref, map_ref, grp * GX + gx)
+
+    @pl.when(grp == 3)
+    def _():
+        load_weights(weight_ref, weight_s, gx)
+        regroup(recv_ref, 0, PGROUPS, 5, SLOTS, group_s, 0)
+        interpolate(tabs_ref, T1_ROW, weight_s, group_s, PGROUPS, cycle_s)
+        prescribe(out_ref, cycle_s, gx)
+        coarse = coarsen(out_ref)
+        send_coarse(coarse, tabs_ref, send_ref)
+        blank = jnp.zeros((8, 128), F32)
+        first = edge_block(out_ref, 0, blank)
+        last = edge_block(out_ref, COLS - 1, blank)
+        send_hits(coarse, tabs_ref, send_ref, blank)
+        lane = iota((8, 128), 1)
+        right = PARENTS + lax.rem(gx + 1, GX)
+        left = PARENTS + lax.rem(gx + GX - 1, GX)
+        send_ref[right] = jnp.where(lane < EDGE, send_ref[right], last)
+        send_ref[left] = jnp.where(lane < EDGE, send_ref[left], first)
+
+
+def third_kernel(
+    recv_ref,
+    x_ref,
+    diff_ref,
+    cor_ref,
+    mix_ref,
+    weight_ref,
+    tabs_ref,
+    map_ref,
+    out_ref,
+    send_ref,
+    last_row_ref,
+    first_row_ref,
+    group_s,
+    cycle_s,
+    weight_s,
+):
+    grp = lax.axis_index("grp")
+    gx = lax.axis_index("gx")
+
+    @pl.when(grp < 3)
+    def _():
+        feed_back(x_ref, out_ref, recv_ref, map_ref, group_s)
+        send_parent_edges(out_ref, send_ref, grp, gx, jnp.zeros((8, 128), F32))
+        last_row_ref[...] = out_ref[:, ROWS - 1, :]
+        first_row_ref[...] = out_ref[:, 0, :]
+
+    @pl.when(grp == 3)
+    def _():
+        update(x_ref, out_ref, recv_ref, None, None, diff_ref, cor_ref, mix_ref, grp, gx)
+        load_weights(weight_ref, weight_s, gx)
+        regroup(recv_ref, 0, PGROUPS, 5, SLOTS, group_s, 0)
+        regroup(recv_ref, PARENTS, 2, 16, HITS, group_s, PGROUPS)
+        interpolate(tabs_ref, T2_ROW, weight_s, group_s, GROUPS, cycle_s)
+        prescribe(out_ref, cycle_s, gx)
+        send_coarse(coarsen(out_ref), tabs_ref, send_ref)
+
+
+def fourth_kernel(
+    recv_ref,
+    x_ref,
+    diff_ref,
+    cor_ref,
+    mix_ref,
+    above_ref,
+    below_ref,
+    map_ref,
+    out_ref,
+    group_s,
+):
+    grp = lax.axis_index("grp")
+    gx = lax.axis_index("gx")
+
+    @pl.when(grp < 3)
+    def _():
+        update(x_ref, out_ref, recv_ref, above_ref, below_ref, diff_ref, cor_ref, mix_ref, grp, gx)
+        feed_back(out_ref, out_ref, recv_ref, map_ref, group_s)
+
+    @pl.when(grp == 3)
+    def _():
+        out_ref[...] = x_ref[...]
+
+
+def call(kernel, name, ins, spaces, outs, scratch):
+    return pl.pallas_call(
+        kernel,
+        name=name,
+        in_specs=[
+            pl.BlockSpec(memory_space=pltpu.SMEM if s == "s" else pltpu.VMEM) for s in spaces
+        ],
+        out_specs=[pl.BlockSpec(memory_space=pltpu.VMEM) for _ in outs],
+        out_shape=[jax.ShapeDtypeStruct(s, d) for s, d in outs],
+        scratch_shapes=[pltpu.VMEM(s, d) for s, d in scratch],
+        compiler_params=pltpu.CompilerParams(vmem_limit_bytes=VMEM_LIMIT),
+    )(*ins)
+
+
+STATE = ((LANES, ROWS, COLS), F32)
+BLOCKS = ((DEVICES, 8, 128), F32)
+RIM = ((LANES, COLS), F32)
+ROWMAJOR = ((ROWS, LANES, COLS), F32)
+GROUPED = ((GROUPS, LANES, 128), F32)
+CYCLE = ((3, LANES, 128), F32)
+WEIGHTS = ((16, 128), F32)
+TABS = ((TAB_ROWS, 128), jnp.int32)
+MAP = ((ROWS, 128), jnp.int32)
+TERMS = ((TILES, GX, 128), F32)
+
+
+def exchange(blocks):
+    return lax.all_to_all(blocks, ("grp", "gx"), 0, 0, tiled=True)
+
+
+def rims(last_row, first_row):
+    above = lax.ppermute(last_row, "grp", [(0, 1), (1, 2)])
+    below = lax.ppermute(first_row, "grp", [(1, 0), (2, 1)])
+    return above, below
+
+
+def shards(atmosphere, diffusion, coriolis, mixing, owner, cell, weight, fb_owner, fb_cell):
+    send, tabs, last_row, first_row = call(
+        first_kernel,
+        "tables",
+        (atmosphere, owner, cell, fb_owner, fb_cell, fb_owner, fb_cell),
+        "vvvvvss",
+        (BLOCKS, TABS, RIM, RIM),
+        (((TILES, GX, 128), jnp.int32), TERMS, TERMS, ROWMAJOR, ((128, 128), F32)),
+    )
+    above, below = rims(last_row, first_row)
+    recv = exchange(send)
+    state, send, flag, place = call(
+        second_kernel,
+        "substep_one",
+        (recv, atmosphere, diffusion, coriolis, mixing, above, below, weight, tabs, fb_owner, fb_cell),
+        "vvvssvvvvvv",
+        (STATE, BLOCKS, ((8, 128), F32), MAP),
+        (ROWMAJOR, GROUPED, CYCLE, WEIGHTS),
+    )
+    recv = exchange(send)
+    state, send, last_row, first_row = call(
+        third_kernel,
+        "substep_two",
+        (recv, state, diffusion, coriolis, mixing, weight, tabs, place),
+        "vvvssvvv",
+        (STATE, BLOCKS, RIM, RIM),
+        (GROUPED, CYCLE, WEIGHTS),
+    )
+    above, below = rims(last_row, first_row)
+    recv = exchange(send)
+    (state,) = call(
+        fourth_kernel,
+        "finish",
+        (recv, state, diffusion, coriolis, mixing, above, below, place),
+        "vvvssvvv",
+        (STATE,),
+        (GROUPED,),
+    )
+    inputs = (atmosphere, diffusion, coriolis, mixing, owner, cell, weight, fb_owner, fb_cell)
+    return lax.cond(flag[0, 127] > 0.5, lambda s, *a: dense_plan(*a), lambda s, *a: s, state, *inputs)
+
+
 def solution(mesh):
     placed = (P(None, "grp", "gx"), P("grp", "gx"), P("grp"), P(), P(), P(), P(), P(), P())
     return jax.shard_map(

time: 1920 us -> 104 us (0.05)
  waiting for transfers between devices: 1330 us -> 13.7 us
  local copies, waits for them, and re-layouts: 287 us -> 3.79 us
  blocking collectives: 192 us -> 21.3 us
  other arithmetic: 49.5 us -> 0 us
    reduce_scatter x2 -> x0, waiting for transfers between devices: 1310 us -> none  [shards(): lax.psum_scatter(everything, ('grp', 'gx'), scatter_dimension=1, tiled=True)]
    gather x6 -> x0, local copies, waits for them, and re-layouts: 186 us -> none  [shards(): cycle_terms = cycle_terms + jnp.take(flat_now, positions, axis=1) * weights]
    all_gather x2 -> x0, blocking collectives: 170 us -> none  [shards(): lax.all_gather(shared, 'gx', axis=1, tiled=True)]
    concatenate x10 -> x0, local copies, waits for them, and re-layouts: 33.3 us -> none  [the longest x2 21.5 us: shards(): everything = jnp.concatenate([padding, cycle_terms], axis=1)]
    add x4 -> x0, other arithmetic: 32 us -> none  [the longest x2 23.7 us: shards(): cycle_terms = cycle_terms + jnp.take(flat_now, positions, axis=1) * weights]
    scatter x7 -> x0, local copies, waits for them, and re-layouts: 28.6 us -> none  [the longest x3 22.6 us: shards(): fresh_flat.at[:, place_positions]]
    all_to_all x0 -> x2, starting transfers between devices: none -> 25.8 us  [exchange(): return lax.all_to_all(blocks, ('grp', 'gx'), 0, 0, tiled=True)]
    ppermute x8 -> x4, starting transfers between devices: 34.8 us -> 10.9 us  [the longest x2 7.09 us: rims(): above = lax.ppermute(last_row, 'grp', [(0, 1), (1, 2)])]
  transfers between devices with their start and end apart: 10 -> 6, of which waited for: 7 -> 4; matrix products, arithmetic and copies ran while one was open for 3% -> 2% of each run, Pallas kernels for 0% -> 0%
where the time goes in v1:
time: 104 us
  starting transfers between devices  36.8 us (35%)
  blocking collectives  21.3 us (20%)
  between operations  14.2 us (14%)
  waiting for transfers between devices  13.7 us (13%)
  Pallas kernels  13.5 us (13%)
  local copies, waits for them, and re-layouts  3.79 us (4%)
    all_to_all x2, starting transfers between devices, exchange(): return lax.all_to_all(blocks, ('grp', 'gx'), 0, 0, tiled=True)  25.8 us
    all_to_all x1, blocking collectives, exchange(): return lax.all_to_all(blocks, ('grp', 'gx'), 0, 0, tiled=True)  21.3 us
    pallas_call x4, Pallas kernels, call(): pl.pallas_call(kernel, name=name, in_specs=[pl.BlockSpec(memory_space=plt...  13.5 us
    all_to_all x2, waiting for transfers between devices, exchange(): return lax.all_to_all(blocks, ('grp', 'gx'), 0, 0, tiled=True)  8.23 us
    ppermute x2, starting transfers between devices, rims(): above = lax.ppermute(last_row, 'grp', [(0, 1), (1, 2)])  7.09 us
    ppermute x2, waiting for transfers between devices, rims(): below = lax.ppermute(first_row, 'grp', [(1, 0), (2, 1)])  5.46 us
    ppermute x2, starting transfers between devices, rims(): below = lax.ppermute(first_row, 'grp', [(1, 0), (2, 1)])  3.84 us
    unnamed x21, local copies, waits for them, and re-layouts  3.2 us
  transfers between devices with their start and end apart: 6, of which 4 were waited for; matrix products, arithmetic and copies ran while one was open for 2% of the time, Pallas kernels for 0%

profile of v1, /device:TPU:1, one launch (start us, length us, event | category | flops | bytes accessed | tf_op | source)
XLA Modules:
  0.0 103.5 jit_solution(3898085327111935157)
XLA Ops:
  6.5 0.0 copy-start.3
  6.5 0.0 copy-start.5
  6.5 0.0 copy-start
  6.5 0.0 copy-start.16
  6.5 0.0 copy-start.17
  6.6 0.0 copy-start.4
  6.6 0.0 copy-start.20
  6.6 0.0 copy-start.28
  6.6 0.0 copy-start.29
  6.6 1.1 %copy.204.owner_ref = s32[32,3,288]{2,1,0:T(4,128)S(1)} copy(s32[32,3,288]{2,0,1:T(8,128)} %param.33) | data formatting | bytes 221184 | tf_op args[4]
  7.7 1.0 copy.205.cell_ref
  8.7 4.3 %tables.1 = (f32[128,8,128]{2,1,0:T(8,128)}, s32[160,128]{1,0:T(8,128)S(1)}, f32[40,128]{1,0:T(8,128)S(1)}, f32[40,128]{1,0:T(8,128)S(1)}) custom-call(f32[40,16,128]{2,1,0:T(8,128)} %x_ref.3, s32[32,3,288]{2,1,0:T(4,128)S(1)} %copy.204.owner_ref, s32[32,3,288]{2,1,0:T(4,128)S(1)} %copy.205.cell_ref, s32[32,128]{1,0:T(8,128)} %fb_owner_ref.3, ...), custom_call_target="tpu_custom_call" | custom-call | tf_op jit(solution)/shard_map/tables/pallas_call | solution.py:697
  13.1 17.9 %all-to-all-start = ((f32[128,8,128]{2,1,0:T(8,128)}), f32[128,8,128]{2,1,0:T(8,128)S(1)}, u32[]{:S(2)}, u32[]{:S(2)}) async-start(f32[128,8,128]{2,1,0:T(8,128)} %get-tuple-element.145), calls=%async_computation.2 | async-start | bytes 1048576 | tf_op jit(solution)/shard_map/all_to_all | solution.py:723
  30.9 3.5 %collective-permute-start.8 = (f32[40,128]{1,0:T(8,128)S(1)}, f32[40,128]{1,0:T(8,128)S(1)}, u32[]{:S(2)}, u32[]{:S(2)}) collective-permute-start(f32[40,128]{1,0:T(8,128)S(1)} %get-tuple-element.146), channel_id=1, source_target_pairs={{0,32},{32,64},{1,33},{33,65},{2,34},{34,66},{3,35},{35,67},{4,36}... | collective-permute-start | bytes 61448 | tf_op jit(solution)/shard_map/ppermute | solution.py:727
  34.5 1.9 %collective-permute-start.9 = (f32[40,128]{1,0:T(8,128)S(1)}, f32[40,128]{1,0:T(8,128)S(1)}, u32[]{:S(2)}, u32[]{:S(2)}) collective-permute-start(f32[40,128]{1,0:T(8,128)S(1)} %get-tuple-element.147), channel_id=1, source_target_pairs={{32,0},{64,32},{33,1},{65,33},{34,2},{66,34},{35,3},{67,35},{36,4}... | collective-permute-start | bytes 61448 | tf_op jit(solution)/shard_map/ppermute | solution.py:728
  36.4 1.0 copy.206.weight_ref
  37.4 0.0 collective-permute-done.8.above_ref
  37.4 2.8 %collective-permute-done.9.below_ref = f32[40,128]{1,0:T(8,128)S(1)} collective-permute-done((f32[40,128]{1,0:T(8,128)S(1)}, f32[40,128]{1,0:T(8,128)S(1)}, u32[]{:S(2)}, u32[]{:S(2)}) %collective-permute-start.9) | collective-permute-done | bytes 20512 | tf_op jit(solution)/shard_map/ppermute | solution.py:728
  40.3 4.1 %all-to-all-done.recv_ref = f32[128,8,128]{2,1,0:T(8,128)S(1)} async-done(((f32[128,8,128]{2,1,0:T(8,128)}), f32[128,8,128]{2,1,0:T(8,128)S(1)}, u32[]{:S(2)}, u32[]{:S(2)}) %all-to-all-start) | async-done | bytes 524320 | tf_op jit(solution)/shard_map/all_to_all | solution.py:723
  44.4 3.0 %substep_one.1 = (f32[40,16,128]{2,1,0:T(8,128)S(1)}, f32[128,8,128]{2,1,0:T(8,128)S(1)}, f32[8,128]{1,0:T(8,128)S(1)}, s32[16,128]{1,0:T(8,128)S(1)}) custom-call(f32[128,8,128]{2,1,0:T(8,128)S(1)} %all-to-all-done.recv_ref, f32[40,16,128]{2,1,0:T(8,128)} %x_ref.3, f32[16,128]{1,0:T(8,128)} %diff_ref.5, f32[16]{0:T(128)} %cor_ref.5, f32[10]{0:T(128)} %mix_ref.5, ...), custom_call_target="tpu_custom_call" | custom-call | tf_op jit(solution)/shard_map/substep_one/pallas_call | solution.py:697
  47.4 21.3 %all_to_all.15.recv_ref = f32[128,8,128]{2,1,0:T(8,128)S(1)} all-to-all(f32[128,8,128]{2,1,0:T(8,128)S(1)} %get-tuple-element.150), channel_id=1, replica_groups=mesh['grp'=4,'gx'=32] {'grp','gx'}, dimensions={0} | all-to-all | bytes 1048576 | tf_op jit(solution)/shard_map/all_to_all | solution.py:723
  68.7 0.0 copy-done.20
  68.8 0.0 copy-done.28
  68.8 0.0 copy-done.29
  68.8 2.9 %substep_two.1 = (f32[40,16,128]{2,1,0:T(8,128)S(1)}, f32[128,8,128]{2,1,0:T(8,128)}, f32[40,128]{1,0:T(8,128)S(1)}, f32[40,128]{1,0:T(8,128)S(1)}) custom-call(f32[128,8,128]{2,1,0:T(8,128)S(1)} %all_to_all.15.recv_ref, f32[40,16,128]{2,1,0:T(8,128)S(1)} %get-tuple-element.151.x_ref, f32[16,128]{1,0:T(8,128)S(1)} %copy-done.20, f32[16]{0:T(128)S(1)} %copy-done.28, ...), custom_call_target="tpu_custom_call" | custom-call | tf_op jit(solution)/shard_map/substep_two/pallas_call | solution.py:697
  71.7 8.0 %all-to-all-start.2 = ((f32[128,8,128]{2,1,0:T(8,128)}), f32[128,8,128]{2,1,0:T(8,128)S(1)}, u32[]{:S(2)}, u32[]{:S(2)}) async-start(f32[128,8,128]{2,1,0:T(8,128)} %get-tuple-element.153), calls=%async_computation.4 | async-start | bytes 1048576 | tf_op jit(solution)/shard_map/all_to_all | solution.py:723
  79.7 3.5 %collective-permute-start.10 = (f32[40,128]{1,0:T(8,128)S(1)}, f32[40,128]{1,0:T(8,128)S(1)}, u32[]{:S(2)}, u32[]{:S(2)}) collective-permute-start(f32[40,128]{1,0:T(8,128)S(1)} %get-tuple-element.155), channel_id=1, source_target_pairs={{0,32},{32,64},{1,33},{33,65},{2,34},{34,66},{3,35},{35,67},{4,36}... | collective-permute-start | bytes 61448 | tf_op jit(solution)/shard_map/ppermute | solution.py:727
  83.3 1.9 %collective-permute-start.11 = (f32[40,128]{1,0:T(8,128)S(1)}, f32[40,128]{1,0:T(8,128)S(1)}, u32[]{:S(2)}, u32[]{:S(2)}) collective-permute-start(f32[40,128]{1,0:T(8,128)S(1)} %get-tuple-element.156), channel_id=1, source_target_pairs={{32,0},{64,32},{33,1},{65,33},{34,2},{66,34},{35,3},{67,35},{36,4}... | collective-permute-start | bytes 61448 | tf_op jit(solution)/shard_map/ppermute | solution.py:728
  85.2 0.6 slice.381
  86.4 0.0 collective-permute-done.10.above_ref
  86.4 2.6 %collective-permute-done.11.below_ref = f32[40,128]{1,0:T(8,128)S(1)} collective-permute-done((f32[40,128]{1,0:T(8,128)S(1)}, f32[40,128]{1,0:T(8,128)S(1)}, u32[]{:S(2)}, u32[]{:S(2)}) %collective-permute-start.11) | collective-permute-done | bytes 20512 | tf_op jit(solution)/shard_map/ppermute | solution.py:728
  89.0 4.1 %all-to-all-done.2.recv_ref = f32[128,8,128]{2,1,0:T(8,128)S(1)} async-done(((f32[128,8,128]{2,1,0:T(8,128)}), f32[128,8,128]{2,1,0:T(8,128)S(1)}, u32[]{:S(2)}, u32[]{:S(2)}) %all-to-all-start.2) | async-done | bytes 524320 | tf_op jit(solution)/shard_map/all_to_all | solution.py:723
  93.2 3.2 %finish.1 = f32[40,16,128]{2,1,0:T(8,128)} custom-call(f32[128,8,128]{2,1,0:T(8,128)S(1)} %all-to-all-done.2.recv_ref, f32[40,16,128]{2,1,0:T(8,128)S(1)} %get-tuple-element.154.x_ref, f32[16,128]{1,0:T(8,128)S(1)} %copy-done.20, f32[16]{0:T(128)S(1)} %copy-done.28, f32[10]{0:T(128)S(1)} %copy-done.29, f32[40,128]{1,0:T(8,128)S(1)} %collective-permute-done.10.above_ref, ...), custom_call_target="tpu_custom_call" | custom-call | tf_op jit(solution)/shard_map/finish/pallas_call | solution.py:697
  96.4 0.0 copy-done.3
  96.4 0.0 copy-done.5
  96.4 0.0 copy-done
  96.4 0.0 copy-done.16
  96.4 0.0 copy-done.17
  96.4 0.0 copy-done.4
  96.4 0.2 conditional.1
Async XLA Ops:
  6.5 89.9 %copy-start.3 = (s32[32,3,288]{2,0,1:T(8,128)S(1)}, s32[32,3,288]{2,0,1:T(8,128)}, u32[]{:S(2)}) copy-start(s32[32,3,288]{2,0,1:T(8,128)} %param.33) | copy-start | bytes 331780
  6.5 89.9 %copy-start.5 = (s32[32,3,288]{2,0,1:T(8,128)S(1)}, s32[32,3,288]{2,0,1:T(8,128)}, u32[]{:S(2)}) copy-start(s32[32,3,288]{2,0,1:T(8,128)} %param.34) | copy-start | bytes 331780
  6.5 89.9 %copy-start = (f32[40,16,128]{2,1,0:T(8,128)S(1)}, f32[40,16,128]{2,1,0:T(8,128)}, u32[]{:S(2)}) copy-start(f32[40,16,128]{2,1,0:T(8,128)} %x_ref.3) | copy-start | bytes 983044
  6.5 89.9 %copy-start.16 = (s32[32,128]{1,0:T(8,128)S(1)}, s32[32,128]{1,0:T(8,128)}, u32[]{:S(2)}) copy-start(s32[32,128]{1,0:T(8,128)} %fb_owner_ref.3) | copy-start | bytes 49156
  6.5 89.9 %copy-start.17 = (s32[32,128]{1,0:T(8,128)S(1)}, s32[32,128]{1,0:T(8,128)}, u32[]{:S(2)}) copy-start(s32[32,128]{1,0:T(8,128)} %fb_cell_ref.3) | copy-start | bytes 49156
  6.6 89.9 %copy-start.4 = (f32[32,3,288]{2,0,1:T(8,128)S(1)}, f32[32,3,288]{2,0,1:T(8,128)}, u32[]{:S(2)}) copy-start(f32[32,3,288]{2,0,1:T(8,128)} %param.35) | copy-start | bytes 331780
  6.6 62.2 %copy-start.20 = (f32[16,128]{1,0:T(8,128)S(1)}, f32[16,128]{1,0:T(8,128)}, u32[]{:S(2)}) copy-start(f32[16,128]{1,0:T(8,128)} %diff_ref.5) | copy-start | bytes 24580
  6.6 62.2 %copy-start.28 = (f32[16]{0:T(128)S(1)}, f32[16]{0:T(128)}, u32[]{:S(2)}) copy-start(f32[16]{0:T(128)} %cor_ref.5) | copy-start | bytes 196
  6.6 62.2 %copy-start.29 = (f32[10]{0:T(128)S(1)}, f32[10]{0:T(128)}, u32[]{:S(2)}) copy-start(f32[10]{0:T(128)} %mix_ref.5) | copy-start | bytes 124
  13.1 31.3 %all-to-all-start = ((f32[128,8,128]{2,1,0:T(8,128)}), f32[128,8,128]{2,1,0:T(8,128)S(1)}, u32[]{:S(2)}, u32[]{:S(2)}) async-start(f32[128,8,128]{2,1,0:T(8,128)} %get-tuple-element.145), calls=%async_computation.2 | async-start | bytes 1048576 | tf_op jit(solution)/shard_map/all_to_all | solution.py:723
  30.9 6.5 %collective-permute-start.8 = (f32[40,128]{1,0:T(8,128)S(1)}, f32[40,128]{1,0:T(8,128)S(1)}, u32[]{:S(2)}, u32[]{:S(2)}) collective-permute-start(f32[40,128]{1,0:T(8,128)S(1)} %get-tuple-element.146), channel_id=1, source_target_pairs={{0,32},{32,64},{1,33},{33,65},{2,34},{34,66},{3,35},{35,67},{4,36}... | collective-permute-start | bytes 61448 | tf_op jit(solution)/shard_map/ppermute | solution.py:727
  34.5 5.8 %collective-permute-start.9 = (f32[40,128]{1,0:T(8,128)S(1)}, f32[40,128]{1,0:T(8,128)S(1)}, u32[]{:S(2)}, u32[]{:S(2)}) collective-permute-start(f32[40,128]{1,0:T(8,128)S(1)} %get-tuple-element.147), channel_id=1, source_target_pairs={{32,0},{64,32},{33,1},{65,33},{34,2},{66,34},{35,3},{67,35},{36,4}... | collective-permute-start | bytes 61448 | tf_op jit(solution)/shard_map/ppermute | solution.py:728
  71.7 21.5 %all-to-all-start.2 = ((f32[128,8,128]{2,1,0:T(8,128)}), f32[128,8,128]{2,1,0:T(8,128)S(1)}, u32[]{:S(2)}, u32[]{:S(2)}) async-start(f32[128,8,128]{2,1,0:T(8,128)} %get-tuple-element.153), calls=%async_computation.4 | async-start | bytes 1048576 | tf_op jit(solution)/shard_map/all_to_all | solution.py:723
  79.7 6.7 %collective-permute-start.10 = (f32[40,128]{1,0:T(8,128)S(1)}, f32[40,128]{1,0:T(8,128)S(1)}, u32[]{:S(2)}, u32[]{:S(2)}) collective-permute-start(f32[40,128]{1,0:T(8,128)S(1)} %get-tuple-element.155), channel_id=1, source_target_pairs={{0,32},{32,64},{1,33},{33,65},{2,34},{34,66},{3,35},{35,67},{4,36}... | collective-permute-start | bytes 61448 | tf_op jit(solution)/shard_map/ppermute | solution.py:727
  83.3 5.8 %collective-permute-start.11 = (f32[40,128]{1,0:T(8,128)S(1)}, f32[40,128]{1,0:T(8,128)S(1)}, u32[]{:S(2)}, u32[]{:S(2)}) collective-permute-start(f32[40,128]{1,0:T(8,128)S(1)} %get-tuple-element.156), channel_id=1, source_target_pairs={{32,0},{64,32},{33,1},{65,33},{34,2},{66,34},{35,3},{67,35},{36,4}... | collective-permute-start | bytes 61448 | tf_op jit(solution)/shard_map/ppermute | solution.py:728

commit v2 on v1

--- a/solution.py
+++ b/solution.py
@@ -21,8 +21,7 @@
 EDGE = 40
 FG = 5
 T1_ROW = 128
-T2_ROW = 144
-TAB_ROWS = 160
+TAB_ROWS = 144
 PGROUPS = 20
 GROUPS = 22
 VMEM_LIMIT = 48 * 1024 * 1024
@@ -46,7 +45,26 @@
 
 def broadcast(value, axis, source):
     kept = jnp.where(lax.axis_index(axis) == source, value, 0).astype(value.dtype)
-    return lax.psum(kept, axis)
+    for other in range(lax.axis_size(axis)):
+        if other != source:
+            kept = kept + lax.ppermute(jnp.where(lax.axis_index(axis) == source, value, 0), axis, [(source, other)])
+    return kept
+
+
+def gather_columns(value, axis):
+    count = lax.axis_size(axis)
+    copies = jnp.broadcast_to(value[None], (count,) + value.shape)
+    blocks = lax.all_to_all(copies, axis, 0, 0, tiled=True)
+    return blocks.transpose(1, 0, 2).reshape(value.shape[0], -1)
+
+
+def reduce_cycle(terms, column_count, group_count):
+    blocks = terms.reshape(terms.shape[0], column_count, -1).transpose(1, 0, 2)
+    partial = lax.all_to_all(blocks, "gx", 0, 0, tiled=True).sum(axis=0)
+    total = partial
+    for group in range(group_count - 1):
+        total = total + lax.ppermute(partial, "grp", [(group, group_count - 1)])
+    return total
 
 
 def advance(extended, center, diffusion, coriolis, mixing):
@@ -107,9 +125,7 @@
             positions = jnp.where(mine, stencil_cell[:, member, :].reshape(-1), 0)
             weights = jnp.where(mine, stencil_weight[:, member, :].reshape(-1), 0.0)
             cycle_terms = cycle_terms + jnp.take(flat_now, positions, axis=1) * weights
-        padding = jnp.zeros((lane_count, (group_count - 1) * column_count * perimeter), jnp.float32)
-        everything = jnp.concatenate([padding, cycle_terms], axis=1)
-        cycle = lax.psum_scatter(everything, ("grp", "gx"), scatter_dimension=1, tiled=True)
+        cycle = reduce_cycle(cycle_terms, column_count, group_count)
         extended = padded(current, (("grp", 1), ("gx", 2)), 1)
         upper_rim = jnp.where(group_index == 0, extended[:, 1:2, :], extended[:, 0:1, :])
         lower_rim = jnp.where(
@@ -137,7 +153,7 @@
         shared = broadcast(coarse, "grp", group_count - 1)
         place_positions = jnp.where(owner_flat == own_rank, target_flat, cell_count)
         result_flat = fresh_flat.at[:, place_positions].set(
-            lax.all_gather(shared, "gx", axis=1, tiled=True), mode="drop"
+            gather_columns(shared, "gx"), mode="drop"
         )
         current = result_flat.reshape(lane_count, row_count, col_count)
     return current
@@ -254,7 +270,32 @@
     return jnp.concatenate([block, pltpu.roll(block, 128 - LANES, 1)], axis=0)
 
 
-def update(x_ref, out_ref, recv_ref, above_ref, below_ref, diff_ref, cor_ref, mix_ref, grp, gx):
+def update(x_ref, out_ref, diff_ref, cor_ref, mix_ref):
+    lane = iota((ROWS, COLS), 1)
+    row = iota((ROWS, COLS), 0)
+    diff = diff_ref[...]
+    cor = jnp.zeros((ROWS, COLS), F32)
+    for r in range(ROWS):
+        cor = jnp.where(row == r, cor_ref[r], cor)
+    for f in range(LANES):
+        level = f % LEVELS
+        x = x_ref[f]
+        up = jnp.where(row == 0, 0.0, pltpu.roll(x, 1, 0))
+        down = jnp.where(row == ROWS - 1, 0.0, pltpu.roll(x, ROWS - 1, 0))
+        westward = jnp.where(lane == 0, 0.0, pltpu.roll(x + down, 1, 1))
+        eastward = jnp.where(lane == COLS - 1, 0.0, pltpu.roll(x + up, COLS - 1, 1))
+        laplace = (westward + eastward) + (up + down) - 6.0 * x
+        upper = x if level == LEVELS - 1 else x_ref[f + 1]
+        lower = x if level == 0 else x_ref[f - 1]
+        extra = mix_ref[level] * (upper - 2.0 * x + lower)
+        if f < LEVELS:
+            extra = extra + cor * x_ref[f + LEVELS]
+        elif f < 2 * LEVELS:
+            extra = extra - cor * x_ref[f - LEVELS]
+        out_ref[f] = x + diff * laplace + extra
+
+
+def add_columns(from_ref, out_ref, recv_ref, diff_ref, grp, gx):
     nest = grp == 3
     right = lax.rem(gx + 1, GX)
     left = lax.rem(gx + GX - 1, GX)
@@ -266,43 +307,41 @@
     low_left = unpack_edge(recv_ref[jnp.minimum(grp + 1, 3) * GX + left])[0:1]
     top_right = jnp.where(grp == 0, from_right[0:1], top_right)
     low_left = jnp.where(grp == 2, from_left[ROWS - 1 : ROWS], low_left)
+    top_right = jnp.where(nest, 0.0, top_right)
+    low_left = jnp.where(nest, 0.0, low_left)
     left_sum = from_left + jnp.where(row == ROWS - 1, low_left, pltpu.roll(from_left, ROWS - 1, 0))
     right_sum = from_right + jnp.where(row == 0, top_right, pltpu.roll(from_right, 1, 0))
-    nest_left = from_left + jnp.where(row == ROWS - 1, 0.0, pltpu.roll(from_left, ROWS - 1, 0))
-    nest_right = from_right + jnp.where(row == 0, 0.0, pltpu.roll(from_right, 1, 0))
-    left_sum = jnp.where(nest, jnp.where(gx == 0, 0.0, nest_left), left_sum)
-    right_sum = jnp.where(nest, jnp.where(gx == GX - 1, 0.0, nest_right), right_sum)
+    left_sum = jnp.where(jnp.logical_and(nest, gx == 0), 0.0, left_sum)
+    right_sum = jnp.where(jnp.logical_and(nest, gx == GX - 1), 0.0, right_sum)
     diff = diff_ref[...]
-    cor = jnp.zeros((ROWS, COLS), F32)
-    for r in range(ROWS):
-        cor = jnp.where(row == r, cor_ref[r], cor)
+    left_sum = left_sum * diff[:, 0:1]
+    right_sum = right_sum * diff[:, COLS - 1 : COLS]
+    source = jnp.bitwise_and(EDGE + jnp.right_shift(lane + 1, 1), 127)
+    spread = jnp.concatenate(
+        [
+            jnp.where(
+                jnp.bitwise_and(lane[0:8], 1) == 0,
+                take(left_sum[h : h + 8], source[0:8]),
+                take(right_sum[h : h + 8], jnp.where(lane[0:8] == 127, EDGE, source[0:8])),
+            )
+            for h in (0, 8)
+        ],
+        axis=0,
+    )
+    outer = jnp.logical_or(lane == 0, lane == COLS - 1)
     for f in range(LANES):
-        level = f % LEVELS
-        x = x_ref[f]
-        if above_ref is None:
-            above = jnp.zeros((1, COLS), F32)
-            below = jnp.zeros((1, COLS), F32)
-        else:
-            above = jnp.where(grp == 0, x[0:1], above_ref[f : f + 1, :])
-            below = jnp.where(grp == 2, x[ROWS - 1 : ROWS], below_ref[f : f + 1, :])
-            above = jnp.where(nest, 0.0, above)
-            below = jnp.where(nest, 0.0, below)
-        up = jnp.where(row == 0, above, pltpu.roll(x, 1, 0))
-        down = jnp.where(row == ROWS - 1, below, pltpu.roll(x, ROWS - 1, 0))
-        at = EDGE + f
-        westward = jnp.where(lane == 0, left_sum[:, at : at + 1], pltpu.roll(x + down, 1, 1))
-        eastward = jnp.where(
-            lane == COLS - 1, right_sum[:, at : at + 1], pltpu.roll(x + up, COLS - 1, 1)
-        )
-        laplace = (westward + eastward) + (up + down) - 6.0 * x
-        upper = x if level == LEVELS - 1 else x_ref[f + 1]
-        lower = x if level == 0 else x_ref[f - 1]
-        extra = mix_ref[level] * (upper - 2.0 * x + lower)
-        if f < LEVELS:
-            extra = extra + cor * x_ref[f + LEVELS]
-        elif f < 2 * LEVELS:
-            extra = extra - cor * x_ref[f - LEVELS]
-        out_ref[f] = x + diff * laplace + extra
+        moved = spread if f == 0 else pltpu.roll(spread, 128 - 2 * f, 1)
+        out_ref[f] = from_ref[f] + jnp.where(outer, moved, 0.0)
+
+
+def add_rows(x_ref, out_ref, above_ref, below_ref, diff_ref, grp):
+    lane = iota((LANES, COLS), 1)
+    above = jnp.where(grp == 0, x_ref[:, 0, :], above_ref[...])
+    below = jnp.where(grp == 2, x_ref[:, ROWS - 1, :], below_ref[...])
+    above = above + jnp.where(lane == COLS - 1, 0.0, pltpu.roll(above, COLS - 1, 1))
+    below = below + jnp.where(lane == 0, 0.0, pltpu.roll(below, 1, 1))
+    out_ref[:, 0, :] = out_ref[:, 0, :] + diff_ref[0:1, :] * above
+    out_ref[:, ROWS - 1, :] = out_ref[:, ROWS - 1, :] + diff_ref[ROWS - 1 : ROWS, :] * below
 
 
 def regroup(recv_ref, base, groups, per, width, group_s, first):
@@ -346,7 +385,7 @@
 def load_weights(weight_ref, weight_s, gx):
     weight_s[...] = jnp.zeros((16, 128), F32)
     for k in range(3):
-        own = weight_ref[pl.ds(gx, 1), k, :]
+        own = weight_ref[k, pl.ds(gx, 1), :]
         weight_s[3 * k : 3 * k + 1, :] = own[:, 0:128]
         weight_s[3 * k + 1 : 3 * k + 2, :] = own[:, 128:256]
         weight_s[3 * k + 2 : 3 * k + 3, 0:32] = own[:, 256:288]
@@ -380,13 +419,14 @@
     return coarse
 
 
-def send_coarse(coarse, tabs_ref, send_ref):
-    group_of = iota((8, 128), 1) // SLOTS
+def send_coarse(coarse, tabs_ref, send_ref, base):
+    lane = iota((8, 128), 1)
+    group_of = lane // SLOTS
 
     def body(o):
         index = jnp.broadcast_to(tabs_ref[pl.ds(o, 1), :], (8, 128))
-        block = take(coarse[0:8], index)
-        for k in range(1, FG):
+        block = base
+        for k in range(FG):
             block = jnp.where(group_of == k, take(coarse[8 * k : 8 * k + 8], index), block)
         send_ref[o] = block
 
@@ -449,58 +489,68 @@
     map_ref[...] = jnp.where(block < 0, -1, code)
 
 
-def first_kernel(
-    x_ref,
-    owner_ref,
-    cell_ref,
-    fb_owner_ref,
-    fb_cell_ref,
-    fb_owner_sm,
-    fb_cell_sm,
-    send_ref,
-    tabs_ref,
-    last_row_ref,
-    first_row_ref,
-    gid_s,
-    mark_s,
-    value_s,
-    rows_s,
-    turned_s,
-):
-    grp = lax.axis_index("grp")
-    gx = lax.axis_index("gx")
-    me = grp * GX + gx
-    lane = iota((8, 128), 1)
-    last_row_ref[...] = x_ref[:, ROWS - 1, :]
-    first_row_ref[...] = x_ref[:, 0, :]
+def load_terms(owner_ref, cell_ref, gid_s):
     for k in range(3):
-        gid = owner_ref[:, k, :] * 2048 + cell_ref[:, k, :]
+        gid = owner_ref[k] * 2048 + cell_ref[k]
         gid_s[3 * k] = gid[:, 0:128]
         gid_s[3 * k + 1] = gid[:, 128:256]
         gid_s[3 * k + 2] = jnp.full((GX, 128), -1, jnp.int32)
         gid_s[3 * k + 2, :, 0:32] = gid[:, 256:288]
 
-    def flag_block(over):
-        worst = jnp.max(over, axis=0, keepdims=True)
-        flag = jnp.where(worst > 0.5, 1.0, 0.0)
-        return jnp.where(lane == 127, jnp.broadcast_to(flag, (8, 128)), 0.0)
+
+def flag_block(over):
+    worst = jnp.max(over, axis=0, keepdims=True)
+    flag = jnp.where(worst > 0.5, 1.0, 0.0)
+    return jnp.where(iota((8, 128), 1) == 127, jnp.broadcast_to(flag, (8, 128)), 0.0)
+
+
+def first_kernel(
+    x_ref, owner_ref, cell_ref, send_ref, table_ref, flag_ref, last_row_ref, first_row_ref,
+    gid_s, mark_s, value_s, rows_s,
+):
+    grp = lax.axis_index("grp")
+    gx = lax.axis_index("gx")
+    blank = jnp.zeros((8, 128), F32)
+    last_row_ref[...] = x_ref[:, ROWS - 1, :]
+    first_row_ref[...] = x_ref[:, 0, :]
 
     @pl.when(grp < 3)
     def _():
+        load_terms(owner_ref, cell_ref, gid_s)
         gids = [gid_s[t] for t in range(TILES)]
-        masks = [jnp.right_shift(g, 11) == me for g in gids]
+        masks = [jnp.right_shift(g, 11) == grp * GX + gx for g in gids]
         values = [jnp.bitwise_and(g, 2047).astype(F32) for g in gids]
         table, total = slot_table(masks, values, SLOTS, mark_s, value_s)
-        tabs_ref[0:GX, :] = table.astype(jnp.int32)
-        base = flag_block(jnp.where(total > float(SLOTS), 1.0, 0.0))
-        send_ref[...] = jnp.broadcast_to(base[None], (DEVICES, 8, 128))
+        table_ref[...] = table.astype(jnp.int32)
+        flag_ref[...] = flag_block(jnp.where(total > float(SLOTS), 1.0, 0.0))
         for r in range(ROWS):
             rows_s[r] = x_ref[:, r, :]
-        send_cells(rows_s, tabs_ref, send_ref, base)
-        send_parent_edges(x_ref, send_ref, grp, gx, base)
+        send_cells(rows_s, table_ref, send_ref, None)
+        send_parent_edges(x_ref, send_ref, grp, gx, blank)
 
     @pl.when(grp == 3)
     def _():
+        send_ref[PARENTS + lax.rem(gx + 1, GX)] = edge_block(x_ref, COLS - 1, blank)
+        send_ref[PARENTS + lax.rem(gx + GX - 1, GX)] = edge_block(x_ref, 0, blank)
+
+
+def tables_kernel(
+    x_ref, diff_ref, cor_ref, mix_ref, owner_ref, cell_ref, fb_owner_ref, fb_cell_ref,
+    fb_owner_sm, fb_cell_sm, flag_in_ref, fresh_ref, tabs_ref, flag_ref, map_ref,
+    gid_s, mark_s, value_s,
+):
+    grp = lax.axis_index("grp")
+    gx = lax.axis_index("gx")
+    update(x_ref, fresh_ref, diff_ref, cor_ref, mix_ref)
+
+    @pl.when(grp < 3)
+    def _():
+        flag_ref[...] = flag_in_ref[...]
+        feedback_map(fb_owner_ref, fb_cell_ref, map_ref, grp * GX + gx)
+
+    @pl.when(grp == 3)
+    def _():
+        load_terms(owner_ref, cell_ref, gid_s)
         own = fb_owner_ref[pl.ds(gx, 1), :]
         hot = iota((PARENTS, 128), 0) == own
         found, total = ranks([hot])
@@ -516,17 +566,15 @@
         )
         tabs_ref[0:PARENTS, :] = table.astype(jnp.int32)
 
-        terms = [gid_s[t, pl.ds(gx, 1), :] for t in range(TILES)]
-        owners = [jnp.right_shift(t, 11) for t in terms]
+        owners = [jnp.right_shift(gid_s[t, pl.ds(gx, 1), :], 11) for t in range(TILES)]
         hots = [iota((PARENTS, 128), 0) == o for o in owners]
         found, _ = ranks(hots)
-        codes = []
         for t in range(TILES):
             slot = jnp.sum(jnp.where(hots[t], found[t], 0.0), axis=0, keepdims=True)
             slot = jnp.minimum(slot.astype(jnp.int32), SLOTS - 1)
             group = jnp.right_shift(owners[t] * 205, 10)
-            codes.append(group * 128 + (owners[t] - 5 * group) * SLOTS + slot)
-            tabs_ref[T1_ROW + t : T1_ROW + t + 1, :] = codes[t]
+            code = group * 128 + (owners[t] - 5 * group) * SLOTS + slot
+            tabs_ref[T1_ROW + t : T1_ROW + t + 1, :] = code
 
         def seek(c, found_at):
             for s in range(4):
@@ -542,10 +590,58 @@
         )
         tabs_ref[PARENTS : PARENTS + GX, :] = table.astype(jnp.int32)
         over = jnp.maximum(
-            over,
-            jnp.max(jnp.where(total > float(HITS), 1.0, 0.0), axis=0, keepdims=True),
-        )
-
+            over, jnp.max(jnp.where(total > float(HITS), 1.0, 0.0), axis=0, keepdims=True)
+        )
+        flag_ref[...] = flag_block(over)
+
+
+def second_kernel(
+    recv_ref, x_ref, fresh_ref, diff_ref, above_ref, below_ref, weight_ref, table_ref, tabs_ref,
+    flag_ref, out_ref, send_ref, rows_s, group_s, cycle_s, weight_s,
+):
+    grp = lax.axis_index("grp")
+    gx = lax.axis_index("gx")
+    add_columns(fresh_ref, out_ref, recv_ref, diff_ref, grp, gx)
+    base = flag_ref[...]
+
+    @pl.when(grp < 3)
+    def _():
+        add_rows(x_ref, out_ref, above_ref, below_ref, diff_ref, grp)
+        for r in range(ROWS):
+            rows_s[r] = out_ref[:, r, :]
+        for d in range(PARENTS):
+            send_ref[d] = base
+        send_cells(rows_s, table_ref, send_ref, base)
+
+    @pl.when(grp == 3)
+    def _():
+        load_weights(weight_ref, weight_s, gx)
+        regroup(recv_ref, 0, PGROUPS, 5, SLOTS, group_s, 0)
+        interpolate(tabs_ref, T1_ROW, weight_s, group_s, PGROUPS, cycle_s)
+        prescribe(out_ref, cycle_s, gx)
+        coarse = coarsen(out_ref)
+        send_coarse(coarse, tabs_ref, send_ref, base)
+        first = edge_block(out_ref, 0, base)
+        last = edge_block(out_ref, COLS - 1, base)
+        send_hits(coarse, tabs_ref, send_ref, base)
+        lane = iota((8, 128), 1)
+        right = PARENTS + lax.rem(gx + 1, GX)
+        left = PARENTS + lax.rem(gx + GX - 1, GX)
+        send_ref[right] = jnp.where(lane < EDGE, send_ref[right], last)
+        send_ref[left] = jnp.where(lane < EDGE, send_ref[left], first)
+
+
+def hits_kernel(
+    x_ref, diff_ref, cor_ref, mix_ref, owner_ref, cell_ref, fb_owner_ref, fb_cell_ref, tabs_ref,
+    fresh_ref, codes_ref, gid_s, turned_s,
+):
+    gx = lax.axis_index("gx")
+
+    @pl.when(lax.axis_index("grp") == 3)
+    def _():
+        update(x_ref, fresh_ref, diff_ref, cor_ref, mix_ref)
+        load_terms(owner_ref, cell_ref, gid_s)
+        terms = [gid_s[t, pl.ds(gx, 1), :] for t in range(TILES)]
         fed = (fb_owner_ref[...] * 2048 + fb_cell_ref[...]).astype(F32)
         turned_s[...] = jnp.concatenate([fed, jnp.full((96, 128), -2.0, F32)], axis=0).T
         wide = [jnp.broadcast_to(t.astype(F32), (8, 128)) for t in terms]
@@ -567,133 +663,64 @@
             slot = jnp.minimum(slot.astype(jnp.int32), HITS - 1)
             code = (PGROUPS + jnp.right_shift(sources[t], 4)) * 128
             code = code + jnp.bitwise_and(sources[t], 15) * HITS + slot
-            tabs_ref[T2_ROW + t : T2_ROW + t + 1, :] = jnp.where(sources[t] >= 0, code, codes[t])
-
-        base = flag_block(over)
-        send_ref[...] = jnp.broadcast_to(base[None], (DEVICES, 8, 128))
-        send_ref[PARENTS + lax.rem(gx + 1, GX)] = edge_block(x_ref, COLS - 1, base)
-        send_ref[PARENTS + lax.rem(gx + GX - 1, GX)] = edge_block(x_ref, 0, base)
-
-
-def second_kernel(
-    recv_ref,
-    x_ref,
-    diff_ref,
-    cor_ref,
-    mix_ref,
-    above_ref,
-    below_ref,
-    weight_ref,
-    tabs_ref,
-    fb_owner_ref,
-    fb_cell_ref,
-    out_ref,
-    send_ref,
-    flag_ref,
-    map_ref,
-    rows_s,
-    group_s,
-    cycle_s,
-    weight_s,
+            plain = tabs_ref[T1_ROW + t : T1_ROW + t + 1, :]
+            codes_ref[t : t + 1, :] = jnp.where(sources[t] >= 0, code, plain)
+
+
+def third_kernel(
+    recv_ref, x_ref, fresh_ref, diff_ref, weight_ref, tabs_ref, codes_ref, map_ref,
+    out_ref, send_ref, flag_ref, last_row_ref, first_row_ref, group_s, cycle_s, weight_s,
 ):
     grp = lax.axis_index("grp")
     gx = lax.axis_index("gx")
+    blank = jnp.zeros((8, 128), F32)
     flag = recv_ref[0]
     for d in range(1, DEVICES):
         flag = jnp.maximum(flag, recv_ref[d])
     flag_ref[...] = flag
-    update(x_ref, out_ref, recv_ref, above_ref, below_ref, diff_ref, cor_ref, mix_ref, grp, gx)
 
     @pl.when(grp < 3)
     def _():
-        for r in range(ROWS):
-            rows_s[r] = out_ref[:, r, :]
-        send_cells(rows_s, tabs_ref, send_ref, None)
-        feedback_map(fb_owner_ref, fb_cell_ref, map_ref, grp * GX + gx)
+        feed_back(x_ref, out_ref, recv_ref, map_ref, group_s)
+        send_parent_edges(out_ref, send_ref, grp, gx, blank)
+        last_row_ref[...] = out_ref[:, ROWS - 1, :]
+        first_row_ref[...] = out_ref[:, 0, :]
 
     @pl.when(grp == 3)
     def _():
+        add_columns(fresh_ref, out_ref, recv_ref, diff_ref, grp, gx)
         load_weights(weight_ref, weight_s, gx)
         regroup(recv_ref, 0, PGROUPS, 5, SLOTS, group_s, 0)
-        interpolate(tabs_ref, T1_ROW, weight_s, group_s, PGROUPS, cycle_s)
+        regroup(recv_ref, PARENTS, 2, 16, HITS, group_s, PGROUPS)
+        interpolate(codes_ref, 0, weight_s, group_s, GROUPS, cycle_s)
         prescribe(out_ref, cycle_s, gx)
-        coarse = coarsen(out_ref)
-        send_coarse(coarse, tabs_ref, send_ref)
-        blank = jnp.zeros((8, 128), F32)
-        first = edge_block(out_ref, 0, blank)
-        last = edge_block(out_ref, COLS - 1, blank)
-        send_hits(coarse, tabs_ref, send_ref, blank)
-        lane = iota((8, 128), 1)
-        right = PARENTS + lax.rem(gx + 1, GX)
-        left = PARENTS + lax.rem(gx + GX - 1, GX)
-        send_ref[right] = jnp.where(lane < EDGE, send_ref[right], last)
-        send_ref[left] = jnp.where(lane < EDGE, send_ref[left], first)
-
-
-def third_kernel(
-    recv_ref,
-    x_ref,
-    diff_ref,
-    cor_ref,
-    mix_ref,
-    weight_ref,
-    tabs_ref,
-    map_ref,
-    out_ref,
-    send_ref,
-    last_row_ref,
-    first_row_ref,
-    group_s,
-    cycle_s,
-    weight_s,
+        send_coarse(coarsen(out_ref), tabs_ref, send_ref, blank)
+
+
+def parents_kernel(x_ref, diff_ref, cor_ref, mix_ref, fresh_ref):
+    @pl.when(lax.axis_index("grp") < 3)
+    def _():
+        update(x_ref, fresh_ref, diff_ref, cor_ref, mix_ref)
+
+
+def fourth_kernel(
+    recv_ref, x_ref, fresh_ref, diff_ref, above_ref, below_ref, map_ref, out_ref, group_s
 ):
     grp = lax.axis_index("grp")
     gx = lax.axis_index("gx")
 
     @pl.when(grp < 3)
     def _():
-        feed_back(x_ref, out_ref, recv_ref, map_ref, group_s)
-        send_parent_edges(out_ref, send_ref, grp, gx, jnp.zeros((8, 128), F32))
-        last_row_ref[...] = out_ref[:, ROWS - 1, :]
-        first_row_ref[...] = out_ref[:, 0, :]
+        add_columns(fresh_ref, out_ref, recv_ref, diff_ref, grp, gx)
+        add_rows(x_ref, out_ref, above_ref, below_ref, diff_ref, grp)
+        feed_back(out_ref, out_ref, recv_ref, map_ref, group_s)
 
     @pl.when(grp == 3)
     def _():
-        update(x_ref, out_ref, recv_ref, None, None, diff_ref, cor_ref, mix_ref, grp, gx)
-        load_weights(weight_ref, weight_s, gx)
-        regroup(recv_ref, 0, PGROUPS, 5, SLOTS, group_s, 0)
-        regroup(recv_ref, PARENTS, 2, 16, HITS, group_s, PGROUPS)
-        interpolate(tabs_ref, T2_ROW, weight_s, group_s, GROUPS, cycle_s)
-        prescribe(out_ref, cycle_s, gx)
-        send_coarse(coarsen(out_ref), tabs_ref, send_ref)
-
-
-def fourth_kernel(
-    recv_ref,
-    x_ref,
-    diff_ref,
-    cor_ref,
-    mix_ref,
-    above_ref,
-    below_ref,
-    map_ref,
-    out_ref,
-    group_s,
-):
-    grp = lax.axis_index("grp")
-    gx = lax.axis_index("gx")
-
-    @pl.when(grp < 3)
-    def _():
-        update(x_ref, out_ref, recv_ref, above_ref, below_ref, diff_ref, cor_ref, mix_ref, grp, gx)
-        feed_back(out_ref, out_ref, recv_ref, map_ref, group_s)
-
-    @pl.when(grp == 3)
-    def _():
         out_ref[...] = x_ref[...]
 
 
-def call(kernel, name, ins, spaces, outs, scratch):
+def call(kernel, name, ins, spaces, outs, scratch, flops=1000000):
     return pl.pallas_call(
         kernel,
         name=name,
@@ -704,6 +731,7 @@
         out_shape=[jax.ShapeDtypeStruct(s, d) for s, d in outs],
         scratch_shapes=[pltpu.VMEM(s, d) for s, d in scratch],
         compiler_params=pltpu.CompilerParams(vmem_limit_bytes=VMEM_LIMIT),
+        cost_estimate=pl.CostEstimate(flops=flops, bytes_accessed=4000000, transcendentals=0),
     )(*ins)
 
 
@@ -715,6 +743,10 @@
 CYCLE = ((3, LANES, 128), F32)
 WEIGHTS = ((16, 128), F32)
 TABS = ((TAB_ROWS, 128), jnp.int32)
+TABLE = ((GX, 128), jnp.int32)
+CODES = ((16, 128), jnp.int32)
+BLOCK = ((8, 128), F32)
+GIDS = ((TILES, GX, 128), jnp.int32)
 MAP = ((ROWS, 128), jnp.int32)
 TERMS = ((TILES, GX, 128), F32)
 
@@ -730,44 +762,63 @@
 
 
 def shards(atmosphere, diffusion, coriolis, mixing, owner, cell, weight, fb_owner, fb_cell):
-    send, tabs, last_row, first_row = call(
+    inputs = (atmosphere, diffusion, coriolis, mixing, owner, cell, weight, fb_owner, fb_cell)
+    owner, cell, weight = (jnp.transpose(a, (1, 0, 2)) for a in (owner, cell, weight))
+    physics = (diffusion, coriolis, mixing)
+    send, table, flag, last_row, first_row = call(
         first_kernel,
+        "first_cells",
+        (atmosphere, owner, cell),
+        "vvv",
+        (BLOCKS, TABLE, BLOCK, RIM, RIM),
+        (GIDS, TERMS, TERMS, ROWMAJOR),
+    )
+    recv = exchange(send)
+    above, below = rims(last_row, first_row)
+    fresh, tabs, flag, place = call(
+        tables_kernel,
         "tables",
-        (atmosphere, owner, cell, fb_owner, fb_cell, fb_owner, fb_cell),
-        "vvvvvss",
-        (BLOCKS, TABS, RIM, RIM),
-        (((TILES, GX, 128), jnp.int32), TERMS, TERMS, ROWMAJOR, ((128, 128), F32)),
-    )
-    above, below = rims(last_row, first_row)
-    recv = exchange(send)
-    state, send, flag, place = call(
+        (atmosphere,) + physics + (owner, cell, fb_owner, fb_cell, fb_owner, fb_cell, flag),
+        "vvssvvvvssv",
+        (STATE, TABS, BLOCK, MAP),
+        (GIDS, TERMS, TERMS),
+    )
+    state, send = call(
         second_kernel,
         "substep_one",
-        (recv, atmosphere, diffusion, coriolis, mixing, above, below, weight, tabs, fb_owner, fb_cell),
-        "vvvssvvvvvv",
-        (STATE, BLOCKS, ((8, 128), F32), MAP),
+        (recv, atmosphere, fresh, diffusion, above, below, weight, table, tabs, flag),
+        "vvvvvvvvvv",
+        (STATE, BLOCKS),
         (ROWMAJOR, GROUPED, CYCLE, WEIGHTS),
     )
     recv = exchange(send)
-    state, send, last_row, first_row = call(
+    fresh, codes = call(
+        hits_kernel,
+        "hits",
+        (state,) + physics + (owner, cell, fb_owner, fb_cell, tabs),
+        "vvssvvvvv",
+        (STATE, CODES),
+        (GIDS, ((128, 128), F32)),
+    )
+    state, send, flag, last_row, first_row = call(
         third_kernel,
         "substep_two",
-        (recv, state, diffusion, coriolis, mixing, weight, tabs, place),
-        "vvvssvvv",
-        (STATE, BLOCKS, RIM, RIM),
+        (recv, state, fresh, diffusion, weight, tabs, codes, place),
+        "vvvvvvvv",
+        (STATE, BLOCKS, BLOCK, RIM, RIM),
         (GROUPED, CYCLE, WEIGHTS),
     )
+    recv = exchange(send)
     above, below = rims(last_row, first_row)
-    recv = exchange(send)
+    (fresh,) = call(parents_kernel, "parents", (state,) + physics, "vvss", (STATE,), ())
     (state,) = call(
         fourth_kernel,
         "finish",
-        (recv, state, diffusion, coriolis, mixing, above, below, place),
-        "vvvssvvv",
+        (recv, state, fresh, diffusion, above, below, place),
+        "vvvvvvv",
         (STATE,),
         (GROUPED,),
     )
-    inputs = (atmosphere, diffusion, coriolis, mixing, owner, cell, weight, fb_owner, fb_cell)
     return lax.cond(flag[0, 127] > 0.5, lambda s, *a: dense_plan(*a), lambda s, *a: s, state, *inputs)
 
 

time: 104 us -> 81.2 us (0.78)
  blocking collectives: 21.3 us -> 0 us
  between operations: 14.2 us -> 0.88 us
  waiting for transfers between devices: 13.7 us -> 24.3 us
  local copies, waits for them, and re-layouts: 3.79 us -> 1.35 us
  Pallas kernels: 13.5 us -> 15.7 us
  starting transfers between devices: 36.8 us -> 38.2 us
    all_to_all x1 -> x0, blocking collectives: 21.3 us -> none  [exchange(): return lax.all_to_all(blocks, ('grp', 'gx'), 0, 0, tiled=True)]
    all_to_all x2 -> x3, waiting for transfers between devices: 8.23 us -> 21.1 us  [exchange(): return lax.all_to_all(blocks, ('grp', 'gx'), 0, 0, tiled=True)]
    unnamed x21 -> x20, local copies, waits for them, and re-layouts: 3.2 us -> 0.77 us
    pallas_call x4 -> x7, Pallas kernels: 13.5 us -> 15.7 us  [call(): pl.pallas_call(kernel, name=name, in_specs=[pl.BlockSpec(memory_space=plt...]
    ppermute x2, waiting for transfers between devices: 5.46 us -> 3.25 us  [rims(): below = lax.ppermute(first_row, 'grp', [(1, 0), (2, 1)])]
    all_to_all x2 -> x3, starting transfers between devices: 25.8 us -> 27.3 us  [exchange(): return lax.all_to_all(blocks, ('grp', 'gx'), 0, 0, tiled=True)]
  transfers between devices with their start and end apart: 6 -> 7, of which waited for: 4 -> 5; matrix products, arithmetic and copies ran while one was open for 2% -> 1% of each run, Pallas kernels for 0% -> 5%
where the time goes in v2:
time: 81.2 us; the launch traced here: 80.7 us
  starting transfers between devices  38.2 us (47%)
  waiting for transfers between devices  24.3 us (30%)
  Pallas kernels  15.7 us (19%)
  local copies, waits for them, and re-layouts  1.35 us (2%)
  between operations  0.88 us (1%)
    all_to_all x3, starting transfers between devices, exchange(): return lax.all_to_all(blocks, ('grp', 'gx'), 0, 0, tiled=True)  27.3 us
    all_to_all x3, waiting for transfers between devices, exchange(): return lax.all_to_all(blocks, ('grp', 'gx'), 0, 0, tiled=True)  21.1 us
    pallas_call x7, Pallas kernels, call(): pl.pallas_call(kernel, name=name, in_specs=[pl.BlockSpec(memory_space=plt...  15.7 us
    ppermute x2, starting transfers between devices, rims(): above = lax.ppermute(last_row, 'grp', [(0, 1), (1, 2)])  7.09 us
    ppermute x2, starting transfers between devices, rims(): below = lax.ppermute(first_row, 'grp', [(1, 0), (2, 1)])  3.84 us
    ppermute x2, waiting for transfers between devices, rims(): below = lax.ppermute(first_row, 'grp', [(1, 0), (2, 1)])  3.25 us
  transfers between devices with their start and end apart: 7, of which 5 were waited for; matrix products, arithmetic and copies ran while one was open for 1% of the time, Pallas kernels for 5%

profile of v2, /device:TPU:1, one launch (start us, length us, event | category | flops | bytes accessed | tf_op | source)
XLA Modules:
  0.0 80.7 jit_solution(10343069400467904083)
XLA Ops:
  0.0 0.0 copy-start.2
  0.0 0.0 copy-start.3
  0.0 0.0 copy-start.5
  0.0 0.0 copy-start.27
  0.0 0.0 copy-start.30
  0.0 0.0 copy-start.15
  0.0 0.0 copy-start.18
  0.1 0.0 copy-start.4
  0.1 4.1 %first_cells.1 = (f32[128,8,128]{2,1,0:T(8,128)}, s32[32,128]{1,0:T(8,128)S(1)}, f32[8,128]{1,0:T(8,128)S(1)}, f32[40,128]{1,0:T(8,128)S(1)}, f32[40,128]{1,0:T(8,128)S(1)}) custom-call(f32[40,16,128]{2,1,0:T(8,128)} %x_ref.5, s32[3,32,288]{2,1,0:T(8,128)} %bitcast.171, s32[3,32,288]{2,1,0:T(8,128)} %bitcast.174), custom_call_target="tpu_custom_call" | custom-call | flops 1000000 | bytes 4000000 | tf_op jit(solution)/shard_map/first_cells/pallas_call | solution.py:724
  4.2 0.0 copy-start
  4.2 11.5 %all-to-all-start.4 = ((f32[128,8,128]{2,1,0:T(8,128)}), f32[128,8,128]{2,1,0:T(8,128)S(1)}, u32[]{:S(2)}, u32[]{:S(2)}) async-start(f32[128,8,128]{2,1,0:T(8,128)} %get-tuple-element.151), calls=%async_computation.4 | async-start | bytes 1048576 | tf_op jit(solution)/shard_map/all_to_all | solution.py:755
  15.7 3.5 %collective-permute-start.20 = (f32[40,128]{1,0:T(8,128)S(1)}, f32[40,128]{1,0:T(8,128)S(1)}, u32[]{:S(2)}, u32[]{:S(2)}) collective-permute-start(f32[40,128]{1,0:T(8,128)S(1)} %get-tuple-element.154), channel_id=1, source_target_pairs={{0,32},{32,64},{1,33},{33,65},{2,34},{34,66},{3,35},{35,67},{4,36}... | collective-permute-start | bytes 61448 | tf_op jit(solution)/shard_map/ppermute | solution.py:759
  19.2 1.9 %collective-permute-start.21 = (f32[40,128]{1,0:T(8,128)S(1)}, f32[40,128]{1,0:T(8,128)S(1)}, u32[]{:S(2)}, u32[]{:S(2)}) collective-permute-start(f32[40,128]{1,0:T(8,128)S(1)} %get-tuple-element.155), channel_id=1, source_target_pairs={{32,0},{64,32},{33,1},{65,33},{34,2},{66,34},{35,3},{67,35},{36,4}... | collective-permute-start | bytes 61448 | tf_op jit(solution)/shard_map/ppermute | solution.py:760
  21.2 2.4 %tables.1 = (f32[40,16,128]{2,1,0:T(8,128)S(1)}, s32[144,128]{1,0:T(8,128)S(1)}, f32[8,128]{1,0:T(8,128)S(1)}, s32[16,128]{1,0:T(8,128)S(1)}) custom-call(f32[40,16,128]{2,1,0:T(8,128)} %x_ref.5, f32[16,128]{1,0:T(8,128)} %diff_ref.11, f32[16]{0:T(128)} %cor_ref.5, f32[10]{0:T(128)} %mix_ref.5, s32[3,32,288]{2,1,0:T(8,128)} %bitcast.172, ...), custom_call_target="tpu_custom_call" | custom-call | flops 1000000 | bytes 4000000 | tf_op jit(solution)/shard_map/tables/pallas_call | solution.py:724
  23.6 0.0 collective-permute-done.20.above_ref
  23.6 1.5 %collective-permute-done.21.below_ref = f32[40,128]{1,0:T(8,128)S(1)} collective-permute-done((f32[40,128]{1,0:T(8,128)S(1)}, f32[40,128]{1,0:T(8,128)S(1)}, u32[]{:S(2)}, u32[]{:S(2)}) %collective-permute-start.21) | collective-permute-done | bytes 20512 | tf_op jit(solution)/shard_map/ppermute | solution.py:760
  25.0 4.1 %all-to-all-done.4.recv_ref = f32[128,8,128]{2,1,0:T(8,128)S(1)} async-done(((f32[128,8,128]{2,1,0:T(8,128)}), f32[128,8,128]{2,1,0:T(8,128)S(1)}, u32[]{:S(2)}, u32[]{:S(2)}) %all-to-all-start.4) | async-done | bytes 524320 | tf_op jit(solution)/shard_map/all_to_all | solution.py:755
  29.1 3.5 %substep_one.1 = (f32[40,16,128]{2,1,0:T(8,128)S(1)}, f32[128,8,128]{2,1,0:T(8,128)}) custom-call(f32[128,8,128]{2,1,0:T(8,128)S(1)} %all-to-all-done.4.recv_ref, f32[40,16,128]{2,1,0:T(8,128)} %x_ref.5, f32[40,16,128]{2,1,0:T(8,128)S(1)} %get-tuple-element.153.fresh_ref, f32[16,128]{1,0:T(8,128)} %diff_ref.11, ...), custom_call_target="tpu_custom_call" | custom-call | flops 1000000 | bytes 4000000 | tf_op jit(solution)/shard_map/substep_one/pallas_call | solution.py:724
  32.7 8.1 %all-to-all-start.5 = ((f32[128,8,128]{2,1,0:T(8,128)}), f32[128,8,128]{2,1,0:T(8,128)S(1)}, u32[]{:S(2)}, u32[]{:S(2)}) async-start(f32[128,8,128]{2,1,0:T(8,128)} %get-tuple-element.159), calls=%async_computation.5 | async-start | bytes 1048576 | tf_op jit(solution)/shard_map/all_to_all | solution.py:755
  40.8 0.0 copy-done.2
  40.8 0.0 copy-done.3
  40.8 0.0 copy-done.5
  40.9 0.0 copy-done.27
  40.9 0.0 copy-done.30
  40.9 0.0 copy-done.15
  40.9 0.0 copy-done.18
  40.9 0.6 hits.1
  41.5 12.8 %all-to-all-done.5.recv_ref = f32[128,8,128]{2,1,0:T(8,128)S(1)} async-done(((f32[128,8,128]{2,1,0:T(8,128)}), f32[128,8,128]{2,1,0:T(8,128)S(1)}, u32[]{:S(2)}, u32[]{:S(2)}) %all-to-all-start.5) | async-done | bytes 524320 | tf_op jit(solution)/shard_map/all_to_all | solution.py:755
  54.3 0.0 copy-done.4
  54.3 2.6 %substep_two.1 = (f32[40,16,128]{2,1,0:T(8,128)S(1)}, f32[128,8,128]{2,1,0:T(8,128)}, f32[8,128]{1,0:T(8,128)S(1)}, f32[40,128]{1,0:T(8,128)S(1)}, f32[40,128]{1,0:T(8,128)S(1)}) custom-call(f32[128,8,128]{2,1,0:T(8,128)S(1)} %all-to-all-done.5.recv_ref, f32[40,16,128]{2,1,0:T(8,128)S(1)} %get-tuple-element.160.x_ref, ...), custom_call_target="tpu_custom_call" | custom-call | flops 1000000 | bytes 4000000 | tf_op jit(solution)/shard_map/substep_two/pallas_call | solution.py:724
  56.9 7.7 %all-to-all-start.6 = ((f32[128,8,128]{2,1,0:T(8,128)}), f32[128,8,128]{2,1,0:T(8,128)S(1)}, u32[]{:S(2)}, u32[]{:S(2)}) async-start(f32[128,8,128]{2,1,0:T(8,128)} %get-tuple-element.165), calls=%async_computation.6 | async-start | bytes 1048576 | tf_op jit(solution)/shard_map/all_to_all | solution.py:755
  64.5 3.5 %collective-permute-start.22 = (f32[40,128]{1,0:T(8,128)S(1)}, f32[40,128]{1,0:T(8,128)S(1)}, u32[]{:S(2)}, u32[]{:S(2)}) collective-permute-start(f32[40,128]{1,0:T(8,128)S(1)} %get-tuple-element.167), channel_id=1, source_target_pairs={{0,32},{32,64},{1,33},{33,65},{2,34},{34,66},{3,35},{35,67},{4,36}... | collective-permute-start | bytes 61448 | tf_op jit(solution)/shard_map/ppermute | solution.py:759
  68.1 1.9 %collective-permute-start.23 = (f32[40,128]{1,0:T(8,128)S(1)}, f32[40,128]{1,0:T(8,128)S(1)}, u32[]{:S(2)}, u32[]{:S(2)}) collective-permute-start(f32[40,128]{1,0:T(8,128)S(1)} %get-tuple-element.168), channel_id=1, source_target_pairs={{32,0},{64,32},{33,1},{65,33},{34,2},{66,34},{35,3},{67,35},{36,4}... | collective-permute-start | bytes 61448 | tf_op jit(solution)/shard_map/ppermute | solution.py:760
  70.0 0.6 slice.381
  71.3 0.8 %parents.1.fresh_ref = f32[40,16,128]{2,1,0:T(8,128)S(1)} custom-call(f32[40,16,128]{2,1,0:T(8,128)S(1)} %get-tuple-element.166.x_ref, f32[16,128]{1,0:T(8,128)S(1)} %copy-done.5, f32[16]{0:T(128)S(1)} %copy-done.27, f32[10]{0:T(128)S(1)} %copy-done.30), custom_call_target="tpu_custom_call" | custom-call | flops 1000000 | bytes 4000000 | tf_op jit(solution)/shard_map/parents/pallas_call | solution.py:724
  72.1 0.0 collective-permute-done.22.above_ref
  72.1 1.8 %collective-permute-done.23.below_ref = f32[40,128]{1,0:T(8,128)S(1)} collective-permute-done((f32[40,128]{1,0:T(8,128)S(1)}, f32[40,128]{1,0:T(8,128)S(1)}, u32[]{:S(2)}, u32[]{:S(2)}) %collective-permute-start.23) | collective-permute-done | bytes 20512 | tf_op jit(solution)/shard_map/ppermute | solution.py:760
  73.9 4.1 %all-to-all-done.6.recv_ref = f32[128,8,128]{2,1,0:T(8,128)S(1)} async-done(((f32[128,8,128]{2,1,0:T(8,128)}), f32[128,8,128]{2,1,0:T(8,128)S(1)}, u32[]{:S(2)}, u32[]{:S(2)}) %all-to-all-start.6) | async-done | bytes 524320 | tf_op jit(solution)/shard_map/all_to_all | solution.py:755
  78.0 1.7 %finish.1 = f32[40,16,128]{2,1,0:T(8,128)S(1)} custom-call(f32[128,8,128]{2,1,0:T(8,128)S(1)} %all-to-all-done.6.recv_ref, f32[40,16,128]{2,1,0:T(8,128)S(1)} %get-tuple-element.166.x_ref, f32[40,16,128]{2,1,0:T(8,128)S(1)} %parents.1.fresh_ref, f32[16,128]{1,0:T(8,128)S(1)} %copy-done.5, f32[40,128]{1,0:T(8,128)S(1)} %collective-permute-done.22.above_ref, ...), custom_call_target="tpu_custom_call" | custom-call | flops 1000000 | bytes 4000000 | tf_op jit(solution)/shard_map/finish/pallas_call | solution.py:724
  79.7 0.0 copy-done
  79.8 0.2 conditional.1
  80.0 0.0 copy-start.14
  80.0 0.7 copy-done.14
Async XLA Ops:
  0.0 40.8 %copy-start.2 = (s32[32,3,288]{2,0,1:T(8,128)S(1)}, s32[32,3,288]{2,0,1:T(8,128)}, u32[]{:S(2)}) copy-start(s32[32,3,288]{2,0,1:T(8,128)} %param.33) | copy-start | bytes 331780
  0.0 40.8 %copy-start.3 = (s32[32,3,288]{2,0,1:T(8,128)S(1)}, s32[32,3,288]{2,0,1:T(8,128)}, u32[]{:S(2)}) copy-start(s32[32,3,288]{2,0,1:T(8,128)} %param.34) | copy-start | bytes 331780
  0.0 40.8 %copy-start.5 = (f32[16,128]{1,0:T(8,128)S(1)}, f32[16,128]{1,0:T(8,128)}, u32[]{:S(2)}) copy-start(f32[16,128]{1,0:T(8,128)} %diff_ref.11) | copy-start | bytes 24580
  0.0 40.8 %copy-start.27 = (f32[16]{0:T(128)S(1)}, f32[16]{0:T(128)}, u32[]{:S(2)}) copy-start(f32[16]{0:T(128)} %cor_ref.5) | copy-start | bytes 196
  0.0 40.8 %copy-start.30 = (f32[10]{0:T(128)S(1)}, f32[10]{0:T(128)}, u32[]{:S(2)}) copy-start(f32[10]{0:T(128)} %mix_ref.5) | copy-start | bytes 124
  0.0 40.8 %copy-start.15 = (s32[32,128]{1,0:T(8,128)S(1)}, s32[32,128]{1,0:T(8,128)}, u32[]{:S(2)}) copy-start(s32[32,128]{1,0:T(8,128)} %fb_owner_ref.3) | copy-start | bytes 49156
  0.0 40.8 %copy-start.18 = (s32[32,128]{1,0:T(8,128)S(1)}, s32[32,128]{1,0:T(8,128)}, u32[]{:S(2)}) copy-start(s32[32,128]{1,0:T(8,128)} %fb_cell_ref.3) | copy-start | bytes 49156
  0.1 54.2 %copy-start.4 = (f32[32,3,288]{2,0,1:T(8,128)S(1)}, f32[32,3,288]{2,0,1:T(8,128)}, u32[]{:S(2)}) copy-start(f32[32,3,288]{2,0,1:T(8,128)} %param.35) | copy-start | bytes 331780
  4.2 75.6 %copy-start = (f32[40,16,128]{2,1,0:T(8,128)S(1)}, f32[40,16,128]{2,1,0:T(8,128)}, u32[]{:S(2)}) copy-start(f32[40,16,128]{2,1,0:T(8,128)} %x_ref.5) | copy-start | bytes 983044
  4.2 25.0 %all-to-all-start.4 = ((f32[128,8,128]{2,1,0:T(8,128)}), f32[128,8,128]{2,1,0:T(8,128)S(1)}, u32[]{:S(2)}, u32[]{:S(2)}) async-start(f32[128,8,128]{2,1,0:T(8,128)} %get-tuple-element.151), calls=%async_computation.4 | async-start | bytes 1048576 | tf_op jit(solution)/shard_map/all_to_all | solution.py:755
  15.7 7.9 %collective-permute-start.20 = (f32[40,128]{1,0:T(8,128)S(1)}, f32[40,128]{1,0:T(8,128)S(1)}, u32[]{:S(2)}, u32[]{:S(2)}) collective-permute-start(f32[40,128]{1,0:T(8,128)S(1)} %get-tuple-element.154), channel_id=1, source_target_pairs={{0,32},{32,64},{1,33},{33,65},{2,34},{34,66},{3,35},{35,67},{4,36}... | collective-permute-start | bytes 61448 | tf_op jit(solution)/shard_map/ppermute | solution.py:759
  19.2 5.8 %collective-permute-start.21 = (f32[40,128]{1,0:T(8,128)S(1)}, f32[40,128]{1,0:T(8,128)S(1)}, u32[]{:S(2)}, u32[]{:S(2)}) collective-permute-start(f32[40,128]{1,0:T(8,128)S(1)} %get-tuple-element.155), channel_id=1, source_target_pairs={{32,0},{64,32},{33,1},{65,33},{34,2},{66,34},{35,3},{67,35},{36,4}... | collective-permute-start | bytes 61448 | tf_op jit(solution)/shard_map/ppermute | solution.py:760
  32.7 21.6 %all-to-all-start.5 = ((f32[128,8,128]{2,1,0:T(8,128)}), f32[128,8,128]{2,1,0:T(8,128)S(1)}, u32[]{:S(2)}, u32[]{:S(2)}) async-start(f32[128,8,128]{2,1,0:T(8,128)} %get-tuple-element.159), calls=%async_computation.5 | async-start | bytes 1048576 | tf_op jit(solution)/shard_map/all_to_all | solution.py:755
  56.9 21.1 %all-to-all-start.6 = ((f32[128,8,128]{2,1,0:T(8,128)}), f32[128,8,128]{2,1,0:T(8,128)S(1)}, u32[]{:S(2)}, u32[]{:S(2)}) async-start(f32[128,8,128]{2,1,0:T(8,128)} %get-tuple-element.165), calls=%async_computation.6 | async-start | bytes 1048576 | tf_op jit(solution)/shard_map/all_to_all | solution.py:755
  64.5 7.5 %collective-permute-start.22 = (f32[40,128]{1,0:T(8,128)S(1)}, f32[40,128]{1,0:T(8,128)S(1)}, u32[]{:S(2)}, u32[]{:S(2)}) collective-permute-start(f32[40,128]{1,0:T(8,128)S(1)} %get-tuple-element.167), channel_id=1, source_target_pairs={{0,32},{32,64},{1,33},{33,65},{2,34},{34,66},{3,35},{35,67},{4,36}... | collective-permute-start | bytes 61448 | tf_op jit(solution)/shard_map/ppermute | solution.py:759
  68.1 5.8 %collective-permute-start.23 = (f32[40,128]{1,0:T(8,128)S(1)}, f32[40,128]{1,0:T(8,128)S(1)}, u32[]{:S(2)}, u32[]{:S(2)}) collective-permute-start(f32[40,128]{1,0:T(8,128)S(1)} %get-tuple-element.168), channel_id=1, source_target_pairs={{32,0},{64,32},{33,1},{65,33},{34,2},{66,34},{35,3},{67,35},{36,4}... | collective-permute-start | bytes 61448 | tf_op jit(solution)/shard_map/ppermute | solution.py:760
  80.0 0.7 copy-start.14

commit v3 on v2

--- a/solution.py
+++ b/solution.py
@@ -20,11 +20,14 @@
 HITS = 8
 EDGE = 40
 FG = 5
-T1_ROW = 128
-TAB_ROWS = 144
 PGROUPS = 20
 GROUPS = 22
-VMEM_LIMIT = 48 * 1024 * 1024
+ENTRIES = 128
+PLANES = 2
+MEANS = 8 * PLANES
+SENT = PARENTS * 8
+TAKEN = GX * 8
+VMEM_LIMIT = 24 * 1024 * 1024
 
 
 def padded(cells, sides, width):
@@ -163,17 +166,22 @@
     return lax.broadcasted_iota(jnp.int32, shape, dim)
 
 
-def chunks(count, step, body):
-    def run(c, carry):
-        for s in range(step):
-            body(c * step + s)
-        return carry
-
-    lax.fori_loop(0, count // step, run, 0)
+def rows_of(device):
+    return pl.ds(pl.multiple_of(8 * device, 8), 8)
 
 
 def take(tile, index):
     return jnp.take_along_axis(tile, index, axis=1, mode="promise_in_bounds")
+
+
+def halves(values):
+    high = values.astype(jnp.bfloat16)
+    return high, (values - high.astype(F32)).astype(jnp.bfloat16)
+
+
+def product(left, right, contract=(1, 0)):
+    dims = (((contract[0],), (contract[1],)), ((), ()))
+    return lax.dot_general(left, right, dims, preferred_element_type=F32)
 
 
 def ranks(masks):
@@ -182,8 +190,8 @@
     stacked = stacked.astype(jnp.bfloat16)
     before = jnp.where(iota((128, 128), 0) < iota((128, 128), 1), 1.0, 0.0).astype(jnp.bfloat16)
     ones = jnp.ones((128, 128), jnp.bfloat16)
-    within = jnp.dot(stacked, before, preferred_element_type=F32)
-    totals = jnp.dot(stacked, ones, preferred_element_type=F32)
+    within = product(stacked, before)
+    totals = product(stacked, ones)
     carry = jnp.zeros((rows, 128), F32)
     found = []
     for t in range(len(masks)):
@@ -236,12 +244,12 @@
                 shift = (SLOTS * (k - (q - 5 * g))) % 128
                 moved = cells[k] if shift == 0 else pltpu.roll(cells[k], shift, 1)
                 block = jnp.where(group_of == k, moved, block)
-            send_ref[PARENTS + q] = block
-
-
-def edge_block(x_ref, col, base):
+            send_ref[8 * (PARENTS + q) : 8 * (PARENTS + q) + 8, :] = block
+
+
+def edge_block(x_ref, col):
     lane = iota((8, 128), 1)
-    block = base
+    block = jnp.zeros((8, 128), F32)
     for h in range(2):
         for f in range(LANES):
             edge = x_ref[f, 8 * h : 8 * h + 8, col : col + 1]
@@ -249,21 +257,21 @@
     return block
 
 
-def send_parent_edges(x_ref, send_ref, grp, gx, base):
-    first = edge_block(x_ref, 0, base)
-    last = edge_block(x_ref, COLS - 1, base)
+def send_parent_edges(x_ref, send_ref, grp, gx):
+    first = edge_block(x_ref, 0)
+    last = edge_block(x_ref, COLS - 1)
     right = lax.rem(gx + 1, GX)
     left = lax.rem(gx + GX - 1, GX)
-    send_ref[grp * GX + right] = last
-    send_ref[grp * GX + left] = first
+    send_ref[rows_of(grp * GX + right), :] = last
+    send_ref[rows_of(grp * GX + left), :] = first
 
     @pl.when(grp > 0)
     def _():
-        send_ref[(grp - 1) * GX + right] = last
+        send_ref[rows_of((grp - 1) * GX + right), :] = last
 
     @pl.when(grp < 2)
     def _():
-        send_ref[(grp + 1) * GX + left] = first
+        send_ref[rows_of((grp + 1) * GX + left), :] = first
 
 
 def unpack_edge(block):
@@ -301,10 +309,10 @@
     left = lax.rem(gx + GX - 1, GX)
     lane = iota((ROWS, COLS), 1)
     row = iota((ROWS, COLS), 0)
-    from_left = unpack_edge(recv_ref[grp * GX + left])
-    from_right = unpack_edge(recv_ref[grp * GX + right])
-    top_right = unpack_edge(recv_ref[jnp.maximum(grp - 1, 0) * GX + right])[ROWS - 1 : ROWS]
-    low_left = unpack_edge(recv_ref[jnp.minimum(grp + 1, 3) * GX + left])[0:1]
+    from_left = unpack_edge(recv_ref[rows_of(grp * GX + left), :])
+    from_right = unpack_edge(recv_ref[rows_of(grp * GX + right), :])
+    top_right = unpack_edge(recv_ref[rows_of(jnp.maximum(grp - 1, 0) * GX + right), :])[ROWS - 1 : ROWS]
+    low_left = unpack_edge(recv_ref[rows_of(jnp.minimum(grp + 1, 3) * GX + left), :])[0:1]
     top_right = jnp.where(grp == 0, from_right[0:1], top_right)
     low_left = jnp.where(grp == 2, from_left[ROWS - 1 : ROWS], low_left)
     top_right = jnp.where(nest, 0.0, top_right)
@@ -344,59 +352,88 @@
     out_ref[:, ROWS - 1, :] = out_ref[:, ROWS - 1, :] + diff_ref[ROWS - 1 : ROWS, :] * below
 
 
-def regroup(recv_ref, base, groups, per, width, group_s, first):
-    lane = iota((8, 128), 1)
-    member_of = lane // width
+def chunks(count, step, body):
+    def run(c, carry):
+        for s in range(step):
+            body(c * step + s)
+        return carry
+
+    lax.fori_loop(0, count // step, run, 0)
+
+
+def regroup(recv_ref, group_s):
+    member_of = iota((8, 128), 1) // SLOTS
 
     def body(g):
         tiles = [jnp.zeros((8, 128), F32) for _ in range(FG)]
-        for i in range(per):
-            block = recv_ref[jnp.minimum(base + g * per + i, DEVICES - 1)]
+        for i in range(5):
+            block = recv_ref[rows_of(g * 5 + i), :]
             for k in range(FG):
-                shift = (width * (i - k)) % 128
+                shift = (SLOTS * (i - k)) % 128
                 moved = block if shift == 0 else pltpu.roll(block, shift, 1)
                 tiles[k] = jnp.where(member_of == i, moved, tiles[k])
         for k in range(FG):
-            group_s[first + g, 8 * k : 8 * k + 8, :] = tiles[k]
-
-    chunks(groups, 2 if groups % 2 == 0 else 1, body)
-
-
-def interpolate(tabs_ref, first_row, weight_s, group_s, groups, cycle_s):
-    cycle_s[...] = jnp.zeros((3, LANES, 128), F32)
-
-    def body(t):
-        code = jnp.broadcast_to(tabs_ref[pl.ds(first_row + t, 1), :], (8, 128))
+            group_s[g, 8 * k : 8 * k + 8, :] = tiles[k]
+
+    chunks(PGROUPS, 2, body)
+
+
+def regroup_hits(recv_ref, group_s):
+    for h in range(2):
+        first = SENT + 128 * h
+        group_s[PGROUPS + h] = recv_ref[first : first + 128, :].T[0:LANES]
+
+
+def interpolate(codes_ref, weight_s, group_s, groups, cycle_s, column_s):
+    def cells_of(t):
+        code = jnp.broadcast_to(codes_ref[pl.ds(t, 1), :], (8, 128))
         index = jnp.bitwise_and(code, 127)
         group = jnp.right_shift(code, 7)
+        weight = weight_s[pl.ds(t, 1), :]
         cells = [jnp.zeros((8, 128), F32) for _ in range(FG)]
         for g in range(groups):
             here = group == g
             for k in range(FG):
                 cells[k] = jnp.where(here, take(group_s[g, 8 * k : 8 * k + 8, :], index), cells[k])
-        weight = weight_s[pl.ds(t, 1), :]
-        span = lax.rem(t, 3)
-        for k in range(FG):
-            cycle_s[span, 8 * k : 8 * k + 8, :] += weight * cells[k]
-
-    chunks(TILES, 1, body)
+        return [weight * c for c in cells]
+
+    cycle_s[...] = jnp.zeros((2, LANES, 128), F32)
+
+    def body(t):
+        span = jnp.bitwise_and(t, 1)
+        for k, cells in enumerate(cells_of(t)):
+            cycle_s[span, 8 * k : 8 * k + 8, :] += cells
+
+    chunks(6, 1, body)
+    for k, cells in enumerate(cells_of(6)):
+        total = cells + pltpu.roll(cells, 96, 1) + pltpu.roll(cells, 64, 1)
+        column_s[8 * k : 8 * k + 8, :] = total
 
 
 def load_weights(weight_ref, weight_s, gx):
-    weight_s[...] = jnp.zeros((16, 128), F32)
+    weight_s[...] = jnp.zeros((8, 128), F32)
     for k in range(3):
         own = weight_ref[k, pl.ds(gx, 1), :]
-        weight_s[3 * k : 3 * k + 1, :] = own[:, 0:128]
-        weight_s[3 * k + 1 : 3 * k + 2, :] = own[:, 128:256]
-        weight_s[3 * k + 2 : 3 * k + 3, 0:32] = own[:, 256:288]
-
-
-def prescribe(out_ref, cycle_s, gx):
+        weight_s[2 * k : 2 * k + 1, :] = own[:, 0:128]
+        weight_s[2 * k + 1 : 2 * k + 2, :] = own[:, 128:256]
+        weight_s[6:7, 32 * k : 32 * k + 32] = own[:, 256:288]
+
+
+def pack_tiles(rows):
+    lane = iota((1, 128), 1)
+    last = rows[2]
+    for k in (1, 2):
+        moved = pltpu.roll(jnp.broadcast_to(rows[3 * k + 2], (8, 128)), 32 * k, 1)[0:1]
+        last = jnp.where(lane >= 32 * k, moved, last)
+    return [rows[3 * k + span] for k in range(3) for span in range(2)] + [last]
+
+
+def prescribe(out_ref, cycle_s, column_s, gx):
     lane = iota((ROWS, COLS), 1)
 
     @pl.when(jnp.logical_or(gx == 0, gx == GX - 1))
     def _():
-        turned = jnp.concatenate([cycle_s[2], jnp.zeros((88, 128), F32)], axis=0).T
+        turned = jnp.concatenate([column_s[...], jnp.zeros((88, 128), F32)], axis=0).T
         column = jnp.where(gx == 0, turned[0:ROWS, :], turned[ROWS : 2 * ROWS, :])
         at = jnp.where(gx == 0, 0, COLS - 1)
         for f in range(LANES):
@@ -406,87 +443,87 @@
     out_ref[:, ROWS - 1, :] = cycle_s[1]
 
 
-def coarsen(out_ref):
-    coarse = jnp.zeros((LANES, 128), F32)
+def send_coarse(out_ref, pick_ref, send_ref, base, count):
+    mean = jnp.where(iota((32, 128), 1) // 4 == iota((32, 128), 0), 1.0 / 16.0, 0.0)
+    parts = []
     for i in range(4):
         total = (out_ref[:, 4 * i, :] + out_ref[:, 4 * i + 1, :]) + (
             out_ref[:, 4 * i + 2, :] + out_ref[:, 4 * i + 3, :]
         )
-        mean = jnp.where(iota((128, 128), 1) == 32 * i + iota((128, 128), 0) // 4, 1.0 / 16.0, 0.0)
-        coarse = coarse + jnp.dot(
-            total, mean, precision=lax.Precision.HIGHEST, preferred_element_type=F32
-        )
-    return coarse
-
-
-def send_coarse(coarse, tabs_ref, send_ref, base):
-    lane = iota((8, 128), 1)
-    group_of = lane // SLOTS
-
-    def body(o):
-        index = jnp.broadcast_to(tabs_ref[pl.ds(o, 1), :], (8, 128))
-        block = base
-        for k in range(FG):
-            block = jnp.where(group_of == k, take(coarse[8 * k : 8 * k + 8], index), block)
-        send_ref[o] = block
-
-    chunks(PARENTS, 8, body)
-
-
-def send_hits(coarse, tabs_ref, send_ref, base):
-    group_of = iota((8, 128), 1) // HITS
-
-    def body(q):
-        index = jnp.broadcast_to(tabs_ref[pl.ds(PARENTS + q, 1), :], (8, 128))
-        block = base
-        for k in range(FG):
-            block = jnp.where(group_of == k, take(coarse[8 * k : 8 * k + 8], index), block)
-        send_ref[PARENTS + q] = block
-
-    chunks(GX, 8, body)
-
-
-def feed_back(src_ref, out_ref, recv_ref, map_ref, group_s):
-    regroup(recv_ref, PARENTS, 7, 5, SLOTS, group_s, 0)
+        wide = jnp.concatenate([total, total, jnp.zeros((48, 128), F32)], axis=0)
+        parts.append(
+            lax.dot_general(
+                mean,
+                wide,
+                (((1,), (1,)), ((), ())),
+                precision=lax.Precision.HIGHEST,
+                preferred_element_type=F32,
+            )
+        )
+    coarse = jnp.concatenate(parts, axis=0)
+    plane_of = iota((128, 128), 1) // LANES
+    placed = [jnp.where(plane_of == plane, coarse, 0.0) for plane in range(PLANES)]
+    high, low = halves(jnp.concatenate(placed, axis=0))
+    both = product(pick_ref[0:count, :], jnp.concatenate([high, low], axis=1))
+    sent = both[:, 0:128] + both[:, 128:256]
+    if base is not None:
+        sent = sent + base[0:1, :]
+    send_ref[0:count, :] = sent
+
+
+def feed_back(src_ref, out_ref, recv_ref, pick_ref, map_ref):
+    high, low = halves(recv_ref[SENT : SENT + TAKEN, :])
+    both = product(pick_ref[...], jnp.concatenate([high, low], axis=1))
+    total = both[:, 0:128] + both[:, 128:256]
+    entries = total[0:ENTRIES]
+    for plane in range(1, PLANES):
+        part = total[plane * ENTRIES : (plane + 1) * ENTRIES]
+        entries = entries + pltpu.roll(part, 128 - LANES * plane, 1)
+    turned = entries.T
     for r in range(ROWS):
         code = jnp.broadcast_to(map_ref[r : r + 1, :], (8, 128))
+        fed = code >= 0
         index = jnp.bitwise_and(code, 127)
-        group = jnp.right_shift(code, 7)
-        cells = [src_ref[8 * k : 8 * k + 8, r, :] for k in range(FG)]
-        for g in range(7):
-            here = group == g
-            for k in range(FG):
-                cells[k] = jnp.where(here, take(group_s[g, 8 * k : 8 * k + 8, :], index), cells[k])
         for k in range(FG):
-            out_ref[8 * k : 8 * k + 8, r, :] = cells[k]
-
-
-def feedback_map(owner_ref, cell_ref, map_ref, me):
-    owner = owner_ref[...]
+            span = slice(8 * k, 8 * k + 8)
+            out_ref[span, r, :] = jnp.where(fed, take(turned[span], index), src_ref[span, r, :])
+
+
+def feedback_routes(owner_ref, cell_ref, pick_ref, map_ref, me):
     cell = cell_ref[...]
-    own = owner == me
-    found, _ = ranks([own])
-    slot = jnp.minimum(found[0], float(SLOTS - 1))
-    row = jnp.where(own, jnp.right_shift(cell, 7), -1)
+    own = owner_ref[...] == me
+    found, total = ranks([own])
+    slot = jnp.minimum(found[0], float(MEANS - 1))
+    below = jnp.where(iota((GX, GX), 1) < iota((GX, GX), 0), 1.0, 0.0).astype(jnp.bfloat16)
+    entry = found[0] + product(below, total.astype(jnp.bfloat16))
+    entry = jnp.where(own, entry, -1.0)
+    plane = jnp.floor(slot * 0.125)
+    place = iota((GX, 128), 0).astype(F32) * 8.0 + (slot - 8.0 * plane)
+    row = jnp.right_shift(cell, 7)
     col = jnp.bitwise_and(cell, 127)
-    planes = jnp.zeros((2 * ROWS, 128), F32)
+    cells = jnp.zeros((ROWS, 128), F32)
+    codes = jnp.zeros((ENTRIES, 128), F32)
     for q in range(GX):
-        here = iota((ROWS, 128), 0) == row[q : q + 1, :]
-        codes = jnp.concatenate(
-            [jnp.where(here, float(q + 1), 0.0), jnp.where(here, slot[q : q + 1, :], 0.0)], axis=0
-        )
-        hot = jnp.where(iota((128, 128), 0) == col[q : q + 1, :], 1.0, 0.0)
-        planes = planes + lax.dot_general(
-            codes.astype(jnp.bfloat16),
-            hot.astype(jnp.bfloat16),
-            (((1,), (1,)), ((), ())),
-            preferred_element_type=F32,
-        )
-    block = planes[0:ROWS].astype(jnp.int32) - 1
-    slots = planes[ROWS : 2 * ROWS].astype(jnp.int32)
-    group = jnp.right_shift(block * 205, 10)
-    code = group * 128 + (block - 5 * group) * SLOTS + slots
-    map_ref[...] = jnp.where(block < 0, -1, code)
+        line = slice(q, q + 1)
+        here = jnp.where(iota((ROWS, 128), 0) == row[line], entry[line] + 1.0, 0.0)
+        hot = jnp.where(iota((128, 128), 0) == col[line], 1.0, 0.0)
+        cells = cells + product(here.astype(jnp.bfloat16), hot.astype(jnp.bfloat16), (1, 1))
+        hot = jnp.where(iota((ENTRIES, 128), 0).astype(F32) == entry[line], 1.0, 0.0)
+        both = jnp.where(
+            iota((128, 128), 0) == 0,
+            place[line],
+            jnp.where(iota((128, 128), 0) == 1, plane[line] + 1.0, 0.0),
+        )
+        codes = codes + product(hot.astype(jnp.bfloat16), both.astype(jnp.bfloat16), (1, 1))
+    map_ref[...] = cells.astype(jnp.int32) - 1
+    at = codes[:, 0:1]
+    level = codes[:, 1:2] - 1.0
+    lane = iota((ENTRIES, TAKEN), 1).astype(F32)
+    for p in range(PLANES):
+        hot = jnp.where(jnp.where(level == float(p), at, -1.0) == lane, 1.0, 0.0)
+        pick_ref[p * ENTRIES : (p + 1) * ENTRIES, :] = hot.astype(jnp.bfloat16)
+    count = jnp.sum(jnp.where(own, 1.0, 0.0), axis=0, keepdims=True)
+    return jnp.where(jnp.sum(count, axis=1, keepdims=True) > float(ENTRIES), 1.0, 0.0)
 
 
 def load_terms(owner_ref, cell_ref, gid_s):
@@ -510,7 +547,6 @@
 ):
     grp = lax.axis_index("grp")
     gx = lax.axis_index("gx")
-    blank = jnp.zeros((8, 128), F32)
     last_row_ref[...] = x_ref[:, ROWS - 1, :]
     first_row_ref[...] = x_ref[:, 0, :]
 
@@ -526,18 +562,20 @@
         for r in range(ROWS):
             rows_s[r] = x_ref[:, r, :]
         send_cells(rows_s, table_ref, send_ref, None)
-        send_parent_edges(x_ref, send_ref, grp, gx, blank)
+        send_parent_edges(x_ref, send_ref, grp, gx)
 
     @pl.when(grp == 3)
     def _():
-        send_ref[PARENTS + lax.rem(gx + 1, GX)] = edge_block(x_ref, COLS - 1, blank)
-        send_ref[PARENTS + lax.rem(gx + GX - 1, GX)] = edge_block(x_ref, 0, blank)
+        right = PARENTS + lax.rem(gx + 1, GX)
+        left = PARENTS + lax.rem(gx + GX - 1, GX)
+        send_ref[rows_of(right), :] = edge_block(x_ref, COLS - 1)
+        send_ref[rows_of(left), :] = edge_block(x_ref, 0)
 
 
 def tables_kernel(
     x_ref, diff_ref, cor_ref, mix_ref, owner_ref, cell_ref, fb_owner_ref, fb_cell_ref,
-    fb_owner_sm, fb_cell_sm, flag_in_ref, fresh_ref, tabs_ref, flag_ref, map_ref,
-    gid_s, mark_s, value_s,
+    flag_in_ref, fresh_ref, codes_ref, pick_ref, flag_ref, map_ref, entry_ref,
+    gid_s, mark_s, value_s, found_s, seek_s,
 ):
     grp = lax.axis_index("grp")
     gx = lax.axis_index("gx")
@@ -545,59 +583,92 @@
 
     @pl.when(grp < 3)
     def _():
-        flag_ref[...] = flag_in_ref[...]
-        feedback_map(fb_owner_ref, fb_cell_ref, map_ref, grp * GX + gx)
+        over = feedback_routes(fb_owner_ref, fb_cell_ref, entry_ref, map_ref, grp * GX + gx)
+        lane = iota((8, 128), 1)
+        flag_ref[...] = jnp.where(lane == 127, jnp.maximum(flag_in_ref[...], over), 0.0)
 
     @pl.when(grp == 3)
     def _():
         load_terms(owner_ref, cell_ref, gid_s)
-        own = fb_owner_ref[pl.ds(gx, 1), :]
-        hot = iota((PARENTS, 128), 0) == own
+        own_owner = fb_owner_ref[pl.ds(gx, 1), :]
+        own_cell = fb_cell_ref[pl.ds(gx, 1), :]
+        hot = iota((128, 128), 0) == own_owner
         found, total = ranks([hot])
-        over = jnp.max(jnp.where(total > float(SLOTS), 1.0, 0.0), axis=0, keepdims=True)
-        rank = jnp.sum(jnp.where(hot, found[0], 0.0), axis=0, keepdims=True)
-        slot_of = lax.rem(iota((128, 128), 0), SLOTS).astype(F32)
-        chosen = jnp.where(slot_of == rank, iota((128, 128), 1).astype(F32), 0.0)
-        table = lax.dot_general(
-            jnp.where(hot, 1.0, 0.0).astype(jnp.bfloat16),
-            chosen.astype(jnp.bfloat16),
-            (((1,), (1,)), ((), ())),
-            preferred_element_type=F32,
-        )
-        tabs_ref[0:PARENTS, :] = table.astype(jnp.int32)
+        over = jnp.max(jnp.where(total > float(MEANS), 1.0, 0.0), axis=0, keepdims=True)
+        rank = jnp.sum(jnp.where(hot, found[0], 0.0), axis=0, keepdims=True).astype(jnp.int32)
+        level = jnp.right_shift(rank, 3)
+        place = own_owner * 8 + jnp.bitwise_and(rank, 7)
+        for p in range(PLANES):
+            wanted = jnp.where(level == p, place, -1)
+            for part in range(6):
+                line = iota((128, 128), 0) + 128 * part
+                pick_ref[128 * part : 128 * part + 128, 128 * p : 128 * p + 128] = jnp.where(
+                    line == wanted, 1.0, 0.0
+                ).astype(jnp.bfloat16)
 
         owners = [jnp.right_shift(gid_s[t, pl.ds(gx, 1), :], 11) for t in range(TILES)]
         hots = [iota((PARENTS, 128), 0) == o for o in owners]
         found, _ = ranks(hots)
+        codes = []
         for t in range(TILES):
             slot = jnp.sum(jnp.where(hots[t], found[t], 0.0), axis=0, keepdims=True)
             slot = jnp.minimum(slot.astype(jnp.int32), SLOTS - 1)
             group = jnp.right_shift(owners[t] * 205, 10)
-            code = group * 128 + (owners[t] - 5 * group) * SLOTS + slot
-            tabs_ref[T1_ROW + t : T1_ROW + t + 1, :] = code
-
-        def seek(c, found_at):
-            for s in range(4):
-                b = 4 * c + s
-                wanted = fb_owner_sm[gx, b] * 2048 + fb_cell_sm[gx, b]
-                found_at = [jnp.where(gid_s[t] == wanted, b, found_at[t]) for t in range(TILES)]
-            return found_at
-
-        none = [jnp.full((GX, 128), -1, jnp.int32) for _ in range(TILES)]
-        found_at = lax.fori_loop(0, 32, seek, none)
+            codes.append(group * 128 + (owners[t] - 5 * group) * SLOTS + slot)
+        for t, code in enumerate(pack_tiles(codes)):
+            codes_ref[t : t + 1, :] = code
+
+        hot = jnp.where(hot, 1.0, 0.0).astype(jnp.bfloat16)
+        chosen = iota((32, 128), 0) == rank
+
+        def by_owner(values):
+            picked = jnp.where(chosen, values.astype(F32), 0.0).astype(jnp.bfloat16)
+            return product(picked, hot, (1, 1)).astype(jnp.int32)
+
+        number = by_owner(iota((1, 128), 1) + 1)
+        cells = by_owner(jnp.right_shift(own_cell, 4)) * 16 + by_owner(jnp.bitwise_and(own_cell, 15))
+        seek_s[...] = jnp.where(number > 0, cells * 256 + number - 1, -1)
+        found_s[...] = jnp.full((TILES, GX, 128), -1, jnp.int32)
+
+        def seek(j, carry):
+            line = jnp.broadcast_to(seek_s[pl.ds(j, 1), :], (8, 128))
+            for t in range(TILES):
+                for part in range(GX // 8):
+                    span = slice(8 * part, 8 * part + 8)
+                    gid = gid_s[t, span, :]
+                    entry = take(line, jnp.bitwise_and(jnp.right_shift(gid, 11), 127))
+                    same = jnp.right_shift(entry, 8) == jnp.bitwise_and(gid, 2047)
+                    found_s[t, span, :] = jnp.where(
+                        same, jnp.bitwise_and(entry, 255), found_s[t, span, :]
+                    )
+            return carry
+
+        most = jnp.minimum(jnp.max(total).astype(jnp.int32), 32)
+        lax.fori_loop(0, most, seek, 0)
+        found_at = [found_s[t] for t in range(TILES)]
         table, total = slot_table(
             [f >= 0 for f in found_at], [f.astype(F32) for f in found_at], HITS, mark_s, value_s
         )
-        tabs_ref[PARENTS : PARENTS + GX, :] = table.astype(jnp.int32)
         over = jnp.maximum(
             over, jnp.max(jnp.where(total > float(HITS), 1.0, 0.0), axis=0, keepdims=True)
         )
+        turned = jnp.concatenate([table, jnp.zeros((96, 128), F32)], axis=0).T
+        lane = iota((8, 128), 1).astype(F32)
+        blank = jnp.zeros((16, 128 * (PLANES - 1)), jnp.bfloat16)
+        for pair in range(GX // 2):
+            line = slice(SENT + 16 * pair, SENT + 16 * pair + 16)
+            hits = [
+                jnp.where(turned[0:HITS, q : q + 1] == lane, 1.0, 0.0)
+                for q in (2 * pair, 2 * pair + 1)
+            ]
+            pick_ref[line, 0:128] = jnp.concatenate(hits, axis=0).astype(jnp.bfloat16)
+            pick_ref[line, 128 : 128 * PLANES] = blank
         flag_ref[...] = flag_block(over)
 
 
 def second_kernel(
-    recv_ref, x_ref, fresh_ref, diff_ref, above_ref, below_ref, weight_ref, table_ref, tabs_ref,
-    flag_ref, out_ref, send_ref, rows_s, group_s, cycle_s, weight_s,
+    recv_ref, x_ref, fresh_ref, diff_ref, above_ref, below_ref, weight_ref, table_ref, codes_ref,
+    pick_ref, flag_ref, out_ref, send_ref, rows_s, group_s, cycle_s, column_s, weight_s,
 ):
     grp = lax.axis_index("grp")
     gx = lax.axis_index("gx")
@@ -610,29 +681,24 @@
         for r in range(ROWS):
             rows_s[r] = out_ref[:, r, :]
         for d in range(PARENTS):
-            send_ref[d] = base
+            send_ref[8 * d : 8 * d + 8, :] = base
         send_cells(rows_s, table_ref, send_ref, base)
 
     @pl.when(grp == 3)
     def _():
         load_weights(weight_ref, weight_s, gx)
-        regroup(recv_ref, 0, PGROUPS, 5, SLOTS, group_s, 0)
-        interpolate(tabs_ref, T1_ROW, weight_s, group_s, PGROUPS, cycle_s)
-        prescribe(out_ref, cycle_s, gx)
-        coarse = coarsen(out_ref)
-        send_coarse(coarse, tabs_ref, send_ref, base)
-        first = edge_block(out_ref, 0, base)
-        last = edge_block(out_ref, COLS - 1, base)
-        send_hits(coarse, tabs_ref, send_ref, base)
-        lane = iota((8, 128), 1)
-        right = PARENTS + lax.rem(gx + 1, GX)
-        left = PARENTS + lax.rem(gx + GX - 1, GX)
-        send_ref[right] = jnp.where(lane < EDGE, send_ref[right], last)
-        send_ref[left] = jnp.where(lane < EDGE, send_ref[left], first)
+        regroup(recv_ref, group_s)
+        interpolate(codes_ref, weight_s, group_s, PGROUPS, cycle_s, column_s)
+        prescribe(out_ref, cycle_s, column_s, gx)
+        send_coarse(out_ref, pick_ref, send_ref, base, SENT + TAKEN)
+        right = rows_of(PARENTS + lax.rem(gx + 1, GX))
+        left = rows_of(PARENTS + lax.rem(gx + GX - 1, GX))
+        send_ref[right, :] = send_ref[right, :] + edge_block(out_ref, COLS - 1)
+        send_ref[left, :] = send_ref[left, :] + edge_block(out_ref, 0)
 
 
 def hits_kernel(
-    x_ref, diff_ref, cor_ref, mix_ref, owner_ref, cell_ref, fb_owner_ref, fb_cell_ref, tabs_ref,
+    x_ref, diff_ref, cor_ref, mix_ref, owner_ref, cell_ref, fb_owner_ref, fb_cell_ref, plain_ref,
     fresh_ref, codes_ref, gid_s, turned_s,
 ):
     gx = lax.axis_index("gx")
@@ -658,31 +724,34 @@
         sources = [jnp.max(f, axis=0, keepdims=True) for f in from_block]
         hots = [iota((GX, 128), 0) == s for s in sources]
         found, _ = ranks(hots)
+        codes = []
         for t in range(TILES):
             slot = jnp.sum(jnp.where(hots[t], found[t], 0.0), axis=0, keepdims=True)
             slot = jnp.minimum(slot.astype(jnp.int32), HITS - 1)
             code = (PGROUPS + jnp.right_shift(sources[t], 4)) * 128
             code = code + jnp.bitwise_and(sources[t], 15) * HITS + slot
-            plain = tabs_ref[T1_ROW + t : T1_ROW + t + 1, :]
-            codes_ref[t : t + 1, :] = jnp.where(sources[t] >= 0, code, plain)
+            codes.append(jnp.where(sources[t] >= 0, code, -1))
+        for t, code in enumerate(pack_tiles(codes)):
+            plain = plain_ref[t : t + 1, :]
+            codes_ref[t : t + 1, :] = jnp.where(code >= 0, code, plain)
 
 
 def third_kernel(
-    recv_ref, x_ref, fresh_ref, diff_ref, weight_ref, tabs_ref, codes_ref, map_ref,
-    out_ref, send_ref, flag_ref, last_row_ref, first_row_ref, group_s, cycle_s, weight_s,
+    recv_ref, x_ref, fresh_ref, diff_ref, weight_ref, codes_ref, pick_ref, map_ref, entry_ref,
+    out_ref, send_ref, flag_ref, last_row_ref, first_row_ref,
+    group_s, cycle_s, column_s, weight_s,
 ):
     grp = lax.axis_index("grp")
     gx = lax.axis_index("gx")
-    blank = jnp.zeros((8, 128), F32)
-    flag = recv_ref[0]
+    flag = recv_ref[0:8, :]
     for d in range(1, DEVICES):
-        flag = jnp.maximum(flag, recv_ref[d])
+        flag = jnp.maximum(flag, recv_ref[8 * d : 8 * d + 8, :])
     flag_ref[...] = flag
 
     @pl.when(grp < 3)
     def _():
-        feed_back(x_ref, out_ref, recv_ref, map_ref, group_s)
-        send_parent_edges(out_ref, send_ref, grp, gx, blank)
+        feed_back(x_ref, out_ref, recv_ref, entry_ref, map_ref)
+        send_parent_edges(out_ref, send_ref, grp, gx)
         last_row_ref[...] = out_ref[:, ROWS - 1, :]
         first_row_ref[...] = out_ref[:, 0, :]
 
@@ -690,11 +759,11 @@
     def _():
         add_columns(fresh_ref, out_ref, recv_ref, diff_ref, grp, gx)
         load_weights(weight_ref, weight_s, gx)
-        regroup(recv_ref, 0, PGROUPS, 5, SLOTS, group_s, 0)
-        regroup(recv_ref, PARENTS, 2, 16, HITS, group_s, PGROUPS)
-        interpolate(codes_ref, 0, weight_s, group_s, GROUPS, cycle_s)
-        prescribe(out_ref, cycle_s, gx)
-        send_coarse(coarsen(out_ref), tabs_ref, send_ref, blank)
+        regroup(recv_ref, group_s)
+        regroup_hits(recv_ref, group_s)
+        interpolate(codes_ref, weight_s, group_s, GROUPS, cycle_s, column_s)
+        prescribe(out_ref, cycle_s, column_s, gx)
+        send_coarse(out_ref, pick_ref, send_ref, None, SENT)
 
 
 def parents_kernel(x_ref, diff_ref, cor_ref, mix_ref, fresh_ref):
@@ -704,7 +773,7 @@
 
 
 def fourth_kernel(
-    recv_ref, x_ref, fresh_ref, diff_ref, above_ref, below_ref, map_ref, out_ref, group_s
+    recv_ref, x_ref, fresh_ref, diff_ref, above_ref, below_ref, map_ref, entry_ref, out_ref
 ):
     grp = lax.axis_index("grp")
     gx = lax.axis_index("gx")
@@ -713,42 +782,41 @@
     def _():
         add_columns(fresh_ref, out_ref, recv_ref, diff_ref, grp, gx)
         add_rows(x_ref, out_ref, above_ref, below_ref, diff_ref, grp)
-        feed_back(out_ref, out_ref, recv_ref, map_ref, group_s)
+        feed_back(out_ref, out_ref, recv_ref, entry_ref, map_ref)
 
     @pl.when(grp == 3)
     def _():
         out_ref[...] = x_ref[...]
 
 
-def call(kernel, name, ins, spaces, outs, scratch, flops=1000000):
+def call(kernel, name, ins, spaces, outs, scratch):
+    space = {"s": pltpu.SMEM, "v": pltpu.VMEM}
     return pl.pallas_call(
         kernel,
         name=name,
-        in_specs=[
-            pl.BlockSpec(memory_space=pltpu.SMEM if s == "s" else pltpu.VMEM) for s in spaces
-        ],
+        in_specs=[pl.BlockSpec(memory_space=space[s]) for s in spaces],
         out_specs=[pl.BlockSpec(memory_space=pltpu.VMEM) for _ in outs],
         out_shape=[jax.ShapeDtypeStruct(s, d) for s, d in outs],
         scratch_shapes=[pltpu.VMEM(s, d) for s, d in scratch],
         compiler_params=pltpu.CompilerParams(vmem_limit_bytes=VMEM_LIMIT),
-        cost_estimate=pl.CostEstimate(flops=flops, bytes_accessed=4000000, transcendentals=0),
+        cost_estimate=pl.CostEstimate(flops=1000000, bytes_accessed=4000000, transcendentals=0),
     )(*ins)
 
 
 STATE = ((LANES, ROWS, COLS), F32)
-BLOCKS = ((DEVICES, 8, 128), F32)
+BLOCKS = ((DEVICES * 8, 128), F32)
+BLOCK = ((8, 128), F32)
 RIM = ((LANES, COLS), F32)
 ROWMAJOR = ((ROWS, LANES, COLS), F32)
+MAP = ((ROWS, 128), jnp.int32)
+GIDS = ((TILES, GX, 128), jnp.int32)
+TERMS = ((TILES, GX, 128), F32)
+PICK = ((SENT + TAKEN, PLANES * 128), jnp.bfloat16)
+ENTRY = ((PLANES * ENTRIES, TAKEN), jnp.bfloat16)
 GROUPED = ((GROUPS, LANES, 128), F32)
-CYCLE = ((3, LANES, 128), F32)
-WEIGHTS = ((16, 128), F32)
-TABS = ((TAB_ROWS, 128), jnp.int32)
+CYCLE = ((2, LANES, 128), F32)
 TABLE = ((GX, 128), jnp.int32)
-CODES = ((16, 128), jnp.int32)
-BLOCK = ((8, 128), F32)
-GIDS = ((TILES, GX, 128), jnp.int32)
-MAP = ((ROWS, 128), jnp.int32)
-TERMS = ((TILES, GX, 128), F32)
+CODES = ((8, 128), jnp.int32)
 
 
 def exchange(blocks):
@@ -775,27 +843,27 @@
     )
     recv = exchange(send)
     above, below = rims(last_row, first_row)
-    fresh, tabs, flag, place = call(
+    fresh, codes, pick, flag, place, entry = call(
         tables_kernel,
         "tables",
-        (atmosphere,) + physics + (owner, cell, fb_owner, fb_cell, fb_owner, fb_cell, flag),
-        "vvssvvvvssv",
-        (STATE, TABS, BLOCK, MAP),
-        (GIDS, TERMS, TERMS),
+        (atmosphere,) + physics + (owner, cell, fb_owner, fb_cell, flag),
+        "vvssvvvvv",
+        (STATE, CODES, PICK, BLOCK, MAP, ENTRY),
+        (GIDS, TERMS, TERMS, GIDS, ((32, 128), jnp.int32)),
     )
     state, send = call(
         second_kernel,
         "substep_one",
-        (recv, atmosphere, fresh, diffusion, above, below, weight, table, tabs, flag),
-        "vvvvvvvvvv",
+        (recv, atmosphere, fresh, diffusion, above, below, weight, table, codes, pick, flag),
+        "v" * 11,
         (STATE, BLOCKS),
-        (ROWMAJOR, GROUPED, CYCLE, WEIGHTS),
+        (ROWMAJOR, GROUPED, CYCLE, RIM, BLOCK),
     )
     recv = exchange(send)
     fresh, codes = call(
         hits_kernel,
         "hits",
-        (state,) + physics + (owner, cell, fb_owner, fb_cell, tabs),
+        (state,) + physics + (owner, cell, fb_owner, fb_cell, codes),
         "vvssvvvvv",
         (STATE, CODES),
         (GIDS, ((128, 128), F32)),
@@ -803,10 +871,10 @@
     state, send, flag, last_row, first_row = call(
         third_kernel,
         "substep_two",
-        (recv, state, fresh, diffusion, weight, tabs, codes, place),
-        "vvvvvvvv",
+        (recv, state, fresh, diffusion, weight, codes, pick, place, entry),
+        "v" * 9,
         (STATE, BLOCKS, BLOCK, RIM, RIM),
-        (GROUPED, CYCLE, WEIGHTS),
+        (GROUPED, CYCLE, RIM, BLOCK),
     )
     recv = exchange(send)
     above, below = rims(last_row, first_row)
@@ -814,10 +882,10 @@
     (state,) = call(
         fourth_kernel,
         "finish",
-        (recv, state, fresh, diffusion, above, below, place),
-        "vvvvvvv",
+        (recv, state, fresh, diffusion, above, below, place, entry),
+        "v" * 8,
         (STATE,),
-        (GROUPED,),
+        (),
     )
     return lax.cond(flag[0, 127] > 0.5, lambda s, *a: dense_plan(*a), lambda s, *a: s, state, *inputs)
 

time: 81.2 us -> 75.4 us (0.929)
  starting transfers between devices: 38.2 us -> 34.3 us
  Pallas kernels: 15.7 us -> 14.3 us
    all_to_all x3, starting transfers between devices: 27.3 us -> 23.3 us  [exchange(): return lax.all_to_all(blocks, ('grp', 'gx'), 0, 0, tiled=True)]
    pallas_call x7, Pallas kernels: 15.7 us -> 14.3 us  [call(): pl.pallas_call(kernel, name=name, in_specs=[pl.BlockSpec(memory_space=spa...]
where the time goes in v3:
time: 75.4 us; the launch traced here: 75 us
  starting transfers between devices  34.3 us (45%)
  waiting for transfers between devices  24 us (32%)
  Pallas kernels  14.3 us (19%)
  local copies, waits for them, and re-layouts  1.35 us (2%)
  between operations  0.89 us (1%)
    all_to_all x3, starting transfers between devices, exchange(): return lax.all_to_all(blocks, ('grp', 'gx'), 0, 0, tiled=True)  23.3 us
    all_to_all x3, waiting for transfers between devices, exchange(): return lax.all_to_all(blocks, ('grp', 'gx'), 0, 0, tiled=True)  21.1 us
    pallas_call x7, Pallas kernels, call(): pl.pallas_call(kernel, name=name, in_specs=[pl.BlockSpec(memory_space=spa...  14.3 us
    ppermute x2, starting transfers between devices, rims(): above = lax.ppermute(last_row, 'grp', [(0, 1), (1, 2)])  7.09 us
    ppermute x2, starting transfers between devices, rims(): below = lax.ppermute(first_row, 'grp', [(1, 0), (2, 1)])  3.84 us
    ppermute x2, waiting for transfers between devices, rims(): below = lax.ppermute(first_row, 'grp', [(1, 0), (2, 1)])  2.94 us
  transfers between devices with their start and end apart: 7, of which 5 were waited for; matrix products, arithmetic and copies ran while one was open for 1% of the time, Pallas kernels for 5%

profile of v3, /device:TPU:1, one launch (start us, length us, event | category | flops | bytes accessed | tf_op | source)
XLA Modules:
  0.0 75.0 jit_solution(751774712382783436)
XLA Ops:
  0.0 0.0 copy-start.2
  0.0 0.0 copy-start.3
  0.0 0.0 copy-start.5
  0.0 0.0 copy-start.25
  0.0 0.0 copy-start.28
  0.0 0.0 copy-start.15
  0.0 0.0 copy-start.17
  0.1 0.0 copy-start.4
  0.1 4.1 %first_cells.1 = (f32[1024,128]{1,0:T(8,128)}, s32[32,128]{1,0:T(8,128)S(1)}, f32[8,128]{1,0:T(8,128)S(1)}, f32[40,128]{1,0:T(8,128)S(1)}, f32[40,128]{1,0:T(8,128)S(1)}) custom-call(f32[40,16,128]{2,1,0:T(8,128)} %x_ref.5, s32[3,32,288]{2,1,0:T(8,128)} %bitcast.180, s32[3,32,288]{2,1,0:T(8,128)} %bitcast.183), custom_call_target="tpu_custom_call" | custom-call | flops 1000000 | bytes 4000000 | tf_op jit(solution)/shard_map/first_cells/pallas_call | solution.py:794
  4.2 11.5 %all-to-all-start.4 = ((f32[128,8,128]{2,1,0:T(8,128)}), f32[128,8,128]{2,1,0:T(8,128)S(1)}, u32[]{:S(2)}, u32[]{:S(2)}) async-start(f32[128,8,128]{2,1,0:T(8,128)} %bitcast.58), calls=%async_computation.4 | async-start | bytes 1048576 | tf_op jit(solution)/shard_map/all_to_all | solution.py:823
  15.7 3.5 %collective-permute-start.20 = (f32[40,128]{1,0:T(8,128)S(1)}, f32[40,128]{1,0:T(8,128)S(1)}, u32[]{:S(2)}, u32[]{:S(2)}) collective-permute-start(f32[40,128]{1,0:T(8,128)S(1)} %get-tuple-element.156), channel_id=1, source_target_pairs={{0,32},{32,64},{1,33},{33,65},{2,34},{34,66},{3,35},{35,67},{4,36}... | collective-permute-start | bytes 61448 | tf_op jit(solution)/shard_map/ppermute | solution.py:827
  19.2 1.9 %collective-permute-start.21 = (f32[40,128]{1,0:T(8,128)S(1)}, f32[40,128]{1,0:T(8,128)S(1)}, u32[]{:S(2)}, u32[]{:S(2)}) collective-permute-start(f32[40,128]{1,0:T(8,128)S(1)} %get-tuple-element.157), channel_id=1, source_target_pairs={{32,0},{64,32},{33,1},{65,33},{34,2},{66,34},{35,3},{67,35},{36,4}... | collective-permute-start | bytes 61448 | tf_op jit(solution)/shard_map/ppermute | solution.py:828
  21.2 2.7 %tables.1 = (f32[40,16,128]{2,1,0:T(8,128)S(1)}, s32[8,128]{1,0:T(8,128)S(1)}, bf16[1024,256]{1,0:T(8,128)(2,1)S(1)}, f32[8,128]{1,0:T(8,128)S(1)}, s32[16,128]{1,0:T(8,128)S(1)}, /*index=5*/bf16[256,256]{1,0:T(8,128)(2,1)S(1)}) custom-call(f32[40,16,128]{2,1,0:T(8,128)} %x_ref.5, f32[16,128]{1,0:T(8,128)} %diff_ref.11, f32[16]{0:T(128)} %cor_ref.5, ...), custom_call_target="tpu_custom_call" | custom-call | flops 1000000 | bytes 4000000 | tf_op jit(solution)/shard_map/tables/pallas_call | solution.py:794
  23.8 0.0 copy-start
  23.9 0.0 collective-permute-done.20.above_ref
  23.9 1.2 %collective-permute-done.21.below_ref = f32[40,128]{1,0:T(8,128)S(1)} collective-permute-done((f32[40,128]{1,0:T(8,128)S(1)}, f32[40,128]{1,0:T(8,128)S(1)}, u32[]{:S(2)}, u32[]{:S(2)}) %collective-permute-start.21) | collective-permute-done | bytes 20512 | tf_op jit(solution)/shard_map/ppermute | solution.py:828
  25.0 4.1 %all-to-all-done.4 = f32[128,8,128]{2,1,0:T(8,128)S(1)} async-done(((f32[128,8,128]{2,1,0:T(8,128)}), f32[128,8,128]{2,1,0:T(8,128)S(1)}, u32[]{:S(2)}, u32[]{:S(2)}) %all-to-all-start.4) | async-done | bytes 524320 | tf_op jit(solution)/shard_map/all_to_all | solution.py:823
  29.1 3.5 %substep_one.1 = (f32[40,16,128]{2,1,0:T(8,128)S(1)}, f32[1024,128]{1,0:T(8,128)}) custom-call(f32[1024,128]{1,0:T(8,128)S(1)} %bitcast.158, f32[40,16,128]{2,1,0:T(8,128)} %x_ref.5, f32[40,16,128]{2,1,0:T(8,128)S(1)} %get-tuple-element.155.fresh_ref, f32[16,128]{1,0:T(8,128)} %diff_ref.11, f32[40,128]{1,0:T(8,128)S(1)} %collective-permute-done.20.above_ref, ...), custom_call_target="tpu_custom_call" | custom-call | flops 1000000 | bytes 4000000 | tf_op jit(solution)/shard_map/substep_one/pallas_call | solution.py:794
  32.7 5.5 %all-to-all-start.5 = ((f32[128,8,128]{2,1,0:T(8,128)}), f32[128,8,128]{2,1,0:T(8,128)S(1)}, u32[]{:S(2)}, u32[]{:S(2)}) async-start(f32[128,8,128]{2,1,0:T(8,128)} %bitcast.61), calls=%async_computation.5 | async-start | bytes 1048576 | tf_op jit(solution)/shard_map/all_to_all | solution.py:823
  38.2 0.0 copy-done.2
  38.2 0.0 copy-done.3
  38.2 0.0 copy-done.5
  38.2 0.0 copy-done.25
  38.2 0.0 copy-done.28
  38.2 0.0 copy-done.15
  38.3 0.0 copy-done.17
  38.3 0.6 hits.1
  38.8 12.8 %all-to-all-done.5 = f32[128,8,128]{2,1,0:T(8,128)S(1)} async-done(((f32[128,8,128]{2,1,0:T(8,128)}), f32[128,8,128]{2,1,0:T(8,128)S(1)}, u32[]{:S(2)}, u32[]{:S(2)}) %all-to-all-start.5) | async-done | bytes 524320 | tf_op jit(solution)/shard_map/all_to_all | solution.py:823
  51.7 0.0 copy-done.4
  51.7 1.9 %substep_two.1 = (f32[40,16,128]{2,1,0:T(8,128)S(1)}, f32[1024,128]{1,0:T(8,128)}, f32[8,128]{1,0:T(8,128)S(1)}, f32[40,128]{1,0:T(8,128)S(1)}, f32[40,128]{1,0:T(8,128)S(1)}) custom-call(f32[1024,128]{1,0:T(8,128)S(1)} %bitcast.159, f32[40,16,128]{2,1,0:T(8,128)S(1)} %get-tuple-element.163.x_ref, f32[40,16,128]{2,1,0:T(8,128)S(1)} %get-tuple-element.164.fresh_ref, ...), custom_call_target="tpu_custom_call" | custom-call | flops 1000000 | bytes 4000000 | tf_op jit(solution)/shard_map/substep_two/pallas_call | solution.py:794
  53.5 6.3 %all-to-all-start.6 = ((f32[128,8,128]{2,1,0:T(8,128)}), f32[128,8,128]{2,1,0:T(8,128)S(1)}, u32[]{:S(2)}, u32[]{:S(2)}) async-start(f32[128,8,128]{2,1,0:T(8,128)} %bitcast.64), calls=%async_computation.6 | async-start | bytes 1048576 | tf_op jit(solution)/shard_map/all_to_all | solution.py:823
  59.8 3.5 %collective-permute-start.22 = (f32[40,128]{1,0:T(8,128)S(1)}, f32[40,128]{1,0:T(8,128)S(1)}, u32[]{:S(2)}, u32[]{:S(2)}) collective-permute-start(f32[40,128]{1,0:T(8,128)S(1)} %get-tuple-element.171), channel_id=1, source_target_pairs={{0,32},{32,64},{1,33},{33,65},{2,34},{34,66},{3,35},{35,67},{4,36}... | collective-permute-start | bytes 61448 | tf_op jit(solution)/shard_map/ppermute | solution.py:827
  63.4 1.9 %collective-permute-start.23 = (f32[40,128]{1,0:T(8,128)S(1)}, f32[40,128]{1,0:T(8,128)S(1)}, u32[]{:S(2)}, u32[]{:S(2)}) collective-permute-start(f32[40,128]{1,0:T(8,128)S(1)} %get-tuple-element.172), channel_id=1, source_target_pairs={{32,0},{64,32},{33,1},{65,33},{34,2},{66,34},{35,3},{67,35},{36,4}... | collective-permute-start | bytes 61448 | tf_op jit(solution)/shard_map/ppermute | solution.py:828
  65.3 0.6 slice.381
  66.6 0.8 %parents.1.fresh_ref = f32[40,16,128]{2,1,0:T(8,128)S(1)} custom-call(f32[40,16,128]{2,1,0:T(8,128)S(1)} %get-tuple-element.170.x_ref, f32[16,128]{1,0:T(8,128)S(1)} %copy-done.5, f32[16]{0:T(128)S(1)} %copy-done.25, f32[10]{0:T(128)S(1)} %copy-done.28), custom_call_target="tpu_custom_call" | custom-call | flops 1000000 | bytes 4000000 | tf_op jit(solution)/shard_map/parents/pallas_call | solution.py:794
  67.4 0.0 collective-permute-done.22.above_ref
  67.4 1.8 %collective-permute-done.23.below_ref = f32[40,128]{1,0:T(8,128)S(1)} collective-permute-done((f32[40,128]{1,0:T(8,128)S(1)}, f32[40,128]{1,0:T(8,128)S(1)}, u32[]{:S(2)}, u32[]{:S(2)}) %collective-permute-start.23) | collective-permute-done | bytes 20512 | tf_op jit(solution)/shard_map/ppermute | solution.py:828
  69.2 4.1 %all-to-all-done.6 = f32[128,8,128]{2,1,0:T(8,128)S(1)} async-done(((f32[128,8,128]{2,1,0:T(8,128)}), f32[128,8,128]{2,1,0:T(8,128)S(1)}, u32[]{:S(2)}, u32[]{:S(2)}) %all-to-all-start.6) | async-done | bytes 524320 | tf_op jit(solution)/shard_map/all_to_all | solution.py:823
  73.3 0.8 %finish.1 = f32[40,16,128]{2,1,0:T(8,128)S(1)} custom-call(f32[1024,128]{1,0:T(8,128)S(1)} %bitcast.157, f32[40,16,128]{2,1,0:T(8,128)S(1)} %get-tuple-element.170.x_ref, f32[40,16,128]{2,1,0:T(8,128)S(1)} %parents.1.fresh_ref, f32[16,128]{1,0:T(8,128)S(1)} %copy-done.5, f32[40,128]{1,0:T(8,128)S(1)} %collective-permute-done.22.above_ref, ...), custom_call_target="tpu_custom_call" | custom-call | flops 1000000 | bytes 4000000 | tf_op jit(solution)/shard_map/finish/pallas_call | solution.py:794
  74.1 0.0 copy-done
  74.1 0.2 conditional.1
  74.3 0.0 copy-start.14
  74.3 0.7 copy-done.14
Async XLA Ops:
  0.0 38.2 %copy-start.2 = (s32[32,3,288]{2,0,1:T(8,128)S(1)}, s32[32,3,288]{2,0,1:T(8,128)}, u32[]{:S(2)}) copy-start(s32[32,3,288]{2,0,1:T(8,128)} %param.33) | copy-start | bytes 331780
  0.0 38.2 %copy-start.3 = (s32[32,3,288]{2,0,1:T(8,128)S(1)}, s32[32,3,288]{2,0,1:T(8,128)}, u32[]{:S(2)}) copy-start(s32[32,3,288]{2,0,1:T(8,128)} %param.34) | copy-start | bytes 331780
  0.0 38.2 %copy-start.5 = (f32[16,128]{1,0:T(8,128)S(1)}, f32[16,128]{1,0:T(8,128)}, u32[]{:S(2)}) copy-start(f32[16,128]{1,0:T(8,128)} %diff_ref.11) | copy-start | bytes 24580
  0.0 38.2 %copy-start.25 = (f32[16]{0:T(128)S(1)}, f32[16]{0:T(128)}, u32[]{:S(2)}) copy-start(f32[16]{0:T(128)} %cor_ref.5) | copy-start | bytes 196
  0.0 38.2 %copy-start.28 = (f32[10]{0:T(128)S(1)}, f32[10]{0:T(128)}, u32[]{:S(2)}) copy-start(f32[10]{0:T(128)} %mix_ref.5) | copy-start | bytes 124
  0.0 38.2 %copy-start.15 = (s32[32,128]{1,0:T(8,128)S(1)}, s32[32,128]{1,0:T(8,128)}, u32[]{:S(2)}) copy-start(s32[32,128]{1,0:T(8,128)} %fb_owner_ref.3) | copy-start | bytes 49156
  0.0 38.2 %copy-start.17 = (s32[32,128]{1,0:T(8,128)S(1)}, s32[32,128]{1,0:T(8,128)}, u32[]{:S(2)}) copy-start(s32[32,128]{1,0:T(8,128)} %fb_cell_ref.3) | copy-start | bytes 49156
  0.1 51.6 %copy-start.4 = (f32[32,3,288]{2,0,1:T(8,128)S(1)}, f32[32,3,288]{2,0,1:T(8,128)}, u32[]{:S(2)}) copy-start(f32[32,3,288]{2,0,1:T(8,128)} %param.35) | copy-start | bytes 331780
  4.2 25.0 %all-to-all-start.4 = ((f32[128,8,128]{2,1,0:T(8,128)}), f32[128,8,128]{2,1,0:T(8,128)S(1)}, u32[]{:S(2)}, u32[]{:S(2)}) async-start(f32[128,8,128]{2,1,0:T(8,128)} %bitcast.58), calls=%async_computation.4 | async-start | bytes 1048576 | tf_op jit(solution)/shard_map/all_to_all | solution.py:823
  15.7 8.2 %collective-permute-start.20 = (f32[40,128]{1,0:T(8,128)S(1)}, f32[40,128]{1,0:T(8,128)S(1)}, u32[]{:S(2)}, u32[]{:S(2)}) collective-permute-start(f32[40,128]{1,0:T(8,128)S(1)} %get-tuple-element.156), channel_id=1, source_target_pairs={{0,32},{32,64},{1,33},{33,65},{2,34},{34,66},{3,35},{35,67},{4,36}... | collective-permute-start | bytes 61448 | tf_op jit(solution)/shard_map/ppermute | solution.py:827
  19.2 5.8 %collective-permute-start.21 = (f32[40,128]{1,0:T(8,128)S(1)}, f32[40,128]{1,0:T(8,128)S(1)}, u32[]{:S(2)}, u32[]{:S(2)}) collective-permute-start(f32[40,128]{1,0:T(8,128)S(1)} %get-tuple-element.157), channel_id=1, source_target_pairs={{32,0},{64,32},{33,1},{65,33},{34,2},{66,34},{35,3},{67,35},{36,4}... | collective-permute-start | bytes 61448 | tf_op jit(solution)/shard_map/ppermute | solution.py:828
  23.8 50.2 %copy-start = (f32[40,16,128]{2,1,0:T(8,128)S(1)}, f32[40,16,128]{2,1,0:T(8,128)}, u32[]{:S(2)}) copy-start(f32[40,16,128]{2,1,0:T(8,128)} %x_ref.5) | copy-start | bytes 983044
  32.7 19.0 %all-to-all-start.5 = ((f32[128,8,128]{2,1,0:T(8,128)}), f32[128,8,128]{2,1,0:T(8,128)S(1)}, u32[]{:S(2)}, u32[]{:S(2)}) async-start(f32[128,8,128]{2,1,0:T(8,128)} %bitcast.61), calls=%async_computation.5 | async-start | bytes 1048576 | tf_op jit(solution)/shard_map/all_to_all | solution.py:823
  53.5 19.8 %all-to-all-start.6 = ((f32[128,8,128]{2,1,0:T(8,128)}), f32[128,8,128]{2,1,0:T(8,128)S(1)}, u32[]{:S(2)}, u32[]{:S(2)}) async-start(f32[128,8,128]{2,1,0:T(8,128)} %bitcast.64), calls=%async_computation.6 | async-start | bytes 1048576 | tf_op jit(solution)/shard_map/all_to_all | solution.py:823
  59.8 7.6 %collective-permute-start.22 = (f32[40,128]{1,0:T(8,128)S(1)}, f32[40,128]{1,0:T(8,128)S(1)}, u32[]{:S(2)}, u32[]{:S(2)}) collective-permute-start(f32[40,128]{1,0:T(8,128)S(1)} %get-tuple-element.171), channel_id=1, source_target_pairs={{0,32},{32,64},{1,33},{33,65},{2,34},{34,66},{3,35},{35,67},{4,36}... | collective-permute-start | bytes 61448 | tf_op jit(solution)/shard_map/ppermute | solution.py:827
  63.4 5.8 %collective-permute-start.23 = (f32[40,128]{1,0:T(8,128)S(1)}, f32[40,128]{1,0:T(8,128)S(1)}, u32[]{:S(2)}, u32[]{:S(2)}) collective-permute-start(f32[40,128]{1,0:T(8,128)S(1)} %get-tuple-element.172), channel_id=1, source_target_pairs={{32,0},{64,32},{33,1},{65,33},{34,2},{66,34},{35,3},{67,35},{36,4}... | collective-permute-start | bytes 61448 | tf_op jit(solution)/shard_map/ppermute | solution.py:828
  74.3 0.7 copy-start.14

commit v4 on v3

--- a/solution.py
+++ b/solution.py
@@ -23,8 +23,10 @@
 PGROUPS = 20
 GROUPS = 22
 ENTRIES = 128
-PLANES = 2
-MEANS = 8 * PLANES
+PLANES = 3
+DEPTH = 4
+MEANS = DEPTH * PLANES
+MEAN_ROWS = PARENTS * DEPTH
 SENT = PARENTS * 8
 TAKEN = GX * 8
 VMEM_LIMIT = 24 * 1024 * 1024
@@ -221,7 +223,8 @@
     return jnp.concatenate(parts, axis=0), total
 
 
-def send_cells(rows_s, table_ref, send_ref, flag):
+def send_cells(rows_s, table_ref, blocks_s, send_ref, sems):
+    copies = []
     lane = iota((8, 128), 1)
     group_of = lane // SLOTS
     table = table_ref[0:GX, :]
@@ -239,12 +242,17 @@
             for k in range(FG):
                 cells[k] = jnp.where(here, take(rows_s[r, 8 * k : 8 * k + 8, :], col), cells[k])
         for q in members:
-            block = jnp.zeros((8, 128), F32) if flag is None else flag
+            block = jnp.zeros((8, 128), F32)
             for k in range(FG):
                 shift = (SLOTS * (k - (q - 5 * g))) % 128
                 moved = cells[k] if shift == 0 else pltpu.roll(cells[k], shift, 1)
                 block = jnp.where(group_of == k, moved, block)
-            send_ref[8 * (PARENTS + q) : 8 * (PARENTS + q) + 8, :] = block
+            blocks_s[8 * q : 8 * q + 8, :] = block
+        span = pl.ds(8 * members[0], 8 * len(members))
+        rows = pl.ds(SENT + 8 * members[0], 8 * len(members))
+        copies.append(pltpu.make_async_copy(blocks_s.at[span, :], send_ref.at[rows, :], sems.at[g]))
+        copies[-1].start()
+    return copies
 
 
 def edge_block(x_ref, col):
@@ -257,21 +265,52 @@
     return block
 
 
-def send_parent_edges(x_ref, send_ref, grp, gx):
-    first = edge_block(x_ref, 0)
-    last = edge_block(x_ref, COLS - 1)
+def edge_copies(edges_s, send_ref, sems, grp, gx):
     right = lax.rem(gx + 1, GX)
     left = lax.rem(gx + GX - 1, GX)
-    send_ref[rows_of(grp * GX + right), :] = last
-    send_ref[rows_of(grp * GX + left), :] = first
-
-    @pl.when(grp > 0)
-    def _():
-        send_ref[rows_of((grp - 1) * GX + right), :] = last
+    above = jnp.where(grp == 3, 3, jnp.maximum(grp - 1, 0))
+    below = jnp.where(grp == 3, 3, jnp.minimum(grp + 1, 2))
+    first, last = edges_s.at[0:8, :], edges_s.at[8:16, :]
+    plan = [
+        (last, grp * GX + right),
+        (first, grp * GX + left),
+        (last, above * GX + right),
+        (first, below * GX + left),
+    ]
+    return [
+        pltpu.make_async_copy(source, send_ref.at[rows_of(to), :], sems.at[i])
+        for i, (source, to) in enumerate(plan)
+    ]
+
+
+def send_edges(x_ref, edges_s, send_ref, sems, grp, gx):
+    edges_s[0:8, :] = edge_block(x_ref, 0)
+    edges_s[8:16, :] = edge_block(x_ref, COLS - 1)
+    near = edge_copies(edges_s, send_ref, sems, grp, gx)
+    for copy in near[:2]:
+        copy.start()
+
+    @pl.when(jnp.logical_or(grp == 1, grp == 2))
+    def _():
+        near[2].start()
 
     @pl.when(grp < 2)
     def _():
-        send_ref[rows_of((grp + 1) * GX + left), :] = first
+        near[3].start()
+
+
+def wait_edges(edges_s, send_ref, sems, grp, gx):
+    near = edge_copies(edges_s, send_ref, sems, grp, gx)
+    for copy in near[:2]:
+        copy.wait()
+
+    @pl.when(jnp.logical_or(grp == 1, grp == 2))
+    def _():
+        near[2].wait()
+
+    @pl.when(grp < 2)
+    def _():
+        near[3].wait()
 
 
 def unpack_edge(block):
@@ -303,18 +342,25 @@
         out_ref[f] = x + diff * laplace + extra
 
 
-def add_columns(from_ref, out_ref, recv_ref, diff_ref, grp, gx):
-    nest = grp == 3
+def gather_halo(recv_ref, grp, gx):
     right = lax.rem(gx + 1, GX)
     left = lax.rem(gx + GX - 1, GX)
+    from_left = unpack_edge(recv_ref[rows_of(grp * GX + left), :])
+    from_right = unpack_edge(recv_ref[rows_of(grp * GX + right), :])
+    top_right = unpack_edge(recv_ref[rows_of(jnp.maximum(grp - 1, 0) * GX + right), :])
+    low_left = unpack_edge(recv_ref[rows_of(jnp.minimum(grp + 1, 3) * GX + left), :])
+    row = iota((ROWS, COLS), 0)
+    corners = jnp.where(row == 0, top_right[ROWS - 1 : ROWS], low_left[0:1])
+    return from_left, from_right, corners
+
+
+def add_columns(from_ref, out_ref, halo, diff_ref, grp, gx):
+    from_left, from_right, corners = halo
+    nest = grp == 3
     lane = iota((ROWS, COLS), 1)
     row = iota((ROWS, COLS), 0)
-    from_left = unpack_edge(recv_ref[rows_of(grp * GX + left), :])
-    from_right = unpack_edge(recv_ref[rows_of(grp * GX + right), :])
-    top_right = unpack_edge(recv_ref[rows_of(jnp.maximum(grp - 1, 0) * GX + right), :])[ROWS - 1 : ROWS]
-    low_left = unpack_edge(recv_ref[rows_of(jnp.minimum(grp + 1, 3) * GX + left), :])[0:1]
-    top_right = jnp.where(grp == 0, from_right[0:1], top_right)
-    low_left = jnp.where(grp == 2, from_left[ROWS - 1 : ROWS], low_left)
+    top_right = jnp.where(grp == 0, from_right[0:1], corners[0:1])
+    low_left = jnp.where(grp == 2, from_left[ROWS - 1 : ROWS], corners[1:2])
     top_right = jnp.where(nest, 0.0, top_right)
     low_left = jnp.where(nest, 0.0, low_left)
     left_sum = from_left + jnp.where(row == ROWS - 1, low_left, pltpu.roll(from_left, ROWS - 1, 0))
@@ -342,10 +388,10 @@
         out_ref[f] = from_ref[f] + jnp.where(outer, moved, 0.0)
 
 
-def add_rows(x_ref, out_ref, above_ref, below_ref, diff_ref, grp):
+def add_rows(first_ref, last_ref, out_ref, above_ref, below_ref, diff_ref, grp):
     lane = iota((LANES, COLS), 1)
-    above = jnp.where(grp == 0, x_ref[:, 0, :], above_ref[...])
-    below = jnp.where(grp == 2, x_ref[:, ROWS - 1, :], below_ref[...])
+    above = jnp.where(grp == 0, first_ref[...], above_ref[...])
+    below = jnp.where(grp == 2, last_ref[...], below_ref[...])
     above = above + jnp.where(lane == COLS - 1, 0.0, pltpu.roll(above, COLS - 1, 1))
     below = below + jnp.where(lane == 0, 0.0, pltpu.roll(below, 1, 1))
     out_ref[:, 0, :] = out_ref[:, 0, :] + diff_ref[0:1, :] * above
@@ -443,14 +489,14 @@
     out_ref[:, ROWS - 1, :] = cycle_s[1]
 
 
-def send_coarse(out_ref, pick_ref, send_ref, base, count):
+def coarse_values(out_ref):
     mean = jnp.where(iota((32, 128), 1) // 4 == iota((32, 128), 0), 1.0 / 16.0, 0.0)
     parts = []
     for i in range(4):
         total = (out_ref[:, 4 * i, :] + out_ref[:, 4 * i + 1, :]) + (
             out_ref[:, 4 * i + 2, :] + out_ref[:, 4 * i + 3, :]
         )
-        wide = jnp.concatenate([total, total, jnp.zeros((48, 128), F32)], axis=0)
+        wide = jnp.concatenate([total, total, total, jnp.zeros((8, 128), F32)], axis=0)
         parts.append(
             lax.dot_general(
                 mean,
@@ -463,67 +509,106 @@
     coarse = jnp.concatenate(parts, axis=0)
     plane_of = iota((128, 128), 1) // LANES
     placed = [jnp.where(plane_of == plane, coarse, 0.0) for plane in range(PLANES)]
-    high, low = halves(jnp.concatenate(placed, axis=0))
-    both = product(pick_ref[0:count, :], jnp.concatenate([high, low], axis=1))
-    sent = both[:, 0:128] + both[:, 128:256]
-    if base is not None:
-        sent = sent + base[0:1, :]
-    send_ref[0:count, :] = sent
-
-
-def feed_back(src_ref, out_ref, recv_ref, pick_ref, map_ref):
-    high, low = halves(recv_ref[SENT : SENT + TAKEN, :])
-    both = product(pick_ref[...], jnp.concatenate([high, low], axis=1))
-    total = both[:, 0:128] + both[:, 128:256]
+    return jnp.concatenate(halves(jnp.concatenate(placed, axis=0)), axis=1)
+
+
+def picked(pick, values):
+    both = product(pick, values)
+    return both[:, 0:128] + both[:, 128:256]
+
+
+def unpack_entries(pick_ref, values):
+    total = picked(pick_ref[...], jnp.concatenate(halves(values), axis=1))
     entries = total[0:ENTRIES]
     for plane in range(1, PLANES):
         part = total[plane * ENTRIES : (plane + 1) * ENTRIES]
         entries = entries + pltpu.roll(part, 128 - LANES * plane, 1)
-    turned = entries.T
+    return entries
+
+
+def place_rows(codes, turned, own):
+    code = jnp.broadcast_to(codes, (8, 128))
+    index = jnp.bitwise_and(code, 127)
+    return [
+        jnp.where(code >= 0, take(turned[8 * k : 8 * k + 8], index), own(slice(8 * k, 8 * k + 8)))
+        for k in range(FG)
+    ]
+
+
+def feed_back(src_ref, out_ref, turned, map_ref):
     for r in range(ROWS):
-        code = jnp.broadcast_to(map_ref[r : r + 1, :], (8, 128))
-        fed = code >= 0
-        index = jnp.bitwise_and(code, 127)
+        cells = place_rows(map_ref[r : r + 1, :], turned, lambda span: src_ref[span, r, :])
         for k in range(FG):
-            span = slice(8 * k, 8 * k + 8)
-            out_ref[span, r, :] = jnp.where(fed, take(turned[span], index), src_ref[span, r, :])
-
-
-def feedback_routes(owner_ref, cell_ref, pick_ref, map_ref, me):
-    cell = cell_ref[...]
-    own = owner_ref[...] == me
-    found, total = ranks([own])
-    slot = jnp.minimum(found[0], float(MEANS - 1))
-    below = jnp.where(iota((GX, GX), 1) < iota((GX, GX), 0), 1.0, 0.0).astype(jnp.bfloat16)
-    entry = found[0] + product(below, total.astype(jnp.bfloat16))
-    entry = jnp.where(own, entry, -1.0)
-    plane = jnp.floor(slot * 0.125)
-    place = iota((GX, 128), 0).astype(F32) * 8.0 + (slot - 8.0 * plane)
+            out_ref[8 * k : 8 * k + 8, r, :] = cells[k]
+
+
+def neighbours_of(owner, cell):
     row = jnp.right_shift(cell, 7)
     col = jnp.bitwise_and(cell, 127)
-    cells = jnp.zeros((ROWS, 128), F32)
+    at = jnp.bitwise_and(owner, GX - 1)
+    left = owner - at + jnp.bitwise_and(at + GX - 1, GX - 1)
+    right = owner - at + jnp.bitwise_and(at + 1, GX - 1)
+    top = jnp.logical_and(row == 0, owner >= GX)
+    low = jnp.logical_and(row == ROWS - 1, owner < 2 * GX)
+    beside = jnp.where(col == 0, left, jnp.where(col == COLS - 1, right, -1))
+    across = jnp.where(top, owner - GX, jnp.where(low, owner + GX, -1))
+    diagonal = jnp.where(
+        jnp.logical_and(low, col == 0),
+        left + GX,
+        jnp.where(jnp.logical_and(top, col == COLS - 1), right - GX, -1),
+    )
+    return owner, beside, across, diagonal
+
+
+def feedback_routes(owner_ref, cell_ref, pick_ref, map_ref, halo_ref, me):
+    cell = cell_ref[...]
+    owner = owner_ref[...]
+    row = jnp.right_shift(cell, 7)
+    col = jnp.bitwise_and(cell, 127)
+    own = owner == me
+    left = me - lax.rem(me, GX) + lax.rem(me + GX - 1, GX)
+    right = me - lax.rem(me, GX) + lax.rem(me + 1, GX)
+    above = jnp.logical_and(owner == me - GX, row == ROWS - 1)
+    below = jnp.logical_and(owner == me + GX, row == 0)
+    target = jnp.where(jnp.logical_and(owner == left, col == COLS - 1), row, -1)
+    target = jnp.where(jnp.logical_and(owner == right, col == 0), ROWS + row, target)
+    corner = jnp.logical_and(row == ROWS - 1, col == 0)
+    target = jnp.where(jnp.logical_and(owner == right - GX, corner), 2 * ROWS, target)
+    corner = jnp.logical_and(row == 0, col == COLS - 1)
+    target = jnp.where(jnp.logical_and(owner == left + GX, corner), 2 * ROWS + 1, target)
+    taken = jnp.logical_or(jnp.logical_or(own, target >= 0), jnp.logical_or(above, below))
+    found, total = ranks([taken])
+    slot = jnp.minimum(found[0], float(MEANS - 1))
+    before = jnp.where(iota((GX, GX), 1) < iota((GX, GX), 0), 1.0, 0.0).astype(jnp.bfloat16)
+    entry = found[0] + product(before, total.astype(jnp.bfloat16))
+    plane = jnp.floor(slot * (1.0 / DEPTH))
+    place = iota((GX, 128), 0).astype(F32) * float(DEPTH) + (slot - float(DEPTH) * plane)
+    line = jnp.where(own, row, jnp.where(above, ROWS, jnp.where(below, ROWS + 1, -1)))
+    entry = jnp.where(taken, entry, -1.0)
+    target = target.astype(F32)
+    cells = jnp.zeros((2 * ROWS, 128), F32)
     codes = jnp.zeros((ENTRIES, 128), F32)
     for q in range(GX):
-        line = slice(q, q + 1)
-        here = jnp.where(iota((ROWS, 128), 0) == row[line], entry[line] + 1.0, 0.0)
-        hot = jnp.where(iota((128, 128), 0) == col[line], 1.0, 0.0)
+        one = slice(q, q + 1)
+        here = jnp.where(iota((2 * ROWS, 128), 0) == line[one], entry[one] + 1.0, 0.0)
+        hot = jnp.where(iota((128, 128), 0) == col[one], 1.0, 0.0)
         cells = cells + product(here.astype(jnp.bfloat16), hot.astype(jnp.bfloat16), (1, 1))
-        hot = jnp.where(iota((ENTRIES, 128), 0).astype(F32) == entry[line], 1.0, 0.0)
-        both = jnp.where(
-            iota((128, 128), 0) == 0,
-            place[line],
-            jnp.where(iota((128, 128), 0) == 1, plane[line] + 1.0, 0.0),
-        )
-        codes = codes + product(hot.astype(jnp.bfloat16), both.astype(jnp.bfloat16), (1, 1))
+        hot = jnp.where(iota((ENTRIES, 128), 0).astype(F32) == entry[one], 1.0, 0.0)
+        number = iota((128, 128), 0)
+        facts = jnp.where(number == 1, plane[one] + 1.0, 0.0)
+        facts = jnp.where(number == 0, place[one], jnp.where(number == 2, target[one] + 1.0, facts))
+        codes = codes + product(hot.astype(jnp.bfloat16), facts.astype(jnp.bfloat16), (1, 1))
     map_ref[...] = cells.astype(jnp.int32) - 1
     at = codes[:, 0:1]
     level = codes[:, 1:2] - 1.0
-    lane = iota((ENTRIES, TAKEN), 1).astype(F32)
+    lane = iota((ENTRIES, 128), 1).astype(F32)
     for p in range(PLANES):
         hot = jnp.where(jnp.where(level == float(p), at, -1.0) == lane, 1.0, 0.0)
         pick_ref[p * ENTRIES : (p + 1) * ENTRIES, :] = hot.astype(jnp.bfloat16)
-    count = jnp.sum(jnp.where(own, 1.0, 0.0), axis=0, keepdims=True)
-    return jnp.where(jnp.sum(count, axis=1, keepdims=True) > float(ENTRIES), 1.0, 0.0)
+    goal = codes.T[2:3, :] - 1.0
+    halo_ref[...] = jnp.where(iota((3 * ROWS, 128), 0).astype(F32) == goal, 1.0, 0.0).astype(
+        jnp.bfloat16
+    )
 
 
 def load_terms(owner_ref, cell_ref, gid_s):
@@ -542,39 +627,51 @@
 
 
 def first_kernel(
-    x_ref, owner_ref, cell_ref, send_ref, table_ref, flag_ref, last_row_ref, first_row_ref,
-    gid_s, mark_s, value_s, rows_s,
+    x_ref, owner_ref, cell_ref, send_ref, table_ref, last_row_ref, first_row_ref,
+    x_s, owner_s, cell_s, gid_s, mark_s, value_s, rows_s, blocks_s, edges_s, in_sems, out_sems, edge_sems,
 ):
     grp = lax.axis_index("grp")
     gx = lax.axis_index("gx")
-    last_row_ref[...] = x_ref[:, ROWS - 1, :]
-    first_row_ref[...] = x_ref[:, 0, :]
+    fetch_x = pltpu.make_async_copy(x_ref, x_s, in_sems.at[0])
+    fetch_index = [
+        pltpu.make_async_copy(owner_ref, owner_s, in_sems.at[1]),
+        pltpu.make_async_copy(cell_ref, cell_s, in_sems.at[2]),
+    ]
 
     @pl.when(grp < 3)
     def _():
-        load_terms(owner_ref, cell_ref, gid_s)
+        for copy in fetch_index:
+            copy.start()
+        fetch_x.start()
+        for copy in fetch_index:
+            copy.wait()
+        load_terms(owner_s, cell_s, gid_s)
         gids = [gid_s[t] for t in range(TILES)]
         masks = [jnp.right_shift(g, 11) == grp * GX + gx for g in gids]
         values = [jnp.bitwise_and(g, 2047).astype(F32) for g in gids]
-        table, total = slot_table(masks, values, SLOTS, mark_s, value_s)
+        table, _ = slot_table(masks, values, SLOTS, mark_s, value_s)
         table_ref[...] = table.astype(jnp.int32)
-        flag_ref[...] = flag_block(jnp.where(total > float(SLOTS), 1.0, 0.0))
+        fetch_x.wait()
+        send_edges(x_s, edges_s, send_ref, edge_sems, grp, gx)
+        last_row_ref[...] = x_s[:, ROWS - 1, :]
+        first_row_ref[...] = x_s[:, 0, :]
         for r in range(ROWS):
-            rows_s[r] = x_ref[:, r, :]
-        send_cells(rows_s, table_ref, send_ref, None)
-        send_parent_edges(x_ref, send_ref, grp, gx)
+            rows_s[r] = x_s[:, r, :]
+        for copy in send_cells(rows_s, table_ref, blocks_s, send_ref, out_sems):
+            copy.wait()
 
     @pl.when(grp == 3)
     def _():
-        right = PARENTS + lax.rem(gx + 1, GX)
-        left = PARENTS + lax.rem(gx + GX - 1, GX)
-        send_ref[rows_of(right), :] = edge_block(x_ref, COLS - 1)
-        send_ref[rows_of(left), :] = edge_block(x_ref, 0)
+        fetch_x.start()
+        fetch_x.wait()
+        send_edges(x_s, edges_s, send_ref, edge_sems, grp, gx)
+
+    wait_edges(edges_s, send_ref, edge_sems, grp, gx)
 
 
 def tables_kernel(
-    x_ref, diff_ref, cor_ref, mix_ref, owner_ref, cell_ref, fb_owner_ref, fb_cell_ref,
-    flag_in_ref, fresh_ref, codes_ref, pick_ref, flag_ref, map_ref, entry_ref,
+    x_ref, diff_ref, cor_ref, mix_ref, owner_ref, cell_ref, weight_ref, fb_owner_ref, fb_cell_ref,
+    fresh_ref, codes_ref, weights_ref, pick_ref, hits_ref, flag_ref, map_ref, entry_ref, halo_ref,
     gid_s, mark_s, value_s, found_s, seek_s,
 ):
     grp = lax.axis_index("grp")
@@ -583,32 +680,63 @@
 
     @pl.when(grp < 3)
     def _():
-        over = feedback_routes(fb_owner_ref, fb_cell_ref, entry_ref, map_ref, grp * GX + gx)
-        lane = iota((8, 128), 1)
-        flag_ref[...] = jnp.where(lane == 127, jnp.maximum(flag_in_ref[...], over), 0.0)
+        feedback_routes(
+            fb_owner_ref, fb_cell_ref, entry_ref, map_ref, halo_ref, grp * GX + gx
+        )
 
     @pl.when(grp == 3)
     def _():
         load_terms(owner_ref, cell_ref, gid_s)
-        own_owner = fb_owner_ref[pl.ds(gx, 1), :]
+        load_weights(weight_ref, weights_ref, gx)
+
+        number = iota((PARENTS, 128), 0)
+        everyone = neighbours_of(fb_owner_ref[...], fb_cell_ref[...])
+        back = jnp.zeros((PARENTS, 128), F32)
+        for q in range(GX):
+            hit = number == everyone[0][q : q + 1, :]
+            for other in everyone[1:]:
+                hit = jnp.logical_or(hit, number == other[q : q + 1, :])
+            back = back + jnp.where(hit, 1.0, 0.0)
+        back = jnp.sum(back, axis=1, keepdims=True)
+
         own_cell = fb_cell_ref[pl.ds(gx, 1), :]
-        hot = iota((128, 128), 0) == own_owner
-        found, total = ranks([hot])
+        goals = neighbours_of(fb_owner_ref[pl.ds(gx, 1), :], own_cell)
+        number = iota((128, 128), 0)
+        hots = [number == goal for goal in goals]
+        anyone = jnp.logical_or(jnp.logical_or(hots[0], hots[1]), jnp.logical_or(hots[2], hots[3]))
+        found, total = ranks([anyone])
         over = jnp.max(jnp.where(total > float(MEANS), 1.0, 0.0), axis=0, keepdims=True)
-        rank = jnp.sum(jnp.where(hot, found[0], 0.0), axis=0, keepdims=True).astype(jnp.int32)
-        level = jnp.right_shift(rank, 3)
-        place = own_owner * 8 + jnp.bitwise_and(rank, 7)
+        over = jnp.maximum(
+            over, jnp.max(jnp.where(back > float(ENTRIES), 1.0, 0.0), axis=0, keepdims=True)
+        )
+        most = jnp.minimum(jnp.max(total).astype(jnp.int32), 32)
+        slots = [
+            jnp.sum(jnp.where(h, found[0], 0.0), axis=0, keepdims=True).astype(jnp.int32)
+            for h in hots
+        ]
         for p in range(PLANES):
-            wanted = jnp.where(level == p, place, -1)
-            for part in range(6):
-                line = iota((128, 128), 0) + 128 * part
+            wanted = [
+                jnp.where(
+                    jnp.logical_and(goal >= 0, slot // DEPTH == p), goal * DEPTH + slot % DEPTH, -1
+                )
+                for goal, slot in zip(goals, slots)
+            ]
+            for part in range(MEAN_ROWS // 128):
+                line = number + 128 * part
+                hit = line == wanted[0]
+                for other in wanted[1:]:
+                    hit = jnp.logical_or(hit, line == other)
                 pick_ref[128 * part : 128 * part + 128, 128 * p : 128 * p + 128] = jnp.where(
-                    line == wanted, 1.0, 0.0
+                    hit, 1.0, 0.0
                 ).astype(jnp.bfloat16)
+        hot, rank = hots[0], slots[0]
 
         owners = [jnp.right_shift(gid_s[t, pl.ds(gx, 1), :], 11) for t in range(TILES)]
         hots = [iota((PARENTS, 128), 0) == o for o in owners]
-        found, _ = ranks(hots)
+        found, total = ranks(hots)
+        over = jnp.maximum(
+            over, jnp.max(jnp.where(total > float(SLOTS), 1.0, 0.0), axis=0, keepdims=True)
+        )
         codes = []
         for t in range(TILES):
             slot = jnp.sum(jnp.where(hots[t], found[t], 0.0), axis=0, keepdims=True)
@@ -643,7 +771,6 @@
                     )
             return carry
 
-        most = jnp.minimum(jnp.max(total).astype(jnp.int32), 32)
         lax.fori_loop(0, most, seek, 0)
         found_at = [found_s[t] for t in range(TILES)]
         table, total = slot_table(
@@ -654,47 +781,62 @@
         )
         turned = jnp.concatenate([table, jnp.zeros((96, 128), F32)], axis=0).T
         lane = iota((8, 128), 1).astype(F32)
-        blank = jnp.zeros((16, 128 * (PLANES - 1)), jnp.bfloat16)
         for pair in range(GX // 2):
-            line = slice(SENT + 16 * pair, SENT + 16 * pair + 16)
             hits = [
                 jnp.where(turned[0:HITS, q : q + 1] == lane, 1.0, 0.0)
                 for q in (2 * pair, 2 * pair + 1)
             ]
-            pick_ref[line, 0:128] = jnp.concatenate(hits, axis=0).astype(jnp.bfloat16)
-            pick_ref[line, 128 : 128 * PLANES] = blank
+            line = slice(16 * pair, 16 * pair + 16)
+            hits_ref[line, :] = jnp.concatenate(hits, axis=0).astype(jnp.bfloat16)
         flag_ref[...] = flag_block(over)
 
 
 def second_kernel(
-    recv_ref, x_ref, fresh_ref, diff_ref, above_ref, below_ref, weight_ref, table_ref, codes_ref,
-    pick_ref, flag_ref, out_ref, send_ref, rows_s, group_s, cycle_s, column_s, weight_s,
+    recv_ref, fresh_ref, diff_ref, above_ref, below_ref, first_ref, last_ref, weights_ref, table_ref,
+    codes_ref, pick_ref, hits_ref, flag_ref, out_ref, send_ref, last_row_ref, first_row_ref,
+    rows_s, group_s, cycle_s, column_s, blocks_s, edges_s, out_sems, edge_sems,
 ):
     grp = lax.axis_index("grp")
     gx = lax.axis_index("gx")
-    add_columns(fresh_ref, out_ref, recv_ref, diff_ref, grp, gx)
-    base = flag_ref[...]
+    add_columns(fresh_ref, out_ref, gather_halo(recv_ref, grp, gx), diff_ref, grp, gx)
 
     @pl.when(grp < 3)
     def _():
-        add_rows(x_ref, out_ref, above_ref, below_ref, diff_ref, grp)
+        add_rows(first_ref, last_ref, out_ref, above_ref, below_ref, diff_ref, grp)
+        send_edges(out_ref, edges_s, send_ref, edge_sems, grp, gx)
+        last_row_ref[...] = out_ref[:, ROWS - 1, :]
+        first_row_ref[...] = out_ref[:, 0, :]
         for r in range(ROWS):
             rows_s[r] = out_ref[:, r, :]
-        for d in range(PARENTS):
-            send_ref[8 * d : 8 * d + 8, :] = base
-        send_cells(rows_s, table_ref, send_ref, base)
+        for copy in send_cells(rows_s, table_ref, blocks_s, send_ref, out_sems):
+            copy.wait()
+        wait_edges(edges_s, send_ref, edge_sems, grp, gx)
 
     @pl.when(grp == 3)
     def _():
-        load_weights(weight_ref, weight_s, gx)
         regroup(recv_ref, group_s)
-        interpolate(codes_ref, weight_s, group_s, PGROUPS, cycle_s, column_s)
+        interpolate(codes_ref, weights_ref, group_s, PGROUPS, cycle_s, column_s)
         prescribe(out_ref, cycle_s, column_s, gx)
-        send_coarse(out_ref, pick_ref, send_ref, base, SENT + TAKEN)
+        values = coarse_values(out_ref)
+        base = flag_ref[0:1, :]
+        sent = picked(pick_ref[...], values) + base
+        for j in range(PARENTS // 2):
+            tile = sent[8 * j : 8 * j + 8]
+            blocks_s[16 * j : 16 * j + 8, :] = tile
+            blocks_s[16 * j + 8 : 16 * j + 16, :] = pltpu.roll(tile, DEPTH, 0)
+        copies = [
+            pltpu.make_async_copy(blocks_s.at[rows, :], send_ref.at[rows, :], out_sems.at[i])
+            for i, rows in enumerate((pl.ds(0, SENT), pl.ds(SENT, TAKEN)))
+        ]
+        copies[0].start()
+        blocks_s[SENT : SENT + TAKEN, :] = picked(hits_ref[...], values[0:128]) + base
         right = rows_of(PARENTS + lax.rem(gx + 1, GX))
         left = rows_of(PARENTS + lax.rem(gx + GX - 1, GX))
-        send_ref[right, :] = send_ref[right, :] + edge_block(out_ref, COLS - 1)
-        send_ref[left, :] = send_ref[left, :] + edge_block(out_ref, 0)
+        blocks_s[right, :] = blocks_s[right, :] + edge_block(out_ref, COLS - 1)
+        blocks_s[left, :] = blocks_s[left, :] + edge_block(out_ref, 0)
+        copies[1].start()
+        for copy in copies:
+            copy.wait()
 
 
 def hits_kernel(
@@ -737,67 +879,91 @@
 
 
 def third_kernel(
-    recv_ref, x_ref, fresh_ref, diff_ref, weight_ref, codes_ref, pick_ref, map_ref, entry_ref,
-    out_ref, send_ref, flag_ref, last_row_ref, first_row_ref,
-    group_s, cycle_s, column_s, weight_s,
+    recv_ref, x_ref, fresh_ref, diff_ref, weights_ref, codes_ref, pick_ref, map_ref, entry_ref,
+    halo_ref, above_ref, below_ref, out_ref, send_ref, flag_ref, rims_ref, halos_ref,
+    group_s, cycle_s, column_s, blocks_s, out_sem,
 ):
     grp = lax.axis_index("grp")
     gx = lax.axis_index("gx")
-    flag = recv_ref[0:8, :]
-    for d in range(1, DEVICES):
-        flag = jnp.maximum(flag, recv_ref[8 * d : 8 * d + 8, :])
+    flag = recv_ref[SENT : SENT + 8, :]
+    for q in range(1, GX):
+        flag = jnp.maximum(flag, recv_ref[SENT + 8 * q : SENT + 8 * q + 8, :])
     flag_ref[...] = flag
 
     @pl.when(grp < 3)
     def _():
-        feed_back(x_ref, out_ref, recv_ref, entry_ref, map_ref)
-        send_parent_edges(out_ref, send_ref, grp, gx)
-        last_row_ref[...] = out_ref[:, ROWS - 1, :]
-        first_row_ref[...] = out_ref[:, 0, :]
+        upper = iota((8, 128), 0) < DEPTH
+        tiles = []
+        for j in range(GX // 2):
+            even = recv_ref[SENT + 16 * j : SENT + 16 * j + 8, :]
+            odd = recv_ref[SENT + 16 * j + 8 : SENT + 16 * j + 16, :]
+            tiles.append(jnp.where(upper, even, pltpu.roll(odd, DEPTH, 0)))
+        entries = unpack_entries(entry_ref, jnp.concatenate(tiles, axis=0))
+        turned = entries.T
+        feed_back(x_ref, out_ref, turned, map_ref)
+        for k, cells in enumerate(
+            place_rows(map_ref[ROWS : ROWS + 1, :], turned, lambda span: above_ref[span, :])
+        ):
+            rims_ref[0, 8 * k : 8 * k + 8, :] = cells
+        for k, cells in enumerate(
+            place_rows(map_ref[ROWS + 1 : ROWS + 2, :], turned, lambda span: below_ref[span, :])
+        ):
+            rims_ref[1, 8 * k : 8 * k + 8, :] = cells
+        hot = halo_ref[...]
+        moved = jnp.concatenate(halves(pltpu.roll(entries, EDGE, 1)), axis=1)
+        fed = jnp.sum(hot.astype(F32), axis=1, keepdims=True) > 0.5
+        before = jnp.concatenate(gather_halo(recv_ref, grp, gx), axis=0)
+        halos_ref[...] = jnp.where(fed, picked(hot, moved), before)
 
     @pl.when(grp == 3)
     def _():
-        add_columns(fresh_ref, out_ref, recv_ref, diff_ref, grp, gx)
-        load_weights(weight_ref, weight_s, gx)
+        add_columns(fresh_ref, out_ref, gather_halo(recv_ref, grp, gx), diff_ref, grp, gx)
         regroup(recv_ref, group_s)
         regroup_hits(recv_ref, group_s)
-        interpolate(codes_ref, weight_s, group_s, GROUPS, cycle_s, column_s)
+        interpolate(codes_ref, weights_ref, group_s, GROUPS, cycle_s, column_s)
         prescribe(out_ref, cycle_s, column_s, gx)
-        send_coarse(out_ref, pick_ref, send_ref, None, SENT)
-
-
-def parents_kernel(x_ref, diff_ref, cor_ref, mix_ref, fresh_ref):
-    @pl.when(lax.axis_index("grp") < 3)
+        blocks_s[...] = picked(pick_ref[...], coarse_values(out_ref))
+        copy = pltpu.make_async_copy(blocks_s, send_ref.at[pl.ds(0, MEAN_ROWS), :], out_sem.at[0])
+        copy.start()
+        copy.wait()
+
+
+def parents_kernel(x_ref, diff_ref, cor_ref, mix_ref, rims_ref, halos_ref, fresh_ref):
+    grp = lax.axis_index("grp")
+
+    @pl.when(grp < 3)
     def _():
         update(x_ref, fresh_ref, diff_ref, cor_ref, mix_ref)
-
-
-def fourth_kernel(
-    recv_ref, x_ref, fresh_ref, diff_ref, above_ref, below_ref, map_ref, entry_ref, out_ref
-):
+        halo = (halos_ref[0:ROWS, :], halos_ref[ROWS : 2 * ROWS, :], halos_ref[2 * ROWS : 3 * ROWS, :])
+        add_columns(fresh_ref, fresh_ref, halo, diff_ref, grp, lax.axis_index("gx"))
+        first = x_ref[:, 0, :]
+        last = x_ref[:, ROWS - 1, :]
+        add_rows(first, last, fresh_ref, rims_ref[0], rims_ref[1], diff_ref, grp)
+
+
+def fourth_kernel(recv_ref, x_ref, fresh_ref, map_ref, entry_ref, out_ref):
     grp = lax.axis_index("grp")
-    gx = lax.axis_index("gx")
 
     @pl.when(grp < 3)
     def _():
-        add_columns(fresh_ref, out_ref, recv_ref, diff_ref, grp, gx)
-        add_rows(x_ref, out_ref, above_ref, below_ref, diff_ref, grp)
-        feed_back(out_ref, out_ref, recv_ref, entry_ref, map_ref)
+        entries = unpack_entries(entry_ref, recv_ref[MEAN_ROWS : MEAN_ROWS + 128, :])
+        feed_back(fresh_ref, out_ref, entries.T, map_ref)
 
     @pl.when(grp == 3)
     def _():
         out_ref[...] = x_ref[...]
 
 
-def call(kernel, name, ins, spaces, outs, scratch):
-    space = {"s": pltpu.SMEM, "v": pltpu.VMEM}
+def call(kernel, name, ins, spaces, outs, out_spaces, scratch, sems=()):
+    space = {"s": pltpu.SMEM, "v": pltpu.VMEM, "a": pl.ANY}
     return pl.pallas_call(
         kernel,
         name=name,
         in_specs=[pl.BlockSpec(memory_space=space[s]) for s in spaces],
-        out_specs=[pl.BlockSpec(memory_space=pltpu.VMEM) for _ in outs],
+        out_specs=[pl.BlockSpec(memory_space=space[s]) for s in out_spaces],
         out_shape=[jax.ShapeDtypeStruct(s, d) for s, d in outs],
-        scratch_shapes=[pltpu.VMEM(s, d) for s, d in scratch],
+        scratch_shapes=[pltpu.VMEM(s, d) for s, d in scratch]
+        + [pltpu.SemaphoreType.DMA((n,)) for n in sems],
         compiler_params=pltpu.CompilerParams(vmem_limit_bytes=VMEM_LIMIT),
         cost_estimate=pl.CostEstimate(flops=1000000, bytes_accessed=4000000, transcendentals=0),
     )(*ins)
@@ -808,15 +974,23 @@
 BLOCK = ((8, 128), F32)
 RIM = ((LANES, COLS), F32)
 ROWMAJOR = ((ROWS, LANES, COLS), F32)
-MAP = ((ROWS, 128), jnp.int32)
+MAP = ((2 * ROWS, 128), jnp.int32)
 GIDS = ((TILES, GX, 128), jnp.int32)
 TERMS = ((TILES, GX, 128), F32)
-PICK = ((SENT + TAKEN, PLANES * 128), jnp.bfloat16)
-ENTRY = ((PLANES * ENTRIES, TAKEN), jnp.bfloat16)
+PICK = ((MEAN_ROWS, PLANES * 128), jnp.bfloat16)
+HIT = ((TAKEN, 128), jnp.bfloat16)
+ENTRY = ((PLANES * ENTRIES, 128), jnp.bfloat16)
+HALO = ((3 * ROWS, 128), jnp.bfloat16)
+HALOS = ((3 * ROWS, 128), F32)
+RIMS = ((2, LANES, COLS), F32)
+THIN = ((DEVICES * DEPTH, 128), F32)
 GROUPED = ((GROUPS, LANES, 128), F32)
 CYCLE = ((2, LANES, 128), F32)
 TABLE = ((GX, 128), jnp.int32)
 CODES = ((8, 128), jnp.int32)
+INDEX = ((3, GX, PERIM), jnp.int32)
+EDGES = ((16, 128), F32)
+TO_NEST = ((TAKEN, 128), F32)
 
 
 def exchange(blocks):
@@ -833,58 +1007,75 @@
     inputs = (atmosphere, diffusion, coriolis, mixing, owner, cell, weight, fb_owner, fb_cell)
     owner, cell, weight = (jnp.transpose(a, (1, 0, 2)) for a in (owner, cell, weight))
     physics = (diffusion, coriolis, mixing)
-    send, table, flag, last_row, first_row = call(
+    send, table, last_row, first_row = call(
         first_kernel,
         "first_cells",
         (atmosphere, owner, cell),
-        "vvv",
-        (BLOCKS, TABLE, BLOCK, RIM, RIM),
-        (GIDS, TERMS, TERMS, ROWMAJOR),
+        "aaa",
+        (BLOCKS, TABLE, RIM, RIM),
+        "avvv",
+        (STATE, INDEX, INDEX, GIDS, TERMS, TERMS, ROWMAJOR, TO_NEST, EDGES),
+        (3, 7, 4),
     )
     recv = exchange(send)
     above, below = rims(last_row, first_row)
-    fresh, codes, pick, flag, place, entry = call(
+    fresh, codes, weights, pick, hits, flag, place, entry, halo = call(
         tables_kernel,
         "tables",
-        (atmosphere,) + physics + (owner, cell, fb_owner, fb_cell, flag),
+        (atmosphere,) + physics + (owner, cell, weight, fb_owner, fb_cell),
         "vvssvvvvv",
-        (STATE, CODES, PICK, BLOCK, MAP, ENTRY),
+        (STATE, CODES, BLOCK, PICK, HIT, BLOCK, MAP, ENTRY, HALO),
+        "vvvvvvvvv",
         (GIDS, TERMS, TERMS, GIDS, ((32, 128), jnp.int32)),
     )
-    state, send = call(
+    state, send, next_last, next_first = call(
         second_kernel,
         "substep_one",
-        (recv, atmosphere, fresh, diffusion, above, below, weight, table, codes, pick, flag),
-        "v" * 11,
-        (STATE, BLOCKS),
-        (ROWMAJOR, GROUPED, CYCLE, RIM, BLOCK),
+        (recv, fresh, diffusion, above, below, first_row, last_row, weights, table, codes, pick, hits, flag),
+        "v" * 13,
+        (STATE, BLOCKS, RIM, RIM),
+        "vavv",
+        (ROWMAJOR, GROUPED, CYCLE, RIM, BLOCKS, EDGES),
+        (7, 4),
     )
     recv = exchange(send)
+    above, below = rims(next_last, next_first)
     fresh, codes = call(
         hits_kernel,
         "hits",
         (state,) + physics + (owner, cell, fb_owner, fb_cell, codes),
         "vvssvvvvv",
         (STATE, CODES),
+        "vv",
         (GIDS, ((128, 128), F32)),
     )
-    state, send, flag, last_row, first_row = call(
+    state, send, flag, edge_rows, halos = call(
         third_kernel,
         "substep_two",
-        (recv, state, fresh, diffusion, weight, codes, pick, place, entry),
-        "v" * 9,
-        (STATE, BLOCKS, BLOCK, RIM, RIM),
-        (GROUPED, CYCLE, RIM, BLOCK),
+        (recv, state, fresh, diffusion, weights, codes, pick, place, entry, halo, above, below),
+        "v" * 12,
+        (STATE, THIN, BLOCK, RIMS, HALOS),
+        "vavvv",
+        (GROUPED, CYCLE, RIM, ((MEAN_ROWS, 128), F32)),
+        (1,),
     )
     recv = exchange(send)
-    above, below = rims(last_row, first_row)
-    (fresh,) = call(parents_kernel, "parents", (state,) + physics, "vvss", (STATE,), ())
+    (fresh,) = call(
+        parents_kernel,
+        "parents",
+        (state,) + physics + (edge_rows, halos),
+        "vvssvv",
+        (STATE,),
+        "v",
+        (),
+    )
     (state,) = call(
         fourth_kernel,
         "finish",
-        (recv, state, fresh, diffusion, above, below, place, entry),
-        "v" * 8,
+        (recv, state, fresh, place, entry),
+        "v" * 5,
         (STATE,),
+        "v",
         (),
     )
     return lax.cond(flag[0, 127] > 0.5, lambda s, *a: dense_plan(*a), lambda s, *a: s, state, *inputs)

time: 75.4 us -> 72.8 us (0.966)
  waiting for transfers between devices: 24 us -> 20.6 us
  starting transfers between devices: 34.3 us -> 35.8 us
  Pallas kernels: 14.3 us -> 13.4 us
    all_to_all x3, waiting for transfers between devices: 21.1 us -> 16.4 us  [exchange(): return lax.all_to_all(blocks, ('grp', 'gx'), 0, 0, tiled=True)]
    all_to_all x3, starting transfers between devices: 23.3 us -> 24.8 us  [exchange(): return lax.all_to_all(blocks, ('grp', 'gx'), 0, 0, tiled=True)]
    ppermute x2, waiting for transfers between devices: 2.94 us -> 4.26 us  [rims(): below = lax.ppermute(first_row, 'grp', [(1, 0), (2, 1)])]
    pallas_call x7, Pallas kernels: 14.3 us -> 13.4 us  [call(): pl.pallas_call(kernel, name=name, in_specs=[pl.BlockSpec(memory_space=spa...]
  transfers between devices with their start and end apart: 7 -> 7, of which waited for: 5 -> 5; matrix products, arithmetic and copies ran while one was open for 1% -> 1% of each run, Pallas kernels for 5% -> 6%
where the time goes in v4:
time: 72.8 us; the launch traced here: 72.4 us
  starting transfers between devices  35.8 us (49%)
  waiting for transfers between devices  20.6 us (28%)
  Pallas kernels  13.4 us (18%)
  local copies, waits for them, and re-layouts  1.42 us (2%)
  between operations  0.94 us (1%)
    all_to_all x3, starting transfers between devices, exchange(): return lax.all_to_all(blocks, ('grp', 'gx'), 0, 0, tiled=True)  24.8 us
    all_to_all x3, waiting for transfers between devices, exchange(): return lax.all_to_all(blocks, ('grp', 'gx'), 0, 0, tiled=True)  16.4 us
    pallas_call x7, Pallas kernels, call(): pl.pallas_call(kernel, name=name, in_specs=[pl.BlockSpec(memory_space=spa...  13.4 us
    ppermute x2, starting transfers between devices, rims(): above = lax.ppermute(last_row, 'grp', [(0, 1), (1, 2)])  7.09 us
    ppermute x2, waiting for transfers between devices, rims(): below = lax.ppermute(first_row, 'grp', [(1, 0), (2, 1)])  4.26 us
    ppermute x2, starting transfers between devices, rims(): below = lax.ppermute(first_row, 'grp', [(1, 0), (2, 1)])  3.84 us
  transfers between devices with their start and end apart: 7, of which 5 were waited for; matrix products, arithmetic and copies ran while one was open for 1% of the time, Pallas kernels for 6%

profile of v4, /device:TPU:1, one launch (start us, length us, event | category | flops | bytes accessed | tf_op | source)
XLA Modules:
  0.0 72.4 jit_solution(4834608197688427003)
XLA Ops:
  0.0 0.0 copy-start.2
  0.0 0.0 copy-start.3
  0.0 0.0 copy-start.14
  0.0 0.0 copy-start.25
  0.0 0.0 copy-start.28
  0.0 0.0 copy-start.15
  0.0 0.0 copy-start.17
  0.1 3.9 %first_cells.1 = (f32[1024,128]{1,0:T(8,128)}, s32[32,128]{1,0:T(8,128)S(1)}, f32[40,128]{1,0:T(8,128)S(1)}, f32[40,128]{1,0:T(8,128)S(1)}) custom-call(f32[40,16,128]{2,1,0:T(8,128)} %x_ref.3, s32[3,32,288]{2,1,0:T(8,128)} %bitcast.180, s32[3,32,288]{2,1,0:T(8,128)} %bitcast.183), custom_call_target="tpu_custom_call" | custom-call | flops 1000000 | bytes 4000000 | tf_op jit(solution)/shard_map/first_cells/pallas_call | solution.py:959
  4.0 0.0 copy-start
  4.0 0.0 copy-start.4
  4.0 11.5 %all-to-all-start.4 = ((f32[128,8,128]{2,1,0:T(8,128)}), f32[128,8,128]{2,1,0:T(8,128)S(1)}, u32[]{:S(2)}, u32[]{:S(2)}) async-start(f32[128,8,128]{2,1,0:T(8,128)} %bitcast.58), calls=%async_computation.4 | async-start | bytes 1048576 | tf_op jit(solution)/shard_map/all_to_all | solution.py:997
  15.5 3.5 %collective-permute-start.20 = (f32[40,128]{1,0:T(8,128)S(1)}, f32[40,128]{1,0:T(8,128)S(1)}, u32[]{:S(2)}, u32[]{:S(2)}) collective-permute-start(f32[40,128]{1,0:T(8,128)S(1)} %get-tuple-element.159.last_ref), channel_id=1, source_target_pairs={{0,32},{32,64},{1,33},{33,65},{2,34},{34,66},{3,35},{35,67},{4,36}... | collective-permute-start | bytes 61448 | tf_op jit(solution)/shard_map/ppermute | solution.py:1001
  19.1 1.9 %collective-permute-start.21 = (f32[40,128]{1,0:T(8,128)S(1)}, f32[40,128]{1,0:T(8,128)S(1)}, u32[]{:S(2)}, u32[]{:S(2)}) collective-permute-start(f32[40,128]{1,0:T(8,128)S(1)} %get-tuple-element.160.first_ref), channel_id=1, source_target_pairs={{32,0},{64,32},{33,1},{65,33},{34,2},{66,34},{35,3},{67,35},{36,4}... | collective-permute-start | bytes 61448 | tf_op jit(solution)/shard_map/ppermute | solution.py:1002
  21.0 2.8 %tables.1 = (f32[40,16,128]{2,1,0:T(8,128)S(1)}, s32[8,128]{1,0:T(8,128)S(1)}, f32[8,128]{1,0:T(8,128)S(1)}, bf16[384,384]{1,0:T(8,128)(2,1)S(1)}, bf16[256,128]...) custom-call(f32[40,16,128]{2,1,0:T(8,128)} %x_ref.3, ...), custom_call_target="tpu_custom_call" | custom-call | flops 1000000 | bytes 4000000 | tf_op jit(solution)/shard_map/tables/pallas_call | solution.py:959
  23.8 0.0 collective-permute-done.20.above_ref
  23.8 1.0 %collective-permute-done.21.below_ref = f32[40,128]{1,0:T(8,128)S(1)} collective-permute-done((f32[40,128]{1,0:T(8,128)S(1)}, f32[40,128]{1,0:T(8,128)S(1)}, u32[]{:S(2)}, u32[]{:S(2)}) %collective-permute-start.21) | collective-permute-done | bytes 20512 | tf_op jit(solution)/shard_map/ppermute | solution.py:1002
  24.9 4.1 %all-to-all-done.4 = f32[128,8,128]{2,1,0:T(8,128)S(1)} async-done(((f32[128,8,128]{2,1,0:T(8,128)}), f32[128,8,128]{2,1,0:T(8,128)S(1)}, u32[]{:S(2)}, u32[]{:S(2)}) %all-to-all-start.4) | async-done | bytes 524320 | tf_op jit(solution)/shard_map/all_to_all | solution.py:997
  29.0 3.3 %substep_one.1 = (f32[40,16,128]{2,1,0:T(8,128)S(1)}, f32[1024,128]{1,0:T(8,128)}, f32[40,128]{1,0:T(8,128)S(1)}, f32[40,128]{1,0:T(8,128)S(1)}) custom-call(f32[1024,128]{1,0:T(8,128)S(1)} %bitcast.158, f32[40,16,128]{2,1,0:T(8,128)S(1)} %get-tuple-element.158.fresh_ref, f32[16,128]{1,0:T(8,128)} %diff_ref.9, ...), custom_call_target="tpu_custom_call" | custom-call | flops 1000000 | bytes 4000000 | tf_op jit(solution)/shard_map/substep_one/pallas_call | solution.py:959
  32.3 5.6 %all-to-all-start.5 = ((f32[128,8,128]{2,1,0:T(8,128)}), f32[128,8,128]{2,1,0:T(8,128)S(1)}, u32[]{:S(2)}, u32[]{:S(2)}) async-start(f32[128,8,128]{2,1,0:T(8,128)} %bitcast.61), calls=%async_computation.5 | async-start | bytes 1048576 | tf_op jit(solution)/shard_map/all_to_all | solution.py:997
  37.9 3.5 %collective-permute-start.22 = (f32[40,128]{1,0:T(8,128)S(1)}, f32[40,128]{1,0:T(8,128)S(1)}, u32[]{:S(2)}, u32[]{:S(2)}) collective-permute-start(f32[40,128]{1,0:T(8,128)S(1)} %get-tuple-element.174), channel_id=1, source_target_pairs={{0,32},{32,64},{1,33},{33,65},{2,34},{34,66},{3,35},{35,67},{4,36}... | collective-permute-start | bytes 61448 | tf_op jit(solution)/shard_map/ppermute | solution.py:1001
  41.4 1.9 %collective-permute-start.23 = (f32[40,128]{1,0:T(8,128)S(1)}, f32[40,128]{1,0:T(8,128)S(1)}, u32[]{:S(2)}, u32[]{:S(2)}) collective-permute-start(f32[40,128]{1,0:T(8,128)S(1)} %get-tuple-element.175), channel_id=1, source_target_pairs={{32,0},{64,32},{33,1},{65,33},{34,2},{66,34},{35,3},{67,35},{36,4}... | collective-permute-start | bytes 61448 | tf_op jit(solution)/shard_map/ppermute | solution.py:1002
  43.3 0.0 copy-done.2
  43.3 0.0 copy-done.3
  43.4 0.0 copy-done.14
  43.4 0.0 copy-done.25
  43.4 0.0 copy-done.28
  43.4 0.0 copy-done.15
  43.4 0.0 copy-done.17
  43.4 0.6 hits.1
  44.0 0.0 collective-permute-done.22.above_ref
  44.0 3.2 %collective-permute-done.23.below_ref = f32[40,128]{1,0:T(8,128)S(1)} collective-permute-done((f32[40,128]{1,0:T(8,128)S(1)}, f32[40,128]{1,0:T(8,128)S(1)}, u32[]{:S(2)}, u32[]{:S(2)}) %collective-permute-start.23) | collective-permute-done | bytes 20512 | tf_op jit(solution)/shard_map/ppermute | solution.py:1002
  47.2 4.1 %all-to-all-done.5 = f32[128,8,128]{2,1,0:T(8,128)S(1)} async-done(((f32[128,8,128]{2,1,0:T(8,128)}), f32[128,8,128]{2,1,0:T(8,128)S(1)}, u32[]{:S(2)}, u32[]{:S(2)}) %all-to-all-start.5) | async-done | bytes 524320 | tf_op jit(solution)/shard_map/all_to_all | solution.py:997
  51.3 0.8 %substep_two.1 = (f32[40,16,128]{2,1,0:T(8,128)S(1)}, f32[512,128]{1,0:T(8,128)}, f32[8,128]{1,0:T(8,128)S(1)}, f32[2,40,128]{2,1,0:T(8,128)S(1)}, f32[48,128]{1,0:T(8,128)S(1)}) custom-call(f32[1024,128]{1,0:T(8,128)S(1)} %bitcast.157, f32[40,16,128]{2,1,0:T(8,128)S(1)} %get-tuple-element.168.x_ref, f32[40,16,128]{2,1,0:T(8,128)S(1)} %get-tuple-element.169.fresh_ref, ...), custom_call_target="tpu_custom_call" | custom-call | flops 1000000 | bytes 4000000 | tf_op jit(solution)/shard_map/substep_two/pallas_call | solution.py:959
  52.1 7.8 %all-to-all-start.6 = ((f32[128,4,128]{2,1,0:T(4,128)}), f32[128,4,128]{2,1,0:T(4,128)S(1)}, u32[]{:S(2)}, u32[]{:S(2)}) async-start(f32[128,4,128]{2,1,0:T(4,128)} %bitcast.64), calls=%async_computation.6 | async-start | bytes 524288 | tf_op jit(solution)/shard_map/all_to_all | solution.py:997
  59.9 0.6 slice.381
  61.2 1.3 %parents.1.fresh_ref = f32[40,16,128]{2,1,0:T(8,128)S(1)} custom-call(f32[40,16,128]{2,1,0:T(8,128)S(1)} %get-tuple-element.178.x_ref, f32[16,128]{1,0:T(8,128)S(1)} %copy-done.14, f32[16]{0:T(128)S(1)} %copy-done.25, f32[10]{0:T(128)S(1)} %copy-done.28, f32[2,40,128]{2,1,0:T(8,128)S(1)} %get-tuple-element.179.rims_ref, ...), custom_call_target="tpu_custom_call" | custom-call | flops 1000000 | bytes 4000000 | tf_op jit(solution)/shard_map/parents/pallas_call | solution.py:959
  62.5 8.1 %all-to-all-done.6 = f32[128,4,128]{2,1,0:T(4,128)S(1)} async-done(((f32[128,4,128]{2,1,0:T(4,128)}), f32[128,4,128]{2,1,0:T(4,128)S(1)}, u32[]{:S(2)}, u32[]{:S(2)}) %all-to-all-start.6) | async-done | bytes 262176 | tf_op jit(solution)/shard_map/all_to_all | solution.py:997
  70.6 0.7 finish.1
  71.3 0.0 copy-done
  71.4 0.0 copy-done.4
  71.4 0.3 conditional.1
  71.6 0.0 copy-start.13
  71.7 0.7 copy-done.13
Async XLA Ops:
  0.0 43.3 %copy-start.2 = (s32[32,3,288]{2,0,1:T(8,128)S(1)}, s32[32,3,288]{2,0,1:T(8,128)}, u32[]{:S(2)}) copy-start(s32[32,3,288]{2,0,1:T(8,128)} %param.33) | copy-start | bytes 331780
  0.0 43.3 %copy-start.3 = (s32[32,3,288]{2,0,1:T(8,128)S(1)}, s32[32,3,288]{2,0,1:T(8,128)}, u32[]{:S(2)}) copy-start(s32[32,3,288]{2,0,1:T(8,128)} %param.34) | copy-start | bytes 331780
  0.0 43.4 %copy-start.14 = (f32[16,128]{1,0:T(8,128)S(1)}, f32[16,128]{1,0:T(8,128)}, u32[]{:S(2)}) copy-start(f32[16,128]{1,0:T(8,128)} %diff_ref.9) | copy-start | bytes 24580
  0.0 43.4 %copy-start.25 = (f32[16]{0:T(128)S(1)}, f32[16]{0:T(128)}, u32[]{:S(2)}) copy-start(f32[16]{0:T(128)} %cor_ref.5) | copy-start | bytes 196
  0.0 43.4 %copy-start.28 = (f32[10]{0:T(128)S(1)}, f32[10]{0:T(128)}, u32[]{:S(2)}) copy-start(f32[10]{0:T(128)} %mix_ref.5) | copy-start | bytes 124
  0.0 43.4 %copy-start.15 = (s32[32,128]{1,0:T(8,128)S(1)}, s32[32,128]{1,0:T(8,128)}, u32[]{:S(2)}) copy-start(s32[32,128]{1,0:T(8,128)} %fb_owner_ref.3) | copy-start | bytes 49156
  0.0 43.4 %copy-start.17 = (s32[32,128]{1,0:T(8,128)S(1)}, s32[32,128]{1,0:T(8,128)}, u32[]{:S(2)}) copy-start(s32[32,128]{1,0:T(8,128)} %fb_cell_ref.3) | copy-start | bytes 49156
  4.0 67.4 %copy-start = (f32[40,16,128]{2,1,0:T(8,128)S(1)}, f32[40,16,128]{2,1,0:T(8,128)}, u32[]{:S(2)}) copy-start(f32[40,16,128]{2,1,0:T(8,128)} %x_ref.3) | copy-start | bytes 983044
  4.0 67.4 %copy-start.4 = (f32[32,3,288]{2,0,1:T(8,128)S(1)}, f32[32,3,288]{2,0,1:T(8,128)}, u32[]{:S(2)}) copy-start(f32[32,3,288]{2,0,1:T(8,128)} %param.35) | copy-start | bytes 331780
  4.0 25.0 %all-to-all-start.4 = ((f32[128,8,128]{2,1,0:T(8,128)}), f32[128,8,128]{2,1,0:T(8,128)S(1)}, u32[]{:S(2)}, u32[]{:S(2)}) async-start(f32[128,8,128]{2,1,0:T(8,128)} %bitcast.58), calls=%async_computation.4 | async-start | bytes 1048576 | tf_op jit(solution)/shard_map/all_to_all | solution.py:997
  15.5 8.3 %collective-permute-start.20 = (f32[40,128]{1,0:T(8,128)S(1)}, f32[40,128]{1,0:T(8,128)S(1)}, u32[]{:S(2)}, u32[]{:S(2)}) collective-permute-start(f32[40,128]{1,0:T(8,128)S(1)} %get-tuple-element.159.last_ref), channel_id=1, source_target_pairs={{0,32},{32,64},{1,33},{33,65},{2,34},{34,66},{3,35},{35,67},{4,36}... | collective-permute-start | bytes 61448 | tf_op jit(solution)/shard_map/ppermute | solution.py:1001
  19.1 5.8 %collective-permute-start.21 = (f32[40,128]{1,0:T(8,128)S(1)}, f32[40,128]{1,0:T(8,128)S(1)}, u32[]{:S(2)}, u32[]{:S(2)}) collective-permute-start(f32[40,128]{1,0:T(8,128)S(1)} %get-tuple-element.160.first_ref), channel_id=1, source_target_pairs={{32,0},{64,32},{33,1},{65,33},{34,2},{66,34},{35,3},{67,35},{36,4}... | collective-permute-start | bytes 61448 | tf_op jit(solution)/shard_map/ppermute | solution.py:1002
  32.3 19.0 %all-to-all-start.5 = ((f32[128,8,128]{2,1,0:T(8,128)}), f32[128,8,128]{2,1,0:T(8,128)S(1)}, u32[]{:S(2)}, u32[]{:S(2)}) async-start(f32[128,8,128]{2,1,0:T(8,128)} %bitcast.61), calls=%async_computation.5 | async-start | bytes 1048576 | tf_op jit(solution)/shard_map/all_to_all | solution.py:997
  37.9 6.1 %collective-permute-start.22 = (f32[40,128]{1,0:T(8,128)S(1)}, f32[40,128]{1,0:T(8,128)S(1)}, u32[]{:S(2)}, u32[]{:S(2)}) collective-permute-start(f32[40,128]{1,0:T(8,128)S(1)} %get-tuple-element.174), channel_id=1, source_target_pairs={{0,32},{32,64},{1,33},{33,65},{2,34},{34,66},{3,35},{35,67},{4,36}... | collective-permute-start | bytes 61448 | tf_op jit(solution)/shard_map/ppermute | solution.py:1001
  41.4 5.8 %collective-permute-start.23 = (f32[40,128]{1,0:T(8,128)S(1)}, f32[40,128]{1,0:T(8,128)S(1)}, u32[]{:S(2)}, u32[]{:S(2)}) collective-permute-start(f32[40,128]{1,0:T(8,128)S(1)} %get-tuple-element.175), channel_id=1, source_target_pairs={{32,0},{64,32},{33,1},{65,33},{34,2},{66,34},{35,3},{67,35},{36,4}... | collective-permute-start | bytes 61448 | tf_op jit(solution)/shard_map/ppermute | solution.py:1002
  52.1 18.5 %all-to-all-start.6 = ((f32[128,4,128]{2,1,0:T(4,128)}), f32[128,4,128]{2,1,0:T(4,128)S(1)}, u32[]{:S(2)}, u32[]{:S(2)}) async-start(f32[128,4,128]{2,1,0:T(4,128)} %bitcast.64), calls=%async_computation.6 | async-start | bytes 524288 | tf_op jit(solution)/shard_map/all_to_all | solution.py:997
  71.6 0.7 %copy-start.13 = (f32[40,16,128]{2,1,0:T(8,128)}, f32[40,16,128]{2,1,0:T(8,128)S(1)}, u32[]{:S(2)}) copy-start(f32[40,16,128]{2,1,0:T(8,128)S(1)} %get-tuple-element.335) | copy-start | bytes 983044

commit v5 on v4

--- a/solution.py
+++ b/solution.py
@@ -15,7 +15,7 @@
 PARENTS = 96
 DEVICES = 128
 PERIM = 288
-TILES = 9
+TILES = 7
 SLOTS = 25
 HITS = 8
 EDGE = 40
@@ -217,10 +217,30 @@
         for j in range(slots):
             picked = [jnp.where(m == float(j), v, 0.0) for m, v in zip(marks, vals)]
             while len(picked) > 1:
-                picked = [sum(picked[k : k + 2]) for k in range(0, len(picked), 2)]
+                picked = [sum(picked[k + 1 : k + 2], picked[k]) for k in range(0, len(picked), 2)]
             table = jnp.where(slot_of == j, jnp.sum(picked[0], axis=1, keepdims=True), table)
         parts.append(table)
     return jnp.concatenate(parts, axis=0), total
+
+
+def swap_segments(tiles):
+    segment = iota((8, 128), 1) // SLOTS
+    moved = {}
+    for shift in range(1 - FG, FG):
+        diagonal = None
+        for s in range(FG):
+            if 0 <= s + shift < FG:
+                tile = tiles[s + shift]
+                diagonal = tile if diagonal is None else jnp.where(segment == s, tile, diagonal)
+        by = (SLOTS * shift) % 128
+        moved[shift] = diagonal if by == 0 else pltpu.roll(diagonal, by, 1)
+    results = []
+    for s in range(FG):
+        result = moved[-s]
+        for a in range(1, FG):
+            result = jnp.where(segment == a, moved[a - s], result)
+        results.append(result)
+    return results
 
 
 def send_cells(rows_s, table_ref, blocks_s, send_ref, sems):
@@ -241,13 +261,9 @@
             here = row == r
             for k in range(FG):
                 cells[k] = jnp.where(here, take(rows_s[r, 8 * k : 8 * k + 8, :], col), cells[k])
+        blocks = swap_segments(cells)
         for q in members:
-            block = jnp.zeros((8, 128), F32)
-            for k in range(FG):
-                shift = (SLOTS * (k - (q - 5 * g))) % 128
-                moved = cells[k] if shift == 0 else pltpu.roll(cells[k], shift, 1)
-                block = jnp.where(group_of == k, moved, block)
-            blocks_s[8 * q : 8 * q + 8, :] = block
+            blocks_s[8 * q : 8 * q + 8, :] = blocks[q - 5 * g]
         span = pl.ds(8 * members[0], 8 * len(members))
         rows = pl.ds(SENT + 8 * members[0], 8 * len(members))
         copies.append(pltpu.make_async_copy(blocks_s.at[span, :], send_ref.at[rows, :], sems.at[g]))
@@ -408,20 +424,12 @@
 
 
 def regroup(recv_ref, group_s):
-    member_of = iota((8, 128), 1) // SLOTS
-
     def body(g):
-        tiles = [jnp.zeros((8, 128), F32) for _ in range(FG)]
-        for i in range(5):
-            block = recv_ref[rows_of(g * 5 + i), :]
-            for k in range(FG):
-                shift = (SLOTS * (i - k)) % 128
-                moved = block if shift == 0 else pltpu.roll(block, shift, 1)
-                tiles[k] = jnp.where(member_of == i, moved, tiles[k])
+        tiles = swap_segments([recv_ref[rows_of(g * 5 + i), :] for i in range(5)])
         for k in range(FG):
             group_s[g, 8 * k : 8 * k + 8, :] = tiles[k]
 
-    chunks(PGROUPS, 2, body)
+    chunks(PGROUPS, 4, body)
 
 
 def regroup_hits(recv_ref, group_s):
@@ -463,15 +471,6 @@
         weight_s[2 * k : 2 * k + 1, :] = own[:, 0:128]
         weight_s[2 * k + 1 : 2 * k + 2, :] = own[:, 128:256]
         weight_s[6:7, 32 * k : 32 * k + 32] = own[:, 256:288]
-
-
-def pack_tiles(rows):
-    lane = iota((1, 128), 1)
-    last = rows[2]
-    for k in (1, 2):
-        moved = pltpu.roll(jnp.broadcast_to(rows[3 * k + 2], (8, 128)), 32 * k, 1)[0:1]
-        last = jnp.where(lane >= 32 * k, moved, last)
-    return [rows[3 * k + span] for k in range(3) for span in range(2)] + [last]
 
 
 def prescribe(out_ref, cycle_s, column_s, gx):
@@ -612,12 +611,12 @@
 
 
 def load_terms(owner_ref, cell_ref, gid_s):
+    gid_s[6] = jnp.full((GX, 128), -1, jnp.int32)
     for k in range(3):
         gid = owner_ref[k] * 2048 + cell_ref[k]
-        gid_s[3 * k] = gid[:, 0:128]
-        gid_s[3 * k + 1] = gid[:, 128:256]
-        gid_s[3 * k + 2] = jnp.full((GX, 128), -1, jnp.int32)
-        gid_s[3 * k + 2, :, 0:32] = gid[:, 256:288]
+        gid_s[2 * k] = gid[:, 0:128]
+        gid_s[2 * k + 1] = gid[:, 128:256]
+        gid_s[6, :, 32 * k : 32 * k + 32] = gid[:, 256:288]
 
 
 def flag_block(over):
@@ -743,7 +742,7 @@
             slot = jnp.minimum(slot.astype(jnp.int32), SLOTS - 1)
             group = jnp.right_shift(owners[t] * 205, 10)
             codes.append(group * 128 + (owners[t] - 5 * group) * SLOTS + slot)
-        for t, code in enumerate(pack_tiles(codes)):
+        for t, code in enumerate(codes):
             codes_ref[t : t + 1, :] = code
 
         hot = jnp.where(hot, 1.0, 0.0).astype(jnp.bfloat16)
@@ -855,13 +854,13 @@
         wide = [jnp.broadcast_to(t.astype(F32), (8, 128)) for t in terms]
 
         def match(q, from_block):
-            column = pltpu.roll(turned_s[...], lax.rem(128 - q, 128), 1)[:, 0:1]
+            index = jnp.full((8, 128), q, jnp.int32)
             for s in range(16):
-                part = jnp.broadcast_to(column[8 * s : 8 * s + 8, :], (8, 128))
+                part = take(turned_s[8 * s : 8 * s + 8, :], index)
                 from_block = [jnp.where(part == w, q, f) for w, f in zip(wide, from_block)]
             return from_block
 
-        none = [jnp.full((8, 128), -1, jnp.int32) for _ in range(TILES)]
+        none = [jnp.full((8, 128), -1, jnp.int32) for _ in terms]
         from_block = lax.fori_loop(0, GX, match, none)
         sources = [jnp.max(f, axis=0, keepdims=True) for f in from_block]
         hots = [iota((GX, 128), 0) == s for s in sources]
@@ -873,7 +872,7 @@
             code = (PGROUPS + jnp.right_shift(sources[t], 4)) * 128
             code = code + jnp.bitwise_and(sources[t], 15) * HITS + slot
             codes.append(jnp.where(sources[t] >= 0, code, -1))
-        for t, code in enumerate(pack_tiles(codes)):
+        for t, code in enumerate(codes):
             plain = plain_ref[t : t + 1, :]
             codes_ref[t : t + 1, :] = jnp.where(code >= 0, code, plain)
 
@@ -1069,16 +1068,12 @@
         "v",
         (),
     )
-    (state,) = call(
-        fourth_kernel,
-        "finish",
-        (recv, state, fresh, place, entry),
-        "v" * 5,
-        (STATE,),
-        "v",
-        (),
-    )
-    return lax.cond(flag[0, 127] > 0.5, lambda s, *a: dense_plan(*a), lambda s, *a: s, state, *inputs)
+
+    def finish(received, *_):
+        return call(fourth_kernel, "finish", received, "v" * 5, (STATE,), "v", ())[0]
+
+    received = (recv, state, fresh, place, entry)
+    return lax.cond(flag[0, 127] > 0.5, lambda _, *a: dense_plan(*a), finish, received, *inputs)
 
 
 def solution(mesh):

time: 72.8 us -> 70.7 us (0.971)
  starting transfers between devices: 35.8 us -> 34.2 us
    all_to_all x3, starting transfers between devices: 24.8 us -> 23.3 us  [exchange(): return lax.all_to_all(blocks, ('grp', 'gx'), 0, 0, tiled=True)]
where the time goes in v5:
time: 70.7 us; the launch traced here: 70.3 us
  starting transfers between devices  34.2 us (48%)
  waiting for transfers between devices  20.8 us (29%)
  Pallas kernels  13.6 us (19%)
  between operations  0.9 us (1%)
    all_to_all x3, starting transfers between devices, exchange(): return lax.all_to_all(blocks, ('grp', 'gx'), 0, 0, tiled=True)  23.3 us
    all_to_all x3, waiting for transfers between devices, exchange(): return lax.all_to_all(blocks, ('grp', 'gx'), 0, 0, tiled=True)  16.6 us
    pallas_call x7, Pallas kernels, call(): pl.pallas_call(kernel, name=name, in_specs=[pl.BlockSpec(memory_space=spa...  13.6 us
    ppermute x2, starting transfers between devices, rims(): above = lax.ppermute(last_row, 'grp', [(0, 1), (1, 2)])  7.09 us
    ppermute x2, waiting for transfers between devices, rims(): below = lax.ppermute(first_row, 'grp', [(1, 0), (2, 1)])  4.26 us
    ppermute x2, starting transfers between devices, rims(): below = lax.ppermute(first_row, 'grp', [(1, 0), (2, 1)])  3.84 us
  transfers between devices with their start and end apart: 7, of which 5 were waited for; matrix products, arithmetic and copies ran while one was open for 1% of the time, Pallas kernels for 6%

profile of v5, /device:TPU:1, one launch (start us, length us, event | category | flops | bytes accessed | tf_op | source)
XLA Modules:
  0.0 70.3 jit_solution(16673830517054415493)
XLA Ops:
  0.0 0.0 copy-start.2
  0.0 0.0 copy-start.3
  0.0 0.0 copy-start
  0.0 0.0 copy-start.4
  0.0 0.0 copy-start.13
  0.0 0.0 copy-start.24
  0.0 0.0 copy-start.27
  0.1 0.0 copy-start.14
  0.1 0.0 copy-start.16
  0.1 3.8 %first_cells.1 = (f32[1024,128]{1,0:T(8,128)}, s32[32,128]{1,0:T(8,128)S(1)}, f32[40,128]{1,0:T(8,128)S(1)}, f32[40,128]{1,0:T(8,128)S(1)}) custom-call(f32[40,16,128]{2,1,0:T(8,128)} %x_ref.3, s32[3,32,288]{2,1,0:T(8,128)} %bitcast.179, s32[3,32,288]{2,1,0:T(8,128)} %bitcast.182), custom_call_target="tpu_custom_call" | custom-call | flops 1000000 | bytes 4000000 | tf_op jit(solution)/shard_map/first_cells/pallas_call | solution.py:958
  3.9 11.5 %all-to-all-start.4 = ((f32[128,8,128]{2,1,0:T(8,128)}), f32[128,8,128]{2,1,0:T(8,128)S(1)}, u32[]{:S(2)}, u32[]{:S(2)}) async-start(f32[128,8,128]{2,1,0:T(8,128)} %bitcast.59), calls=%async_computation.4 | async-start | bytes 1048576 | tf_op jit(solution)/shard_map/all_to_all | solution.py:996
  15.4 3.5 %collective-permute-start.20 = (f32[40,128]{1,0:T(8,128)S(1)}, f32[40,128]{1,0:T(8,128)S(1)}, u32[]{:S(2)}, u32[]{:S(2)}) collective-permute-start(f32[40,128]{1,0:T(8,128)S(1)} %get-tuple-element.174.last_ref), channel_id=1, source_target_pairs={{0,32},{32,64},{1,33},{33,65},{2,34},{34,66},{3,35},{35,67},{4,36}... | collective-permute-start | bytes 61448 | tf_op jit(solution)/shard_map/ppermute | solution.py:1000
  18.9 1.9 %collective-permute-start.21 = (f32[40,128]{1,0:T(8,128)S(1)}, f32[40,128]{1,0:T(8,128)S(1)}, u32[]{:S(2)}, u32[]{:S(2)}) collective-permute-start(f32[40,128]{1,0:T(8,128)S(1)} %get-tuple-element.175.first_ref), channel_id=1, source_target_pairs={{32,0},{64,32},{33,1},{65,33},{34,2},{66,34},{35,3},{67,35},{36,4}... | collective-permute-start | bytes 61448 | tf_op jit(solution)/shard_map/ppermute | solution.py:1001
  20.8 2.8 %tables.1 = (f32[40,16,128]{2,1,0:T(8,128)S(1)}, s32[8,128]{1,0:T(8,128)S(1)}, f32[8,128]{1,0:T(8,128)S(1)}, bf16[384,384]{1,0:T(8,128)(2,1)S(1)}, bf16[256,128]...) custom-call(f32[40,16,128]{2,1,0:T(8,128)} %x_ref.3, ...), custom_call_target="tpu_custom_call" | custom-call | flops 1000000 | bytes 4000000 | tf_op jit(solution)/shard_map/tables/pallas_call | solution.py:958
  23.7 0.0 collective-permute-done.20.above_ref
  23.7 1.0 %collective-permute-done.21.below_ref = f32[40,128]{1,0:T(8,128)S(1)} collective-permute-done((f32[40,128]{1,0:T(8,128)S(1)}, f32[40,128]{1,0:T(8,128)S(1)}, u32[]{:S(2)}, u32[]{:S(2)}) %collective-permute-start.21) | collective-permute-done | bytes 20512 | tf_op jit(solution)/shard_map/ppermute | solution.py:1001
  24.7 4.1 %all-to-all-done.4 = f32[128,8,128]{2,1,0:T(8,128)S(1)} async-done(((f32[128,8,128]{2,1,0:T(8,128)}), f32[128,8,128]{2,1,0:T(8,128)S(1)}, u32[]{:S(2)}, u32[]{:S(2)}) %all-to-all-start.4) | async-done | bytes 524320 | tf_op jit(solution)/shard_map/all_to_all | solution.py:996
  28.8 3.2 %substep_one.1 = (f32[40,16,128]{2,1,0:T(8,128)S(1)}, f32[1024,128]{1,0:T(8,128)}, f32[40,128]{1,0:T(8,128)S(1)}, f32[40,128]{1,0:T(8,128)S(1)}) custom-call(f32[1024,128]{1,0:T(8,128)S(1)} %bitcast.158, f32[40,16,128]{2,1,0:T(8,128)S(1)} %get-tuple-element.173.fresh_ref, f32[16,128]{1,0:T(8,128)} %diff_ref.9, ...), custom_call_target="tpu_custom_call" | custom-call | flops 1000000 | bytes 4000000 | tf_op jit(solution)/shard_map/substep_one/pallas_call | solution.py:958
  32.0 5.1 %all-to-all-start.5 = ((f32[128,8,128]{2,1,0:T(8,128)}), f32[128,8,128]{2,1,0:T(8,128)S(1)}, u32[]{:S(2)}, u32[]{:S(2)}) async-start(f32[128,8,128]{2,1,0:T(8,128)} %bitcast.62), calls=%async_computation.5 | async-start | bytes 1048576 | tf_op jit(solution)/shard_map/all_to_all | solution.py:996
  37.1 3.5 %collective-permute-start.22 = (f32[40,128]{1,0:T(8,128)S(1)}, f32[40,128]{1,0:T(8,128)S(1)}, u32[]{:S(2)}, u32[]{:S(2)}) collective-permute-start(f32[40,128]{1,0:T(8,128)S(1)} %get-tuple-element.189), channel_id=1, source_target_pairs={{0,32},{32,64},{1,33},{33,65},{2,34},{34,66},{3,35},{35,67},{4,36}... | collective-permute-start | bytes 61448 | tf_op jit(solution)/shard_map/ppermute | solution.py:1000
  40.7 1.9 %collective-permute-start.23 = (f32[40,128]{1,0:T(8,128)S(1)}, f32[40,128]{1,0:T(8,128)S(1)}, u32[]{:S(2)}, u32[]{:S(2)}) collective-permute-start(f32[40,128]{1,0:T(8,128)S(1)} %get-tuple-element.190), channel_id=1, source_target_pairs={{32,0},{64,32},{33,1},{65,33},{34,2},{66,34},{35,3},{67,35},{36,4}... | collective-permute-start | bytes 61448 | tf_op jit(solution)/shard_map/ppermute | solution.py:1001
  42.6 0.0 copy-done.2
  42.6 0.0 copy-done.3
  42.6 0.0 copy-done.13
  42.6 0.0 copy-done.24
  42.6 0.0 copy-done.27
  42.7 0.0 copy-done.14
  42.7 0.0 copy-done.16
  42.7 0.6 hits.1
  43.2 0.0 collective-permute-done.22.above_ref
  43.3 3.2 %collective-permute-done.23.below_ref = f32[40,128]{1,0:T(8,128)S(1)} collective-permute-done((f32[40,128]{1,0:T(8,128)S(1)}, f32[40,128]{1,0:T(8,128)S(1)}, u32[]{:S(2)}, u32[]{:S(2)}) %collective-permute-start.23) | collective-permute-done | bytes 20512 | tf_op jit(solution)/shard_map/ppermute | solution.py:1001
  46.5 4.1 %all-to-all-done.5 = f32[128,8,128]{2,1,0:T(8,128)S(1)} async-done(((f32[128,8,128]{2,1,0:T(8,128)}), f32[128,8,128]{2,1,0:T(8,128)S(1)}, u32[]{:S(2)}, u32[]{:S(2)}) %all-to-all-start.5) | async-done | bytes 524320 | tf_op jit(solution)/shard_map/all_to_all | solution.py:996
  50.6 0.8 %substep_two.1 = (f32[40,16,128]{2,1,0:T(8,128)S(1)}, f32[512,128]{1,0:T(8,128)}, f32[8,128]{1,0:T(8,128)S(1)}, f32[2,40,128]{2,1,0:T(8,128)S(1)}, f32[48,128]{1,0:T(8,128)S(1)}) custom-call(f32[1024,128]{1,0:T(8,128)S(1)} %bitcast.157, f32[40,16,128]{2,1,0:T(8,128)S(1)} %get-tuple-element.183.x_ref, f32[40,16,128]{2,1,0:T(8,128)S(1)} %get-tuple-element.184.fresh_ref, ...), custom_call_target="tpu_custom_call" | custom-call | flops 1000000 | bytes 4000000 | tf_op jit(solution)/shard_map/substep_two/pallas_call | solution.py:958
  51.4 6.7 %all-to-all-start.6 = ((f32[128,4,128]{2,1,0:T(4,128)}), f32[128,4,128]{2,1,0:T(4,128)S(1)}, u32[]{:S(2)}, u32[]{:S(2)}) async-start(f32[128,4,128]{2,1,0:T(4,128)} %bitcast.65), calls=%async_computation.6 | async-start | bytes 524288 | tf_op jit(solution)/shard_map/all_to_all | solution.py:996
  58.1 0.6 slice.381
  59.4 1.1 %parents.1 = f32[40,16,128]{2,1,0:T(8,128)S(1)} custom-call(f32[40,16,128]{2,1,0:T(8,128)S(1)} %get-tuple-element.193.x_ref, f32[16,128]{1,0:T(8,128)S(1)} %copy-done.13, f32[16]{0:T(128)S(1)} %copy-done.24, f32[10]{0:T(128)S(1)} %copy-done.27, f32[2,40,128]{2,1,0:T(8,128)S(1)} %get-tuple-element.194.rims_ref, f32[48,128]{1,0:T(8,128)S(1)} %get-tuple-element.195.halos_ref), custom_call_target="tpu_custom_call" | custom-call | flops 1000000 | bytes 4000000 | tf_op jit(solution)/shard_map/parents/pallas_call | solution.py:958
  60.5 8.4 %all-to-all-done.6 = f32[128,4,128]{2,1,0:T(4,128)S(1)} async-done(((f32[128,4,128]{2,1,0:T(4,128)}), f32[128,4,128]{2,1,0:T(4,128)S(1)}, u32[]{:S(2)}, u32[]{:S(2)}) %all-to-all-start.6) | async-done | bytes 262176 | tf_op jit(solution)/shard_map/all_to_all | solution.py:996
  68.8 0.0 copy-done
  68.8 0.0 copy-done.4
  68.8 1.4 %conditional.1 = (f32[40,16,128]{2,1,0:T(8,128)}) conditional(s32[]{:T(128)} %bitcast.64, (f32[128,4,128]{2,1,0:T(4,128)S(1)}, f32[40,16,128]{2,1,0:T(8,128)S(1)}, f32[40,16,128]{2,1,0:T(8,128)S(1)}, s32[32,128]{1,0:T(8,128)S(1)}, bf16[384,128]{1,0:T(8,128)(2,1)S(1)}) %tuple.44, (f32[16,128]{1,0:T(8,128)S(1)}, f32[40,16,128]{2,1,0:T(8,128)S(1)}, ...), branch_computations={%region_0.0_spmd, %region_1.9_spmd} | conditional | flops 12829852 | bytes 118900464 | solution.py:1076
  68.8 1.4 %finish.1 = f32[40,16,128]{2,1,0:T(8,128)} custom-call(f32[512,128]{1,0:T(8,128)S(1)} %bitcast.192, f32[40,16,128]{2,1,0:T(8,128)S(1)} %get-tuple-element.135.x_ref, f32[40,16,128]{2,1,0:T(8,128)S(1)} %get-tuple-element.136.fresh_ref, s32[32,128]{1,0:T(8,128)S(1)} %get-tuple-element.137.map_ref, bf16[384,128]{1,0:T(8,128)(2,1)S(1)} %get-tuple-element.138.entry_ref), custom_call_target="tpu_custom_call" | custom-call | flops 1000000 | bytes 4000000 | tf_op jit(solution)/shard_map/cond/branch_0_fun/finish/pallas_call | solution.py:958
Async XLA Ops:
  0.0 42.6 %copy-start.2 = (s32[32,3,288]{2,0,1:T(8,128)S(1)}, s32[32,3,288]{2,0,1:T(8,128)}, u32[]{:S(2)}) copy-start(s32[32,3,288]{2,0,1:T(8,128)} %param.33) | copy-start | bytes 331780
  0.0 42.6 %copy-start.3 = (s32[32,3,288]{2,0,1:T(8,128)S(1)}, s32[32,3,288]{2,0,1:T(8,128)}, u32[]{:S(2)}) copy-start(s32[32,3,288]{2,0,1:T(8,128)} %param.34) | copy-start | bytes 331780
  0.0 68.8 %copy-start = (f32[40,16,128]{2,1,0:T(8,128)S(1)}, f32[40,16,128]{2,1,0:T(8,128)}, u32[]{:S(2)}) copy-start(f32[40,16,128]{2,1,0:T(8,128)} %x_ref.3) | copy-start | bytes 983044
  0.0 68.8 %copy-start.4 = (f32[32,3,288]{2,0,1:T(8,128)S(1)}, f32[32,3,288]{2,0,1:T(8,128)}, u32[]{:S(2)}) copy-start(f32[32,3,288]{2,0,1:T(8,128)} %param.35) | copy-start | bytes 331780
  0.0 42.6 %copy-start.13 = (f32[16,128]{1,0:T(8,128)S(1)}, f32[16,128]{1,0:T(8,128)}, u32[]{:S(2)}) copy-start(f32[16,128]{1,0:T(8,128)} %diff_ref.9) | copy-start | bytes 24580
  0.0 42.6 %copy-start.24 = (f32[16]{0:T(128)S(1)}, f32[16]{0:T(128)}, u32[]{:S(2)}) copy-start(f32[16]{0:T(128)} %cor_ref.5) | copy-start | bytes 196
  0.0 42.6 %copy-start.27 = (f32[10]{0:T(128)S(1)}, f32[10]{0:T(128)}, u32[]{:S(2)}) copy-start(f32[10]{0:T(128)} %mix_ref.5) | copy-start | bytes 124
  0.1 42.6 %copy-start.14 = (s32[32,128]{1,0:T(8,128)S(1)}, s32[32,128]{1,0:T(8,128)}, u32[]{:S(2)}) copy-start(s32[32,128]{1,0:T(8,128)} %fb_owner_ref.3) | copy-start | bytes 49156
  0.1 42.6 %copy-start.16 = (s32[32,128]{1,0:T(8,128)S(1)}, s32[32,128]{1,0:T(8,128)}, u32[]{:S(2)}) copy-start(s32[32,128]{1,0:T(8,128)} %fb_cell_ref.3) | copy-start | bytes 49156
  3.9 25.0 %all-to-all-start.4 = ((f32[128,8,128]{2,1,0:T(8,128)}), f32[128,8,128]{2,1,0:T(8,128)S(1)}, u32[]{:S(2)}, u32[]{:S(2)}) async-start(f32[128,8,128]{2,1,0:T(8,128)} %bitcast.59), calls=%async_computation.4 | async-start | bytes 1048576 | tf_op jit(solution)/shard_map/all_to_all | solution.py:996
  15.4 8.3 %collective-permute-start.20 = (f32[40,128]{1,0:T(8,128)S(1)}, f32[40,128]{1,0:T(8,128)S(1)}, u32[]{:S(2)}, u32[]{:S(2)}) collective-permute-start(f32[40,128]{1,0:T(8,128)S(1)} %get-tuple-element.174.last_ref), channel_id=1, source_target_pairs={{0,32},{32,64},{1,33},{33,65},{2,34},{34,66},{3,35},{35,67},{4,36}... | collective-permute-start | bytes 61448 | tf_op jit(solution)/shard_map/ppermute | solution.py:1000
  18.9 5.8 %collective-permute-start.21 = (f32[40,128]{1,0:T(8,128)S(1)}, f32[40,128]{1,0:T(8,128)S(1)}, u32[]{:S(2)}, u32[]{:S(2)}) collective-permute-start(f32[40,128]{1,0:T(8,128)S(1)} %get-tuple-element.175.first_ref), channel_id=1, source_target_pairs={{32,0},{64,32},{33,1},{65,33},{34,2},{66,34},{35,3},{67,35},{36,4}... | collective-permute-start | bytes 61448 | tf_op jit(solution)/shard_map/ppermute | solution.py:1001
  32.0 18.5 %all-to-all-start.5 = ((f32[128,8,128]{2,1,0:T(8,128)}), f32[128,8,128]{2,1,0:T(8,128)S(1)}, u32[]{:S(2)}, u32[]{:S(2)}) async-start(f32[128,8,128]{2,1,0:T(8,128)} %bitcast.62), calls=%async_computation.5 | async-start | bytes 1048576 | tf_op jit(solution)/shard_map/all_to_all | solution.py:996
  37.1 6.1 %collective-permute-start.22 = (f32[40,128]{1,0:T(8,128)S(1)}, f32[40,128]{1,0:T(8,128)S(1)}, u32[]{:S(2)}, u32[]{:S(2)}) collective-permute-start(f32[40,128]{1,0:T(8,128)S(1)} %get-tuple-element.189), channel_id=1, source_target_pairs={{0,32},{32,64},{1,33},{33,65},{2,34},{34,66},{3,35},{35,67},{4,36}... | collective-permute-start | bytes 61448 | tf_op jit(solution)/shard_map/ppermute | solution.py:1000
  40.7 5.8 %collective-permute-start.23 = (f32[40,128]{1,0:T(8,128)S(1)}, f32[40,128]{1,0:T(8,128)S(1)}, u32[]{:S(2)}, u32[]{:S(2)}) collective-permute-start(f32[40,128]{1,0:T(8,128)S(1)} %get-tuple-element.190), channel_id=1, source_target_pairs={{32,0},{64,32},{33,1},{65,33},{34,2},{66,34},{35,3},{67,35},{36,4}... | collective-permute-start | bytes 61448 | tf_op jit(solution)/shard_map/ppermute | solution.py:1001
  51.4 17.4 %all-to-all-start.6 = ((f32[128,4,128]{2,1,0:T(4,128)}), f32[128,4,128]{2,1,0:T(4,128)S(1)}, u32[]{:S(2)}, u32[]{:S(2)}) async-start(f32[128,4,128]{2,1,0:T(4,128)} %bitcast.65), calls=%async_computation.6 | async-start | bytes 524288 | tf_op jit(solution)/shard_map/all_to_all | solution.py:996

commit v6 on v5

--- a/solution.py
+++ b/solution.py
@@ -20,6 +20,8 @@
 HITS = 8
 EDGE = 40
 FG = 5
+UNROLL = 6
+GROUP_UNROLL = 20
 PGROUPS = 20
 GROUPS = 22
 ENTRIES = 128
@@ -429,7 +431,7 @@
         for k in range(FG):
             group_s[g, 8 * k : 8 * k + 8, :] = tiles[k]
 
-    chunks(PGROUPS, 4, body)
+    chunks(PGROUPS, GROUP_UNROLL, body)
 
 
 def regroup_hits(recv_ref, group_s):
@@ -458,7 +460,7 @@
         for k, cells in enumerate(cells_of(t)):
             cycle_s[span, 8 * k : 8 * k + 8, :] += cells
 
-    chunks(6, 1, body)
+    chunks(6, UNROLL, body)
     for k, cells in enumerate(cells_of(6)):
         total = cells + pltpu.roll(cells, 96, 1) + pltpu.roll(cells, 64, 1)
         column_s[8 * k : 8 * k + 8, :] = total
@@ -496,15 +498,9 @@
             out_ref[:, 4 * i + 2, :] + out_ref[:, 4 * i + 3, :]
         )
         wide = jnp.concatenate([total, total, total, jnp.zeros((8, 128), F32)], axis=0)
-        parts.append(
-            lax.dot_general(
-                mean,
-                wide,
-                (((1,), (1,)), ((), ())),
-                precision=lax.Precision.HIGHEST,
-                preferred_element_type=F32,
-            )
-        )
+        high, low = halves(wide)
+        weights = mean.astype(jnp.bfloat16)
+        parts.append(product(weights, high, (1, 1)) + product(weights, low, (1, 1)))
     coarse = jnp.concatenate(parts, axis=0)
     plane_of = iota((128, 128), 1) // LANES
     placed = [jnp.where(plane_of == plane, coarse, 0.0) for plane in range(PLANES)]
@@ -671,11 +667,12 @@
 def tables_kernel(
     x_ref, diff_ref, cor_ref, mix_ref, owner_ref, cell_ref, weight_ref, fb_owner_ref, fb_cell_ref,
     fresh_ref, codes_ref, weights_ref, pick_ref, hits_ref, flag_ref, map_ref, entry_ref, halo_ref,
-    gid_s, mark_s, value_s, found_s, seek_s,
+    near_diff_ref, gid_s, mark_s, value_s, found_s, seek_s,
 ):
     grp = lax.axis_index("grp")
     gx = lax.axis_index("gx")
     update(x_ref, fresh_ref, diff_ref, cor_ref, mix_ref)
+    near_diff_ref[...] = diff_ref[...]
 
     @pl.when(grp < 3)
     def _():
@@ -861,7 +858,7 @@
             return from_block
 
         none = [jnp.full((8, 128), -1, jnp.int32) for _ in terms]
-        from_block = lax.fori_loop(0, GX, match, none)
+        from_block = lax.fori_loop(0, GX // 2, lambda c, f: match(2 * c + 1, match(2 * c, f)), none)
         sources = [jnp.max(f, axis=0, keepdims=True) for f in from_block]
         hots = [iota((GX, 128), 0) == s for s in sources]
         found, _ = ranks(hots)
@@ -980,6 +977,7 @@
 HIT = ((TAKEN, 128), jnp.bfloat16)
 ENTRY = ((PLANES * ENTRIES, 128), jnp.bfloat16)
 HALO = ((3 * ROWS, 128), jnp.bfloat16)
+DIFFUSION = ((ROWS, COLS), F32)
 HALOS = ((3 * ROWS, 128), F32)
 RIMS = ((2, LANES, COLS), F32)
 THIN = ((DEVICES * DEPTH, 128), F32)
@@ -1018,19 +1016,19 @@
     )
     recv = exchange(send)
     above, below = rims(last_row, first_row)
-    fresh, codes, weights, pick, hits, flag, place, entry, halo = call(
+    fresh, codes, weights, pick, hits, flag, place, entry, halo, near_diffusion = call(
         tables_kernel,
         "tables",
         (atmosphere,) + physics + (owner, cell, weight, fb_owner, fb_cell),
         "vvssvvvvv",
-        (STATE, CODES, BLOCK, PICK, HIT, BLOCK, MAP, ENTRY, HALO),
-        "vvvvvvvvv",
+        (STATE, CODES, BLOCK, PICK, HIT, BLOCK, MAP, ENTRY, HALO, DIFFUSION),
+        "v" * 10,
         (GIDS, TERMS, TERMS, GIDS, ((32, 128), jnp.int32)),
     )
     state, send, next_last, next_first = call(
         second_kernel,
         "substep_one",
-        (recv, fresh, diffusion, above, below, first_row, last_row, weights, table, codes, pick, hits, flag),
+        (recv, fresh, near_diffusion, above, below, first_row, last_row, weights, table, codes, pick, hits, flag),
         "v" * 13,
         (STATE, BLOCKS, RIM, RIM),
         "vavv",

time: 70.7 us -> 68.6 us (0.970)
  starting transfers between devices: 34.2 us -> 32.9 us
    all_to_all x3, starting transfers between devices: 23.3 us -> 22 us  [exchange(): return lax.all_to_all(blocks, ('grp', 'gx'), 0, 0, tiled=True)]
  transfers between devices with their start and end apart: 7 -> 7, of which waited for: 5 -> 5; matrix products, arithmetic and copies ran while one was open for 1% -> 1% of each run, Pallas kernels for 6% -> 7%
where the time goes in v6:
time: 68.6 us; the launch traced here: 68.3 us
  starting transfers between devices  32.9 us (48%)
  waiting for transfers between devices  20.8 us (30%)
  Pallas kernels  13 us (19%)
  between operations  0.9 us (1%)
  local copies, waits for them, and re-layouts  0.7 us (1%)
    all_to_all x3, starting transfers between devices, exchange(): return lax.all_to_all(blocks, ('grp', 'gx'), 0, 0, tiled=True)  22 us
    all_to_all x3, waiting for transfers between devices, exchange(): return lax.all_to_all(blocks, ('grp', 'gx'), 0, 0, tiled=True)  16.5 us
    pallas_call x7, Pallas kernels, call(): pl.pallas_call(kernel, name=name, in_specs=[pl.BlockSpec(memory_space=spa...  13 us
    ppermute x2, starting transfers between devices, rims(): above = lax.ppermute(last_row, 'grp', [(0, 1), (1, 2)])  7.09 us
    ppermute x2, waiting for transfers between devices, rims(): below = lax.ppermute(first_row, 'grp', [(1, 0), (2, 1)])  4.26 us
    ppermute x2, starting transfers between devices, rims(): below = lax.ppermute(first_row, 'grp', [(1, 0), (2, 1)])  3.84 us
  transfers between devices with their start and end apart: 7, of which 5 were waited for; matrix products, arithmetic and copies ran while one was open for 1% of the time, Pallas kernels for 7%

profile of v6, /device:TPU:1, one launch (start us, length us, event | category | flops | bytes accessed | tf_op | source)
XLA Modules:
  0.0 68.3 jit_solution(7163534651416267313)
XLA Ops:
  0.0 0.0 copy-start.2
  0.0 0.0 copy-start.3
  0.0 0.0 copy-start
  0.0 0.0 copy-start.4
  0.0 0.0 copy-start.13
  0.0 0.0 copy-start.24
  0.0 0.0 copy-start.27
  0.1 0.0 copy-start.14
  0.1 0.0 copy-start.16
  0.1 3.8 %first_cells.1 = (f32[1024,128]{1,0:T(8,128)}, s32[32,128]{1,0:T(8,128)S(1)}, f32[40,128]{1,0:T(8,128)S(1)}, f32[40,128]{1,0:T(8,128)S(1)}) custom-call(f32[40,16,128]{2,1,0:T(8,128)} %x_ref.3, s32[3,32,288]{2,1,0:T(8,128)} %bitcast.179, s32[3,32,288]{2,1,0:T(8,128)} %bitcast.182), custom_call_target="tpu_custom_call" | custom-call | flops 1000000 | bytes 4000000 | tf_op jit(solution)/shard_map/first_cells/pallas_call | solution.py:955
  3.9 11.5 %all-to-all-start.4 = ((f32[128,8,128]{2,1,0:T(8,128)}), f32[128,8,128]{2,1,0:T(8,128)S(1)}, u32[]{:S(2)}, u32[]{:S(2)}) async-start(f32[128,8,128]{2,1,0:T(8,128)} %bitcast.59), calls=%async_computation.4 | async-start | bytes 1048576 | tf_op jit(solution)/shard_map/all_to_all | solution.py:994
  15.4 3.5 %collective-permute-start.20 = (f32[40,128]{1,0:T(8,128)S(1)}, f32[40,128]{1,0:T(8,128)S(1)}, u32[]{:S(2)}, u32[]{:S(2)}) collective-permute-start(f32[40,128]{1,0:T(8,128)S(1)} %get-tuple-element.176.last_ref), channel_id=1, source_target_pairs={{0,32},{32,64},{1,33},{33,65},{2,34},{34,66},{3,35},{35,67},{4,36}... | collective-permute-start | bytes 61448 | tf_op jit(solution)/shard_map/ppermute | solution.py:998
  18.9 1.9 %collective-permute-start.21 = (f32[40,128]{1,0:T(8,128)S(1)}, f32[40,128]{1,0:T(8,128)S(1)}, u32[]{:S(2)}, u32[]{:S(2)}) collective-permute-start(f32[40,128]{1,0:T(8,128)S(1)} %get-tuple-element.177.first_ref), channel_id=1, source_target_pairs={{32,0},{64,32},{33,1},{65,33},{34,2},{66,34},{35,3},{67,35},{36,4}... | collective-permute-start | bytes 61448 | tf_op jit(solution)/shard_map/ppermute | solution.py:999
  20.8 2.8 %tables.1 = (f32[40,16,128]{2,1,0:T(8,128)S(1)}, s32[8,128]{1,0:T(8,128)S(1)}, f32[8,128]{1,0:T(8,128)S(1)}, bf16[384,384]{1,0:T(8,128)(2,1)S(1)}, bf16[256,128]...) custom-call(f32[40,16,128]{2,1,0:T(8,128)} %x_ref.3, ...), custom_call_target="tpu_custom_call" | custom-call | flops 1000000 | bytes 4000000 | tf_op jit(solution)/shard_map/tables/pallas_call | solution.py:955
  23.7 0.0 collective-permute-done.20.above_ref
  23.7 1.0 %collective-permute-done.21.below_ref = f32[40,128]{1,0:T(8,128)S(1)} collective-permute-done((f32[40,128]{1,0:T(8,128)S(1)}, f32[40,128]{1,0:T(8,128)S(1)}, u32[]{:S(2)}, u32[]{:S(2)}) %collective-permute-start.21) | collective-permute-done | bytes 20512 | tf_op jit(solution)/shard_map/ppermute | solution.py:999
  24.7 4.1 %all-to-all-done.4 = f32[128,8,128]{2,1,0:T(8,128)S(1)} async-done(((f32[128,8,128]{2,1,0:T(8,128)}), f32[128,8,128]{2,1,0:T(8,128)S(1)}, u32[]{:S(2)}, u32[]{:S(2)}) %all-to-all-start.4) | async-done | bytes 524320 | tf_op jit(solution)/shard_map/all_to_all | solution.py:994
  28.8 2.5 %substep_one.1 = (f32[40,16,128]{2,1,0:T(8,128)S(1)}, f32[1024,128]{1,0:T(8,128)}, f32[40,128]{1,0:T(8,128)S(1)}, f32[40,128]{1,0:T(8,128)S(1)}) custom-call(f32[1024,128]{1,0:T(8,128)S(1)} %bitcast.158, f32[40,16,128]{2,1,0:T(8,128)S(1)} %get-tuple-element.174.fresh_ref, f32[16,128]{1,0:T(8,128)S(1)} %get-tuple-element.175.diff_ref, ...), custom_call_target="tpu_custom_call" | custom-call | flops 1000000 | bytes 4000000 | tf_op jit(solution)/shard_map/substep_one/pallas_call | solution.py:955
  31.4 4.8 %all-to-all-start.5 = ((f32[128,8,128]{2,1,0:T(8,128)}), f32[128,8,128]{2,1,0:T(8,128)S(1)}, u32[]{:S(2)}, u32[]{:S(2)}) async-start(f32[128,8,128]{2,1,0:T(8,128)} %bitcast.62), calls=%async_computation.5 | async-start | bytes 1048576 | tf_op jit(solution)/shard_map/all_to_all | solution.py:994
  36.1 3.5 %collective-permute-start.22 = (f32[40,128]{1,0:T(8,128)S(1)}, f32[40,128]{1,0:T(8,128)S(1)}, u32[]{:S(2)}, u32[]{:S(2)}) collective-permute-start(f32[40,128]{1,0:T(8,128)S(1)} %get-tuple-element.191), channel_id=1, source_target_pairs={{0,32},{32,64},{1,33},{33,65},{2,34},{34,66},{3,35},{35,67},{4,36}... | collective-permute-start | bytes 61448 | tf_op jit(solution)/shard_map/ppermute | solution.py:998
  39.7 1.9 %collective-permute-start.23 = (f32[40,128]{1,0:T(8,128)S(1)}, f32[40,128]{1,0:T(8,128)S(1)}, u32[]{:S(2)}, u32[]{:S(2)}) collective-permute-start(f32[40,128]{1,0:T(8,128)S(1)} %get-tuple-element.192), channel_id=1, source_target_pairs={{32,0},{64,32},{33,1},{65,33},{34,2},{66,34},{35,3},{67,35},{36,4}... | collective-permute-start | bytes 61448 | tf_op jit(solution)/shard_map/ppermute | solution.py:999
  41.6 0.0 copy-done.2
  41.6 0.0 copy-done.3
  41.6 0.0 copy-done.13
  41.6 0.0 copy-done.24
  41.7 0.0 copy-done.27
  41.7 0.0 copy-done.14
  41.7 0.0 copy-done.16
  41.7 0.6 hits.1
  42.3 0.0 collective-permute-done.22.above_ref
  42.3 3.2 %collective-permute-done.23.below_ref = f32[40,128]{1,0:T(8,128)S(1)} collective-permute-done((f32[40,128]{1,0:T(8,128)S(1)}, f32[40,128]{1,0:T(8,128)S(1)}, u32[]{:S(2)}, u32[]{:S(2)}) %collective-permute-start.23) | collective-permute-done | bytes 20512 | tf_op jit(solution)/shard_map/ppermute | solution.py:999
  45.5 4.1 %all-to-all-done.5 = f32[128,8,128]{2,1,0:T(8,128)S(1)} async-done(((f32[128,8,128]{2,1,0:T(8,128)}), f32[128,8,128]{2,1,0:T(8,128)S(1)}, u32[]{:S(2)}, u32[]{:S(2)}) %all-to-all-start.5) | async-done | bytes 524320 | tf_op jit(solution)/shard_map/all_to_all | solution.py:994
  49.6 0.8 %substep_two.1 = (f32[40,16,128]{2,1,0:T(8,128)S(1)}, f32[512,128]{1,0:T(8,128)}, f32[8,128]{1,0:T(8,128)S(1)}, f32[2,40,128]{2,1,0:T(8,128)S(1)}, f32[48,128]{1,0:T(8,128)S(1)}) custom-call(f32[1024,128]{1,0:T(8,128)S(1)} %bitcast.157, f32[40,16,128]{2,1,0:T(8,128)S(1)} %get-tuple-element.185.x_ref, f32[40,16,128]{2,1,0:T(8,128)S(1)} %get-tuple-element.186.fresh_ref, ...), custom_call_target="tpu_custom_call" | custom-call | flops 1000000 | bytes 4000000 | tf_op jit(solution)/shard_map/substep_two/pallas_call | solution.py:955
  50.4 5.7 %all-to-all-start.6 = ((f32[128,4,128]{2,1,0:T(4,128)}), f32[128,4,128]{2,1,0:T(4,128)S(1)}, u32[]{:S(2)}, u32[]{:S(2)}) async-start(f32[128,4,128]{2,1,0:T(4,128)} %bitcast.65), calls=%async_computation.6 | async-start | bytes 524288 | tf_op jit(solution)/shard_map/all_to_all | solution.py:994
  56.1 0.6 slice.381
  57.4 1.1 %parents.1 = f32[40,16,128]{2,1,0:T(8,128)S(1)} custom-call(f32[40,16,128]{2,1,0:T(8,128)S(1)} %get-tuple-element.195.x_ref, f32[16,128]{1,0:T(8,128)S(1)} %copy-done.13, f32[16]{0:T(128)S(1)} %copy-done.24, f32[10]{0:T(128)S(1)} %copy-done.27, f32[2,40,128]{2,1,0:T(8,128)S(1)} %get-tuple-element.196.rims_ref, f32[48,128]{1,0:T(8,128)S(1)} %get-tuple-element.197.halos_ref), custom_call_target="tpu_custom_call" | custom-call | flops 1000000 | bytes 4000000 | tf_op jit(solution)/shard_map/parents/pallas_call | solution.py:955
  58.5 8.3 %all-to-all-done.6 = f32[128,4,128]{2,1,0:T(4,128)S(1)} async-done(((f32[128,4,128]{2,1,0:T(4,128)}), f32[128,4,128]{2,1,0:T(4,128)S(1)}, u32[]{:S(2)}, u32[]{:S(2)}) %all-to-all-start.6) | async-done | bytes 262176 | tf_op jit(solution)/shard_map/all_to_all | solution.py:994
  66.8 0.0 copy-done
  66.9 0.0 copy-done.4
  66.9 1.4 %conditional.1 = (f32[40,16,128]{2,1,0:T(8,128)}) conditional(s32[]{:T(128)} %bitcast.64, (f32[128,4,128]{2,1,0:T(4,128)S(1)}, f32[40,16,128]{2,1,0:T(8,128)S(1)}, f32[40,16,128]{2,1,0:T(8,128)S(1)}, s32[32,128]{1,0:T(8,128)S(1)}, bf16[384,128]{1,0:T(8,128)(2,1)S(1)}) %tuple.44, (f32[16,128]{1,0:T(8,128)S(1)}, f32[40,16,128]{2,1,0:T(8,128)S(1)}, ...), branch_computations={%region_0.0_spmd, %region_1.9_spmd} | conditional | flops 12829852 | bytes 118900464 | solution.py:1074
  66.9 1.4 %finish.1 = f32[40,16,128]{2,1,0:T(8,128)} custom-call(f32[512,128]{1,0:T(8,128)S(1)} %bitcast.192, f32[40,16,128]{2,1,0:T(8,128)S(1)} %get-tuple-element.135.x_ref, f32[40,16,128]{2,1,0:T(8,128)S(1)} %get-tuple-element.136.fresh_ref, s32[32,128]{1,0:T(8,128)S(1)} %get-tuple-element.137.map_ref, bf16[384,128]{1,0:T(8,128)(2,1)S(1)} %get-tuple-element.138.entry_ref), custom_call_target="tpu_custom_call" | custom-call | flops 1000000 | bytes 4000000 | tf_op jit(solution)/shard_map/cond/branch_0_fun/finish/pallas_call | solution.py:955
Async XLA Ops:
  0.0 41.6 %copy-start.2 = (s32[32,3,288]{2,0,1:T(8,128)S(1)}, s32[32,3,288]{2,0,1:T(8,128)}, u32[]{:S(2)}) copy-start(s32[32,3,288]{2,0,1:T(8,128)} %param.33) | copy-start | bytes 331780
  0.0 41.6 %copy-start.3 = (s32[32,3,288]{2,0,1:T(8,128)S(1)}, s32[32,3,288]{2,0,1:T(8,128)}, u32[]{:S(2)}) copy-start(s32[32,3,288]{2,0,1:T(8,128)} %param.34) | copy-start | bytes 331780
  0.0 66.8 %copy-start = (f32[40,16,128]{2,1,0:T(8,128)S(1)}, f32[40,16,128]{2,1,0:T(8,128)}, u32[]{:S(2)}) copy-start(f32[40,16,128]{2,1,0:T(8,128)} %x_ref.3) | copy-start | bytes 983044
  0.0 66.8 %copy-start.4 = (f32[32,3,288]{2,0,1:T(8,128)S(1)}, f32[32,3,288]{2,0,1:T(8,128)}, u32[]{:S(2)}) copy-start(f32[32,3,288]{2,0,1:T(8,128)} %param.35) | copy-start | bytes 331780
  0.0 41.6 %copy-start.13 = (f32[16,128]{1,0:T(8,128)S(1)}, f32[16,128]{1,0:T(8,128)}, u32[]{:S(2)}) copy-start(f32[16,128]{1,0:T(8,128)} %diff_ref.7) | copy-start | bytes 24580
  0.0 41.6 %copy-start.24 = (f32[16]{0:T(128)S(1)}, f32[16]{0:T(128)}, u32[]{:S(2)}) copy-start(f32[16]{0:T(128)} %cor_ref.5) | copy-start | bytes 196
  0.0 41.6 %copy-start.27 = (f32[10]{0:T(128)S(1)}, f32[10]{0:T(128)}, u32[]{:S(2)}) copy-start(f32[10]{0:T(128)} %mix_ref.5) | copy-start | bytes 124
  0.1 41.6 %copy-start.14 = (s32[32,128]{1,0:T(8,128)S(1)}, s32[32,128]{1,0:T(8,128)}, u32[]{:S(2)}) copy-start(s32[32,128]{1,0:T(8,128)} %fb_owner_ref.3) | copy-start | bytes 49156
  0.1 41.6 %copy-start.16 = (s32[32,128]{1,0:T(8,128)S(1)}, s32[32,128]{1,0:T(8,128)}, u32[]{:S(2)}) copy-start(s32[32,128]{1,0:T(8,128)} %fb_cell_ref.3) | copy-start | bytes 49156
  3.9 25.0 %all-to-all-start.4 = ((f32[128,8,128]{2,1,0:T(8,128)}), f32[128,8,128]{2,1,0:T(8,128)S(1)}, u32[]{:S(2)}, u32[]{:S(2)}) async-start(f32[128,8,128]{2,1,0:T(8,128)} %bitcast.59), calls=%async_computation.4 | async-start | bytes 1048576 | tf_op jit(solution)/shard_map/all_to_all | solution.py:994
  15.4 8.3 %collective-permute-start.20 = (f32[40,128]{1,0:T(8,128)S(1)}, f32[40,128]{1,0:T(8,128)S(1)}, u32[]{:S(2)}, u32[]{:S(2)}) collective-permute-start(f32[40,128]{1,0:T(8,128)S(1)} %get-tuple-element.176.last_ref), channel_id=1, source_target_pairs={{0,32},{32,64},{1,33},{33,65},{2,34},{34,66},{3,35},{35,67},{4,36}... | collective-permute-start | bytes 61448 | tf_op jit(solution)/shard_map/ppermute | solution.py:998
  18.9 5.8 %collective-permute-start.21 = (f32[40,128]{1,0:T(8,128)S(1)}, f32[40,128]{1,0:T(8,128)S(1)}, u32[]{:S(2)}, u32[]{:S(2)}) collective-permute-start(f32[40,128]{1,0:T(8,128)S(1)} %get-tuple-element.177.first_ref), channel_id=1, source_target_pairs={{32,0},{64,32},{33,1},{65,33},{34,2},{66,34},{35,3},{67,35},{36,4}... | collective-permute-start | bytes 61448 | tf_op jit(solution)/shard_map/ppermute | solution.py:999
  31.4 18.2 %all-to-all-start.5 = ((f32[128,8,128]{2,1,0:T(8,128)}), f32[128,8,128]{2,1,0:T(8,128)S(1)}, u32[]{:S(2)}, u32[]{:S(2)}) async-start(f32[128,8,128]{2,1,0:T(8,128)} %bitcast.62), calls=%async_computation.5 | async-start | bytes 1048576 | tf_op jit(solution)/shard_map/all_to_all | solution.py:994
  36.1 6.1 %collective-permute-start.22 = (f32[40,128]{1,0:T(8,128)S(1)}, f32[40,128]{1,0:T(8,128)S(1)}, u32[]{:S(2)}, u32[]{:S(2)}) collective-permute-start(f32[40,128]{1,0:T(8,128)S(1)} %get-tuple-element.191), channel_id=1, source_target_pairs={{0,32},{32,64},{1,33},{33,65},{2,34},{34,66},{3,35},{35,67},{4,36}... | collective-permute-start | bytes 61448 | tf_op jit(solution)/shard_map/ppermute | solution.py:998
  39.7 5.8 %collective-permute-start.23 = (f32[40,128]{1,0:T(8,128)S(1)}, f32[40,128]{1,0:T(8,128)S(1)}, u32[]{:S(2)}, u32[]{:S(2)}) collective-permute-start(f32[40,128]{1,0:T(8,128)S(1)} %get-tuple-element.192), channel_id=1, source_target_pairs={{32,0},{64,32},{33,1},{65,33},{34,2},{66,34},{35,3},{67,35},{36,4}... | collective-permute-start | bytes 61448 | tf_op jit(solution)/shard_map/ppermute | solution.py:999
  50.4 16.4 %all-to-all-start.6 = ((f32[128,4,128]{2,1,0:T(4,128)}), f32[128,4,128]{2,1,0:T(4,128)S(1)}, u32[]{:S(2)}, u32[]{:S(2)}) async-start(f32[128,4,128]{2,1,0:T(4,128)} %bitcast.65), calls=%async_computation.6 | async-start | bytes 524288 | tf_op jit(solution)/shard_map/all_to_all | solution.py:994

commit v7 on v6

--- a/solution.py
+++ b/solution.py
@@ -417,6 +417,11 @@
 
 
 def chunks(count, step, body):
+    if count == step:
+        for i in range(count):
+            body(i)
+        return
+
     def run(c, carry):
         for s in range(step):
             body(c * step + s)
@@ -456,7 +461,7 @@
     cycle_s[...] = jnp.zeros((2, LANES, 128), F32)
 
     def body(t):
-        span = jnp.bitwise_and(t, 1)
+        span = t % 2
         for k, cells in enumerate(cells_of(t)):
             cycle_s[span, 8 * k : 8 * k + 8, :] += cells
 
@@ -794,10 +799,9 @@
 ):
     grp = lax.axis_index("grp")
     gx = lax.axis_index("gx")
-    add_columns(fresh_ref, out_ref, gather_halo(recv_ref, grp, gx), diff_ref, grp, gx)
-
     @pl.when(grp < 3)
     def _():
+        add_columns(fresh_ref, out_ref, gather_halo(recv_ref, grp, gx), diff_ref, grp, gx)
         add_rows(first_ref, last_ref, out_ref, above_ref, below_ref, diff_ref, grp)
         send_edges(out_ref, edges_s, send_ref, edge_sems, grp, gx)
         last_row_ref[...] = out_ref[:, ROWS - 1, :]
@@ -810,6 +814,7 @@
 
     @pl.when(grp == 3)
     def _():
+        add_columns(fresh_ref, out_ref, gather_halo(recv_ref, grp, gx), diff_ref, grp, gx)
         regroup(recv_ref, group_s)
         interpolate(codes_ref, weights_ref, group_s, PGROUPS, cycle_s, column_s)
         prescribe(out_ref, cycle_s, column_s, gx)

time: 68.6 us -> 68.6 us (level)
  no operation moved by 1% of the time
where the time goes in v7:
time: 68.6 us; the launch traced here: 68.2 us
  starting transfers between devices  32.9 us (48%)
  waiting for transfers between devices  20.8 us (30%)
  Pallas kernels  12.9 us (19%)
  between operations  0.9 us (1%)
  local copies, waits for them, and re-layouts  0.7 us (1%)
    all_to_all x3, starting transfers between devices, exchange(): return lax.all_to_all(blocks, ('grp', 'gx'), 0, 0, tiled=True)  22 us
    all_to_all x3, waiting for transfers between devices, exchange(): return lax.all_to_all(blocks, ('grp', 'gx'), 0, 0, tiled=True)  16.5 us
    pallas_call x7, Pallas kernels, call(): pl.pallas_call(kernel, name=name, in_specs=[pl.BlockSpec(memory_space=spa...  12.9 us
    ppermute x2, starting transfers between devices, rims(): above = lax.ppermute(last_row, 'grp', [(0, 1), (1, 2)])  7.09 us
    ppermute x2, waiting for transfers between devices, rims(): below = lax.ppermute(first_row, 'grp', [(1, 0), (2, 1)])  4.26 us
    ppermute x2, starting transfers between devices, rims(): below = lax.ppermute(first_row, 'grp', [(1, 0), (2, 1)])  3.84 us
  transfers between devices with their start and end apart: 7, of which 5 were waited for; matrix products, arithmetic and copies ran while one was open for 1% of the time, Pallas kernels for 7%

profile of v7, /device:TPU:1, one launch (start us, length us, event | category | flops | bytes accessed | tf_op | source)
XLA Modules:
  0.0 68.2 jit_solution(2675017881605458486)
XLA Ops:
  0.0 0.0 copy-start.2
  0.0 0.0 copy-start.3
  0.0 0.0 copy-start
  0.0 0.0 copy-start.4
  0.0 0.0 copy-start.13
  0.0 0.0 copy-start.24
  0.0 0.0 copy-start.27
  0.1 0.0 copy-start.14
  0.1 0.0 copy-start.16
  0.1 3.8 %first_cells.1 = (f32[1024,128]{1,0:T(8,128)}, s32[32,128]{1,0:T(8,128)S(1)}, f32[40,128]{1,0:T(8,128)S(1)}, f32[40,128]{1,0:T(8,128)S(1)}) custom-call(f32[40,16,128]{2,1,0:T(8,128)} %x_ref.3, s32[3,32,288]{2,1,0:T(8,128)} %bitcast.179, s32[3,32,288]{2,1,0:T(8,128)} %bitcast.182), custom_call_target="tpu_custom_call" | custom-call | flops 1000000 | bytes 4000000 | tf_op jit(solution)/shard_map/first_cells/pallas_call | solution.py:960
  3.9 11.5 %all-to-all-start.4 = ((f32[128,8,128]{2,1,0:T(8,128)}), f32[128,8,128]{2,1,0:T(8,128)S(1)}, u32[]{:S(2)}, u32[]{:S(2)}) async-start(f32[128,8,128]{2,1,0:T(8,128)} %bitcast.59), calls=%async_computation.4 | async-start | bytes 1048576 | tf_op jit(solution)/shard_map/all_to_all | solution.py:999
  15.4 3.5 %collective-permute-start.20 = (f32[40,128]{1,0:T(8,128)S(1)}, f32[40,128]{1,0:T(8,128)S(1)}, u32[]{:S(2)}, u32[]{:S(2)}) collective-permute-start(f32[40,128]{1,0:T(8,128)S(1)} %get-tuple-element.176.last_ref), channel_id=1, source_target_pairs={{0,32},{32,64},{1,33},{33,65},{2,34},{34,66},{3,35},{35,67},{4,36}... | collective-permute-start | bytes 61448 | tf_op jit(solution)/shard_map/ppermute | solution.py:1003
  18.9 1.9 %collective-permute-start.21 = (f32[40,128]{1,0:T(8,128)S(1)}, f32[40,128]{1,0:T(8,128)S(1)}, u32[]{:S(2)}, u32[]{:S(2)}) collective-permute-start(f32[40,128]{1,0:T(8,128)S(1)} %get-tuple-element.177.first_ref), channel_id=1, source_target_pairs={{32,0},{64,32},{33,1},{65,33},{34,2},{66,34},{35,3},{67,35},{36,4}... | collective-permute-start | bytes 61448 | tf_op jit(solution)/shard_map/ppermute | solution.py:1004
  20.8 2.8 %tables.1 = (f32[40,16,128]{2,1,0:T(8,128)S(1)}, s32[8,128]{1,0:T(8,128)S(1)}, f32[8,128]{1,0:T(8,128)S(1)}, bf16[384,384]{1,0:T(8,128)(2,1)S(1)}, bf16[256,128]...) custom-call(f32[40,16,128]{2,1,0:T(8,128)} %x_ref.3, ...), custom_call_target="tpu_custom_call" | custom-call | flops 1000000 | bytes 4000000 | tf_op jit(solution)/shard_map/tables/pallas_call | solution.py:960
  23.7 0.0 collective-permute-done.20.above_ref
  23.7 1.0 %collective-permute-done.21.below_ref = f32[40,128]{1,0:T(8,128)S(1)} collective-permute-done((f32[40,128]{1,0:T(8,128)S(1)}, f32[40,128]{1,0:T(8,128)S(1)}, u32[]{:S(2)}, u32[]{:S(2)}) %collective-permute-start.21) | collective-permute-done | bytes 20512 | tf_op jit(solution)/shard_map/ppermute | solution.py:1004
  24.7 4.1 %all-to-all-done.4 = f32[128,8,128]{2,1,0:T(8,128)S(1)} async-done(((f32[128,8,128]{2,1,0:T(8,128)}), f32[128,8,128]{2,1,0:T(8,128)S(1)}, u32[]{:S(2)}, u32[]{:S(2)}) %all-to-all-start.4) | async-done | bytes 524320 | tf_op jit(solution)/shard_map/all_to_all | solution.py:999
  28.8 2.4 %substep_one.1 = (f32[40,16,128]{2,1,0:T(8,128)S(1)}, f32[1024,128]{1,0:T(8,128)}, f32[40,128]{1,0:T(8,128)S(1)}, f32[40,128]{1,0:T(8,128)S(1)}) custom-call(f32[1024,128]{1,0:T(8,128)S(1)} %bitcast.158, f32[40,16,128]{2,1,0:T(8,128)S(1)} %get-tuple-element.174.fresh_ref, f32[16,128]{1,0:T(8,128)S(1)} %get-tuple-element.175.diff_ref, ...), custom_call_target="tpu_custom_call" | custom-call | flops 1000000 | bytes 4000000 | tf_op jit(solution)/shard_map/substep_one/pallas_call | solution.py:960
  31.3 4.8 %all-to-all-start.5 = ((f32[128,8,128]{2,1,0:T(8,128)}), f32[128,8,128]{2,1,0:T(8,128)S(1)}, u32[]{:S(2)}, u32[]{:S(2)}) async-start(f32[128,8,128]{2,1,0:T(8,128)} %bitcast.62), calls=%async_computation.5 | async-start | bytes 1048576 | tf_op jit(solution)/shard_map/all_to_all | solution.py:999
  36.0 3.5 %collective-permute-start.22 = (f32[40,128]{1,0:T(8,128)S(1)}, f32[40,128]{1,0:T(8,128)S(1)}, u32[]{:S(2)}, u32[]{:S(2)}) collective-permute-start(f32[40,128]{1,0:T(8,128)S(1)} %get-tuple-element.191), channel_id=1, source_target_pairs={{0,32},{32,64},{1,33},{33,65},{2,34},{34,66},{3,35},{35,67},{4,36}... | collective-permute-start | bytes 61448 | tf_op jit(solution)/shard_map/ppermute | solution.py:1003
  39.6 1.9 %collective-permute-start.23 = (f32[40,128]{1,0:T(8,128)S(1)}, f32[40,128]{1,0:T(8,128)S(1)}, u32[]{:S(2)}, u32[]{:S(2)}) collective-permute-start(f32[40,128]{1,0:T(8,128)S(1)} %get-tuple-element.192), channel_id=1, source_target_pairs={{32,0},{64,32},{33,1},{65,33},{34,2},{66,34},{35,3},{67,35},{36,4}... | collective-permute-start | bytes 61448 | tf_op jit(solution)/shard_map/ppermute | solution.py:1004
  41.5 0.0 copy-done.2
  41.5 0.0 copy-done.3
  41.5 0.0 copy-done.13
  41.5 0.0 copy-done.24
  41.6 0.0 copy-done.27
  41.6 0.0 copy-done.14
  41.6 0.0 copy-done.16
  41.6 0.6 hits.1
  42.2 0.0 collective-permute-done.22.above_ref
  42.2 3.2 %collective-permute-done.23.below_ref = f32[40,128]{1,0:T(8,128)S(1)} collective-permute-done((f32[40,128]{1,0:T(8,128)S(1)}, f32[40,128]{1,0:T(8,128)S(1)}, u32[]{:S(2)}, u32[]{:S(2)}) %collective-permute-start.23) | collective-permute-done | bytes 20512 | tf_op jit(solution)/shard_map/ppermute | solution.py:1004
  45.4 4.1 %all-to-all-done.5 = f32[128,8,128]{2,1,0:T(8,128)S(1)} async-done(((f32[128,8,128]{2,1,0:T(8,128)}), f32[128,8,128]{2,1,0:T(8,128)S(1)}, u32[]{:S(2)}, u32[]{:S(2)}) %all-to-all-start.5) | async-done | bytes 524320 | tf_op jit(solution)/shard_map/all_to_all | solution.py:999
  49.5 0.8 %substep_two.1 = (f32[40,16,128]{2,1,0:T(8,128)S(1)}, f32[512,128]{1,0:T(8,128)}, f32[8,128]{1,0:T(8,128)S(1)}, f32[2,40,128]{2,1,0:T(8,128)S(1)}, f32[48,128]{1,0:T(8,128)S(1)}) custom-call(f32[1024,128]{1,0:T(8,128)S(1)} %bitcast.157, f32[40,16,128]{2,1,0:T(8,128)S(1)} %get-tuple-element.185.x_ref, f32[40,16,128]{2,1,0:T(8,128)S(1)} %get-tuple-element.186.fresh_ref, ...), custom_call_target="tpu_custom_call" | custom-call | flops 1000000 | bytes 4000000 | tf_op jit(solution)/shard_map/substep_two/pallas_call | solution.py:960
  50.3 5.7 %all-to-all-start.6 = ((f32[128,4,128]{2,1,0:T(4,128)}), f32[128,4,128]{2,1,0:T(4,128)S(1)}, u32[]{:S(2)}, u32[]{:S(2)}) async-start(f32[128,4,128]{2,1,0:T(4,128)} %bitcast.65), calls=%async_computation.6 | async-start | bytes 524288 | tf_op jit(solution)/shard_map/all_to_all | solution.py:999
  56.0 0.6 slice.381
  57.3 1.1 %parents.1 = f32[40,16,128]{2,1,0:T(8,128)S(1)} custom-call(f32[40,16,128]{2,1,0:T(8,128)S(1)} %get-tuple-element.195.x_ref, f32[16,128]{1,0:T(8,128)S(1)} %copy-done.13, f32[16]{0:T(128)S(1)} %copy-done.24, f32[10]{0:T(128)S(1)} %copy-done.27, f32[2,40,128]{2,1,0:T(8,128)S(1)} %get-tuple-element.196.rims_ref, f32[48,128]{1,0:T(8,128)S(1)} %get-tuple-element.197.halos_ref), custom_call_target="tpu_custom_call" | custom-call | flops 1000000 | bytes 4000000 | tf_op jit(solution)/shard_map/parents/pallas_call | solution.py:960
  58.4 8.3 %all-to-all-done.6 = f32[128,4,128]{2,1,0:T(4,128)S(1)} async-done(((f32[128,4,128]{2,1,0:T(4,128)}), f32[128,4,128]{2,1,0:T(4,128)S(1)}, u32[]{:S(2)}, u32[]{:S(2)}) %all-to-all-start.6) | async-done | bytes 262176 | tf_op jit(solution)/shard_map/all_to_all | solution.py:999
  66.8 0.0 copy-done
  66.8 0.0 copy-done.4
  66.8 1.4 %conditional.1 = (f32[40,16,128]{2,1,0:T(8,128)}) conditional(s32[]{:T(128)} %bitcast.64, (f32[128,4,128]{2,1,0:T(4,128)S(1)}, f32[40,16,128]{2,1,0:T(8,128)S(1)}, f32[40,16,128]{2,1,0:T(8,128)S(1)}, s32[32,128]{1,0:T(8,128)S(1)}, bf16[384,128]{1,0:T(8,128)(2,1)S(1)}) %tuple.44, (f32[16,128]{1,0:T(8,128)S(1)}, f32[40,16,128]{2,1,0:T(8,128)S(1)}, ...), branch_computations={%region_0.0_spmd, %region_1.9_spmd} | conditional | flops 12829852 | bytes 118900464 | solution.py:1079
  66.8 1.4 %finish.1 = f32[40,16,128]{2,1,0:T(8,128)} custom-call(f32[512,128]{1,0:T(8,128)S(1)} %bitcast.192, f32[40,16,128]{2,1,0:T(8,128)S(1)} %get-tuple-element.135.x_ref, f32[40,16,128]{2,1,0:T(8,128)S(1)} %get-tuple-element.136.fresh_ref, s32[32,128]{1,0:T(8,128)S(1)} %get-tuple-element.137.map_ref, bf16[384,128]{1,0:T(8,128)(2,1)S(1)} %get-tuple-element.138.entry_ref), custom_call_target="tpu_custom_call" | custom-call | flops 1000000 | bytes 4000000 | tf_op jit(solution)/shard_map/cond/branch_0_fun/finish/pallas_call | solution.py:960
Async XLA Ops:
  0.0 41.5 %copy-start.2 = (s32[32,3,288]{2,0,1:T(8,128)S(1)}, s32[32,3,288]{2,0,1:T(8,128)}, u32[]{:S(2)}) copy-start(s32[32,3,288]{2,0,1:T(8,128)} %param.33) | copy-start | bytes 331780
  0.0 41.5 %copy-start.3 = (s32[32,3,288]{2,0,1:T(8,128)S(1)}, s32[32,3,288]{2,0,1:T(8,128)}, u32[]{:S(2)}) copy-start(s32[32,3,288]{2,0,1:T(8,128)} %param.34) | copy-start | bytes 331780
  0.0 66.8 %copy-start = (f32[40,16,128]{2,1,0:T(8,128)S(1)}, f32[40,16,128]{2,1,0:T(8,128)}, u32[]{:S(2)}) copy-start(f32[40,16,128]{2,1,0:T(8,128)} %x_ref.3) | copy-start | bytes 983044
  0.0 66.8 %copy-start.4 = (f32[32,3,288]{2,0,1:T(8,128)S(1)}, f32[32,3,288]{2,0,1:T(8,128)}, u32[]{:S(2)}) copy-start(f32[32,3,288]{2,0,1:T(8,128)} %param.35) | copy-start | bytes 331780
  0.0 41.5 %copy-start.13 = (f32[16,128]{1,0:T(8,128)S(1)}, f32[16,128]{1,0:T(8,128)}, u32[]{:S(2)}) copy-start(f32[16,128]{1,0:T(8,128)} %diff_ref.7) | copy-start | bytes 24580
  0.0 41.5 %copy-start.24 = (f32[16]{0:T(128)S(1)}, f32[16]{0:T(128)}, u32[]{:S(2)}) copy-start(f32[16]{0:T(128)} %cor_ref.5) | copy-start | bytes 196
  0.0 41.5 %copy-start.27 = (f32[10]{0:T(128)S(1)}, f32[10]{0:T(128)}, u32[]{:S(2)}) copy-start(f32[10]{0:T(128)} %mix_ref.5) | copy-start | bytes 124
  0.1 41.5 %copy-start.14 = (s32[32,128]{1,0:T(8,128)S(1)}, s32[32,128]{1,0:T(8,128)}, u32[]{:S(2)}) copy-start(s32[32,128]{1,0:T(8,128)} %fb_owner_ref.3) | copy-start | bytes 49156
  0.1 41.5 %copy-start.16 = (s32[32,128]{1,0:T(8,128)S(1)}, s32[32,128]{1,0:T(8,128)}, u32[]{:S(2)}) copy-start(s32[32,128]{1,0:T(8,128)} %fb_cell_ref.3) | copy-start | bytes 49156
  3.9 25.0 %all-to-all-start.4 = ((f32[128,8,128]{2,1,0:T(8,128)}), f32[128,8,128]{2,1,0:T(8,128)S(1)}, u32[]{:S(2)}, u32[]{:S(2)}) async-start(f32[128,8,128]{2,1,0:T(8,128)} %bitcast.59), calls=%async_computation.4 | async-start | bytes 1048576 | tf_op jit(solution)/shard_map/all_to_all | solution.py:999
  15.4 8.3 %collective-permute-start.20 = (f32[40,128]{1,0:T(8,128)S(1)}, f32[40,128]{1,0:T(8,128)S(1)}, u32[]{:S(2)}, u32[]{:S(2)}) collective-permute-start(f32[40,128]{1,0:T(8,128)S(1)} %get-tuple-element.176.last_ref), channel_id=1, source_target_pairs={{0,32},{32,64},{1,33},{33,65},{2,34},{34,66},{3,35},{35,67},{4,36}... | collective-permute-start | bytes 61448 | tf_op jit(solution)/shard_map/ppermute | solution.py:1003
  18.9 5.8 %collective-permute-start.21 = (f32[40,128]{1,0:T(8,128)S(1)}, f32[40,128]{1,0:T(8,128)S(1)}, u32[]{:S(2)}, u32[]{:S(2)}) collective-permute-start(f32[40,128]{1,0:T(8,128)S(1)} %get-tuple-element.177.first_ref), channel_id=1, source_target_pairs={{32,0},{64,32},{33,1},{65,33},{34,2},{66,34},{35,3},{67,35},{36,4}... | collective-permute-start | bytes 61448 | tf_op jit(solution)/shard_map/ppermute | solution.py:1004
  31.3 18.2 %all-to-all-start.5 = ((f32[128,8,128]{2,1,0:T(8,128)}), f32[128,8,128]{2,1,0:T(8,128)S(1)}, u32[]{:S(2)}, u32[]{:S(2)}) async-start(f32[128,8,128]{2,1,0:T(8,128)} %bitcast.62), calls=%async_computation.5 | async-start | bytes 1048576 | tf_op jit(solution)/shard_map/all_to_all | solution.py:999
  36.0 6.1 %collective-permute-start.22 = (f32[40,128]{1,0:T(8,128)S(1)}, f32[40,128]{1,0:T(8,128)S(1)}, u32[]{:S(2)}, u32[]{:S(2)}) collective-permute-start(f32[40,128]{1,0:T(8,128)S(1)} %get-tuple-element.191), channel_id=1, source_target_pairs={{0,32},{32,64},{1,33},{33,65},{2,34},{34,66},{3,35},{35,67},{4,36}... | collective-permute-start | bytes 61448 | tf_op jit(solution)/shard_map/ppermute | solution.py:1003
  39.6 5.8 %collective-permute-start.23 = (f32[40,128]{1,0:T(8,128)S(1)}, f32[40,128]{1,0:T(8,128)S(1)}, u32[]{:S(2)}, u32[]{:S(2)}) collective-permute-start(f32[40,128]{1,0:T(8,128)S(1)} %get-tuple-element.192), channel_id=1, source_target_pairs={{32,0},{64,32},{33,1},{65,33},{34,2},{66,34},{35,3},{67,35},{36,4}... | collective-permute-start | bytes 61448 | tf_op jit(solution)/shard_map/ppermute | solution.py:1004
  50.3 16.4 %all-to-all-start.6 = ((f32[128,4,128]{2,1,0:T(4,128)}), f32[128,4,128]{2,1,0:T(4,128)S(1)}, u32[]{:S(2)}, u32[]{:S(2)}) async-start(f32[128,4,128]{2,1,0:T(4,128)} %bitcast.65), calls=%async_computation.6 | async-start | bytes 524288 | tf_op jit(solution)/shard_map/all_to_all | solution.py:999
